TPU v7x, 32 devices: a whole 2x2x4 slice. The times are simulated.
32 devices in a mesh: dp: 16 (over z, y, core), mp: 2 (over x).
Axes of the slice: x: 2, y: 2, z: 4, core: 2. Of those that a mesh axis runs over, the one named last changes fastest.
Arguments:
- image_small: bfloat16 [128, 196, 768], P('dp', None, 'mp')
- image_large: bfloat16 [32, 576, 768], P('dp', None, 'mp')
- image_counts: int32 [16, 2], P('dp'), may hold values from 0 to 8, as said below
- norm_gain: float32 [3, 2, 768], P(None, None, 'mp'), may hold values from 0.5 to 2
- norm_shift: float32 [3, 2, 768], P(None, None, 'mp'), may hold values from -3 to 3
- mix_in_small: bfloat16 [3, 196, 384], replicated, may hold values from -0.4375 to 0.4375
- mix_bias_small: float32 [3, 384], replicated, may hold values from -3 to 3
- mix_out_small: bfloat16 [3, 384, 196], replicated, may hold values from -0.3125 to 0.3125
- mix_obias_small: float32 [3, 196], replicated, may hold values from -3 to 3
- mix_in_large: bfloat16 [3, 576, 384], replicated, may hold values from -0.25 to 0.25
- mix_bias_large: float32 [3, 384], replicated, may hold values from -3 to 3
- mix_out_large: bfloat16 [3, 384, 576], replicated, may hold values from -0.3125 to 0.3125
- mix_obias_large: float32 [3, 576], replicated, may hold values from -3 to 3
- chan_in: bfloat16 [3, 768, 3072], P(None, None, 'mp'), may hold values from -0.21875 to 0.21875
- chan_bias: float32 [3, 3072], P(None, 'mp'), may hold values from -3 to 3
- chan_out: bfloat16 [3, 3072, 768], P(None, 'mp'), may hold values from -0.109375 to 0.109375
- chan_obias: float32 [3, 768], P(None, 'mp'), may hold values from -3 to 3
- cot_small: bfloat16 [128, 196, 768], P('dp', None, 'mp'), may hold values from -6 to 6
- cot_large: bfloat16 [32, 576, 768], P('dp', None, 'mp'), may hold values from -6 to 6
Outputs:
- out_small: bfloat16 [128, 196, 768], P('dp', None, 'mp')
- out_large: bfloat16 [32, 576, 768], P('dp', None, 'mp')
- grad_small: float32 [128, 196, 768], P('dp', None, 'mp')
- grad_large: float32 [32, 576, 768], P('dp', None, 'mp')
- grad_norm_gain: float32 [3, 2, 768], P(None, None, 'mp')
- grad_norm_shift: float32 [3, 2, 768], P(None, None, 'mp')
- grad_mix_in_small: float32 [3, 196, 384], replicated
- grad_mix_bias_small: float32 [3, 384], replicated
- grad_mix_out_small: float32 [3, 384, 196], replicated
- grad_mix_obias_small: float32 [3, 196], replicated
- grad_mix_in_large: float32 [3, 576, 384], replicated
- grad_mix_bias_large: float32 [3, 384], replicated
- grad_mix_out_large: float32 [3, 384, 576], replicated
- grad_mix_obias_large: float32 [3, 576], replicated
- grad_chan_in: float32 [3, 768, 3072], P(None, None, 'mp')
- grad_chan_bias: float32 [3, 3072], P(None, 'mp')
- grad_chan_out: float32 [3, 3072, 768], P(None, 'mp')
- grad_chan_obias: float32 [3, 768], P(None, 'mp')
Inputs may be any that keep to these rules, and one draw needn't show every extreme that they name: `image_counts`: column 0 counts the live 224 pixel images of an index of dp, from 1 to 8; column 1 the live 384 pixel images, from 0 to 2; live images fill the first slots of that index; each column reaches its most on some index in every draw.
All inputs are finite; a program needn't handle non-finite values.
Results may differ from a plain program's by a relative error of at most 0.02.
Values may be sent and summed in bfloat16 or wider, within the bound.
No kernel may reach another device: no remote copies, remote signals or barrier semaphores. Data moves between devices by JAX's collectives and lax.ppermute only.
A program may use at most 448 MiB of HBM per device.

v0:
```python
import jax
import jax.numpy as jnp
from jax import lax
from jax.sharding import PartitionSpec as P

EPS = 1e-06
F32 = jnp.float32
B16 = jnp.bfloat16


def gelu_exact(field):
    return jax.nn.gelu(field, approximate=False)


def gelu_pull(point, grad_in):
    return jax.vjp(gelu_exact, point)[1](grad_in)[0]


def norm_apply(stream, gain_vec, shift_vec, feature_count):
    totals = lax.psum(
        (
            jnp.sum(stream[0], -1),
            jnp.sum(stream[0] * stream[0], -1),
            jnp.sum(stream[1], -1),
            jnp.sum(stream[1] * stream[1], -1),
        ),
        "mp",
    )
    centred_list, scale_list, normed_list = ([], [], [])
    for set_index in range(2):
        row_mean = totals[2 * set_index] / feature_count
        spread = totals[2 * set_index + 1] / feature_count - row_mean * row_mean
        row_scale = lax.rsqrt(spread + EPS)
        centred = (stream[set_index] - row_mean[..., None]) * row_scale[..., None]
        centred_list.append(centred)
        scale_list.append(row_scale)
        normed_list.append(centred * gain_vec + shift_vec)
    return (centred_list, scale_list, normed_list)


def norm_back(grad_list, centred_list, scale_list, gain_vec, feature_count):
    scaled = [grad_list[0] * gain_vec, grad_list[1] * gain_vec]
    totals = lax.psum(
        (
            jnp.sum(scaled[0], -1),
            jnp.sum(scaled[0] * centred_list[0], -1),
            jnp.sum(scaled[1], -1),
            jnp.sum(scaled[1] * centred_list[1], -1),
        ),
        "mp",
    )
    back_list = []
    for set_index in range(2):
        inner_term = (
            scaled[set_index]
            - totals[2 * set_index][..., None] / feature_count
            - centred_list[set_index] * (totals[2 * set_index + 1][..., None] / feature_count)
        )
        back_list.append(scale_list[set_index][..., None] * inner_term)
    gain_grad = jnp.sum(grad_list[0] * centred_list[0], axis=(0, 1)) + jnp.sum(
        grad_list[1] * centred_list[1], axis=(0, 1)
    )
    shift_grad = jnp.sum(grad_list[0], axis=(0, 1)) + jnp.sum(grad_list[1], axis=(0, 1))
    return (back_list, gain_grad, shift_grad)


def body(
    image_small,
    image_large,
    image_counts,
    norm_gain,
    norm_shift,
    mix_in_small,
    mix_bias_small,
    mix_out_small,
    mix_obias_small,
    mix_in_large,
    mix_bias_large,
    mix_out_large,
    mix_obias_large,
    chan_in,
    chan_bias,
    chan_out,
    chan_obias,
    cot_small,
    cot_large,
):
    feature_count = norm_gain.shape[2] * lax.axis_size("mp")
    layers = norm_gain.shape[0]
    slot_count = (image_small.shape[0], image_large.shape[0])
    live_masks = [
        (jnp.arange(slot_count[k], dtype=jnp.int32) < image_counts[0, k]).astype(F32)[:, None, None]
        for k in range(2)
    ]
    mixers = (
        (mix_in_small, mix_bias_small, mix_out_small, mix_obias_small),
        (mix_in_large, mix_bias_large, mix_out_large, mix_obias_large),
    )
    stream = [image_small.astype(F32), image_large.astype(F32)]
    kept_state = []
    for layer_pos in range(layers):
        centred_one, scale_one, normed_one = norm_apply(
            stream, norm_gain[layer_pos, 0], norm_shift[layer_pos, 0], feature_count
        )
        lowered, pre_list, act_list, mixed_list = ([], [], [], [])
        for set_index in range(2):
            token_in, token_bias, token_out, token_obias = mixers[set_index]
            normed_low = normed_one[set_index].astype(B16)
            pre_act = (
                jnp.einsum(
                    "nsc,sh->nhc", normed_low, token_in[layer_pos], preferred_element_type=F32
                )
                + token_bias[layer_pos][None, :, None]
            )
            activated = gelu_exact(pre_act).astype(B16)
            branch = jnp.einsum(
                "nhc,hs->nsc", activated, token_out[layer_pos], preferred_element_type=F32
            )
            mixed_list.append(stream[set_index] + branch + token_obias[layer_pos][None, :, None])
            lowered.append(normed_low)
            pre_list.append(pre_act)
            act_list.append(activated)
        centred_two, scale_two, normed_two = norm_apply(
            mixed_list, norm_gain[layer_pos, 1], norm_shift[layer_pos, 1], feature_count
        )
        normed_rows = (normed_two[0].astype(B16), normed_two[1].astype(B16))
        weight_in = chan_in[layer_pos]
        gathered_rows = None
        hidden = (
            jnp.dot(
                lax.all_gather(normed_rows[0], "mp", axis=2, tiled=True),
                weight_in,
                preferred_element_type=F32,
            ),
            jnp.dot(
                lax.all_gather(normed_rows[1], "mp", axis=2, tiled=True),
                weight_in,
                preferred_element_type=F32,
            ),
        )
        hidden = [hidden[k] + chan_bias[layer_pos] for k in range(2)]
        hidden_low = [gelu_exact(hidden[k]).astype(B16) for k in range(2)]
        partial_value = [
            jnp.dot(hidden_low[k], chan_out[layer_pos], preferred_element_type=F32)
            for k in range(2)
        ]
        summed = (
            lax.psum_scatter(
                partial_value[0].astype(jnp.bfloat16), "mp", scatter_dimension=2, tiled=True
            ).astype(jnp.float32),
            lax.psum_scatter(
                partial_value[1].astype(jnp.bfloat16), "mp", scatter_dimension=2, tiled=True
            ).astype(jnp.float32),
        )
        kept_state.append(
            (
                centred_one,
                scale_one,
                lowered,
                pre_list,
                act_list,
                centred_two,
                scale_two,
                normed_rows,
                gathered_rows,
                hidden,
                hidden_low,
            )
        )
        stream = [mixed_list[k] + summed[k] + chan_obias[layer_pos] for k in range(2)]
    out_list = [(stream[k] * live_masks[k]).astype(B16) for k in range(2)]
    grad_stream = [cot_small.astype(F32) * live_masks[0], cot_large.astype(F32) * live_masks[1]]
    mix_terms = [None] * layers
    chan_terms = [None] * layers
    for layer_pos in reversed(range(layers)):
        (
            centred_one,
            scale_one,
            lowered,
            pre_list,
            act_list,
            centred_two,
            scale_two,
            normed_rows,
            gathered_rows,
            hidden,
            hidden_low,
        ) = kept_state[layer_pos]
        grad_low = (grad_stream[0].astype(B16), grad_stream[1].astype(B16))
        obias_grad = jnp.sum(grad_low[0].astype(F32), axis=(0, 1)) + jnp.sum(
            grad_low[1].astype(F32), axis=(0, 1)
        )
        gathered_grad = (
            lax.all_gather(grad_low[0], "mp", axis=2, tiled=True),
            lax.all_gather(grad_low[1], "mp", axis=2, tiled=True),
        )
        out_grad = jnp.einsum(
            "nsf,nsc->fc", hidden_low[0], gathered_grad[0], preferred_element_type=F32
        ) + jnp.einsum("nsf,nsc->fc", hidden_low[1], gathered_grad[1], preferred_element_type=F32)
        hidden_grad = [
            gelu_pull(
                hidden[k],
                jnp.einsum(
                    "nsc,fc->nsf", gathered_grad[k], chan_out[layer_pos], preferred_element_type=F32
                ),
            ).astype(B16)
            for k in range(2)
        ]
        bias_grad = jnp.sum(hidden_grad[0].astype(F32), axis=(0, 1)) + jnp.sum(
            hidden_grad[1].astype(F32), axis=(0, 1)
        )
        contribution = jnp.einsum(
            "nsk,nsf->kf",
            lax.all_gather(normed_rows[0], "mp", axis=2, tiled=True),
            hidden_grad[0],
            preferred_element_type=F32,
        ) + jnp.einsum(
            "nsk,nsf->kf",
            lax.all_gather(normed_rows[1], "mp", axis=2, tiled=True),
            hidden_grad[1],
            preferred_element_type=F32,
        )
        back_terms = [
            jnp.einsum(
                "nsf,cf->nsc", hidden_grad[k], chan_in[layer_pos], preferred_element_type=F32
            )
            for k in range(2)
        ]
        back_rows = (
            lax.psum_scatter(
                back_terms[0].astype(jnp.bfloat16), "mp", scatter_dimension=2, tiled=True
            ).astype(jnp.float32),
            lax.psum_scatter(
                back_terms[1].astype(jnp.bfloat16), "mp", scatter_dimension=2, tiled=True
            ).astype(jnp.float32),
        )
        norm_grad_two, gain_two, shift_two = norm_back(
            back_rows, centred_two, scale_two, norm_gain[layer_pos, 1], feature_count
        )
        mid_grad = [grad_stream[k] + norm_grad_two[k] for k in range(2)]
        token_terms = []
        norm_input = []
        for set_index in range(2):
            token_in, token_bias, token_out, token_obias = mixers[set_index]
            token_grad = mid_grad[set_index].astype(B16)
            token_obias_grad = jnp.sum(token_grad.astype(F32), axis=(0, 2))
            token_out_grad = jnp.einsum(
                "nhc,nsc->hs", act_list[set_index], token_grad, preferred_element_type=F32
            )
            act_grad = jnp.einsum(
                "nsc,hs->nhc", token_grad, token_out[layer_pos], preferred_element_type=F32
            )
            pre_grad = gelu_pull(pre_list[set_index], act_grad).astype(B16)
            token_bias_grad = jnp.sum(pre_grad.astype(F32), axis=(0, 2))
            token_in_grad = jnp.einsum(
                "nsc,nhc->sh", lowered[set_index], pre_grad, preferred_element_type=F32
            )
            norm_input.append(
                jnp.einsum("nhc,sh->nsc", pre_grad, token_in[layer_pos], preferred_element_type=F32)
            )
            token_terms += [token_in_grad, token_bias_grad, token_out_grad, token_obias_grad]
        norm_grad_one, gain_one, shift_one = norm_back(
            norm_input, centred_one, scale_one, norm_gain[layer_pos, 0], feature_count
        )
        grad_stream = [mid_grad[k] + norm_grad_one[k] for k in range(2)]
        chan_local = (
            contribution,
            bias_grad,
            out_grad,
            obias_grad,
            jnp.stack([gain_one, gain_two]),
            jnp.stack([shift_one, shift_two]),
        )
        mix_terms[layer_pos] = lax.psum(
            (
                token_terms[0],
                token_terms[1],
                token_terms[2],
                token_terms[3],
                token_terms[4],
                token_terms[5],
                token_terms[6],
                token_terms[7],
            ),
            ("dp", "mp"),
        )
        chan_terms[layer_pos] = (
            lax.psum(chan_local[0].astype(jnp.bfloat16), "dp").astype(jnp.float32),
            lax.psum(chan_local[1].astype(jnp.bfloat16), "dp").astype(jnp.float32),
            lax.psum(chan_local[2].astype(jnp.bfloat16), "dp").astype(jnp.float32),
            lax.psum(chan_local[3].astype(jnp.bfloat16), "dp").astype(jnp.float32),
            lax.psum(chan_local[4].astype(jnp.bfloat16), "dp").astype(jnp.float32),
            lax.psum(chan_local[5].astype(jnp.bfloat16), "dp").astype(jnp.float32),
        )
    mix_stacked = [jnp.stack([mix_terms[pos][item] for pos in range(layers)]) for item in range(8)]
    chan_stacked = [
        jnp.stack([chan_terms[pos][item] for pos in range(layers)]) for item in range(6)
    ]
    return (
        out_list[0],
        out_list[1],
        grad_stream[0],
        grad_stream[1],
        chan_stacked[4],
        chan_stacked[5],
        mix_stacked[0],
        mix_stacked[1],
        mix_stacked[2],
        mix_stacked[3],
        mix_stacked[4],
        mix_stacked[5],
        mix_stacked[6],
        mix_stacked[7],
        chan_stacked[0],
        chan_stacked[1],
        chan_stacked[2],
        chan_stacked[3],
    )


def solution(mesh):
    in_specs = (
        P("dp", None, "mp"),
        P("dp", None, "mp"),
        P("dp", None),
        P(None, None, "mp"),
        P(None, None, "mp"),
        P(),
        P(),
        P(),
        P(),
        P(),
        P(),
        P(),
        P(),
        P(None, None, "mp"),
        P(None, "mp"),
        P(None, "mp", None),
        P(None, "mp"),
        P("dp", None, "mp"),
        P("dp", None, "mp"),
    )
    out_specs = (
        P("dp", None, "mp"),
        P("dp", None, "mp"),
        P("dp", None, "mp"),
        P("dp", None, "mp"),
        P(None, None, "mp"),
        P(None, None, "mp"),
        P(),
        P(),
        P(),
        P(),
        P(),
        P(),
        P(),
        P(),
        P(None, None, "mp"),
        P(None, "mp"),
        P(None, "mp", None),
        P(None, "mp"),
    )
    return jax.shard_map(body, mesh=mesh, in_specs=in_specs, out_specs=out_specs, check_vma=False)
```

profile of v0, /device:TPU:1, one launch (start us, length us, event | category | flops | bytes accessed | tf_op | source)
XLA Modules:
  0.0 1629.6 jit_solution(15558474669974623325)
XLA Ops:
  17.9 7.2 all-reduce.13
  25.1 14.6 fusion.71
  64.1 31.3 %all-gather.19.cloned.1.call-done = bf16[2,576,768]{2,1,0:T(8,128)(2,1)} async-done(((bf16[2,576,384]{2,1,0:T(8,128)(2,1)}), bf16[2,576,768]{2,1,0:T(8,128)(2,1)}) %all-gather.19.cloned.1.call-update) | async-done | bytes 1769488 | tf_op jit(solution)/shard_map/all_gather | solution.py:136
  95.4 7.1 fusion.272
  102.6 17.4 %multiply_convert_fusion.5 = (bf16[2,576,1536]{2,1,0:T(8,128)(2,1)S(1)}, f32[2,576,1536]{2,1,0:T(8,128)}) fusion(f32[2,576,1536]{2,1,0:T(8,128)S(1)} %get-tuple-element.341, f32[1536]{0:T(1024)S(1)} %get-tuple-element.133, u8[576,1536]{1,0:T(8,128)(4,1)S(1)} %get-tuple-element.65, u8[576,1536]{1,0:T(8,128)(4,1)S(1)} %get-tuple-element.64), kind=kLoop, calls=%fused_computation.117 | loop fusion | flops 125632512 | bytes 19470336 | tf_op jit(solution)/shard_map/convert_element_type | solution.py:142
  127.4 6.5 copy.147
  139.2 9.2 fusion.160
  148.5 23.5 %multiply_convert_fusion.2 = (bf16[8,196,1536]{2,1,0:T(8,128)(2,1)S(1)}, f32[8,196,1536]{2,1,0:T(8,128)}) fusion(f32[8,196,1536]{2,1,0:T(8,128)S(1)} %get-tuple-element.340, f32[1536]{0:T(1024)S(1)} %get-tuple-element.133, u8[196,1536]{1,0:T(8,128)(4,1)S(1)} %get-tuple-element.59, u8[196,1536]{1,0:T(8,128)(4,1)S(1)} %get-tuple-element.58), kind=kLoop, calls=%fused_computation.54 | loop fusion | flops 170999808 | bytes 24692736 | tf_op jit(solution)/shard_map/convert_element_type | solution.py:142
  174.2 6.9 fusion.220
  186.1 6.3 reshape.334
  202.4 27.0 %reduce-scatter.37.cloned.1.call-done = bf16[384,1568]{1,0:T(8,128)(2,1)} async-done(((bf16[768,1568]{1,0:T(8,128)(2,1)}), bf16[384,1568]{1,0:T(8,128)(2,1)}) %reduce-scatter.37.cloned.1.call-update) | async-done | bytes 1204240
  245.4 14.2 fusion.69
  271.8 6.6 all-reduce.10
  284.2 31.4 %all-gather.21.cloned.1.call-done = bf16[2,576,768]{2,1,0:T(8,128)(2,1)} async-done(((bf16[2,576,384]{2,1,0:T(8,128)(2,1)}), bf16[2,576,768]{2,1,0:T(8,128)(2,1)}) %all-gather.21.cloned.1.call-update) | async-done | bytes 1769488 | tf_op jit(solution)/shard_map/all_gather | solution.py:136
  315.6 7.1 fusion.273
  322.7 17.4 %multiply_convert_fusion.4 = (bf16[2,576,1536]{2,1,0:T(8,128)(2,1)S(1)}, f32[2,576,1536]{2,1,0:T(8,128)}) fusion(f32[2,576,1536]{2,1,0:T(8,128)S(1)} %get-tuple-element.347, f32[1536]{0:T(1024)S(1)} %get-tuple-element.134, u8[576,1536]{1,0:T(8,128)(4,1)S(1)} %get-tuple-element.63, u8[576,1536]{1,0:T(8,128)(4,1)S(1)} %get-tuple-element.62), kind=kLoop, calls=%fused_computation.104 | loop fusion | flops 125632512 | bytes 19470336 | tf_op jit(solution)/shard_map/convert_element_type | solution.py:142
  347.6 6.5 copy.149
  359.4 9.3 fusion.161
  368.6 23.5 %multiply_convert_fusion.1 = (bf16[8,196,1536]{2,1,0:T(8,128)(2,1)S(1)}, f32[8,196,1536]{2,1,0:T(8,128)}) fusion(f32[8,196,1536]{2,1,0:T(8,128)S(1)} %get-tuple-element.346, f32[1536]{0:T(1024)S(1)} %get-tuple-element.134, u8[196,1536]{1,0:T(8,128)(4,1)S(1)} %get-tuple-element.57, u8[196,1536]{1,0:T(8,128)(4,1)S(1)} %get-tuple-element.56), kind=kLoop, calls=%fused_computation.41 | loop fusion | flops 170999808 | bytes 24692736 | tf_op jit(solution)/shard_map/convert_element_type | solution.py:142
  394.4 6.9 fusion.226
  406.3 6.3 reshape.336
  422.4 27.2 %reduce-scatter.39.cloned.1.call-done = bf16[384,1568]{1,0:T(8,128)(2,1)} async-done(((bf16[768,1568]{1,0:T(8,128)(2,1)}), bf16[384,1568]{1,0:T(8,128)(2,1)}) %reduce-scatter.39.cloned.1.call-update) | async-done | bytes 1204240
  465.6 14.3 fusion.67
  491.8 6.8 all-reduce.8
  509.4 25.7 %all-gather.23.cloned.1.call-done = bf16[2,576,768]{2,1,0:T(8,128)(2,1)} async-done(((bf16[2,576,384]{2,1,0:T(8,128)(2,1)}), bf16[2,576,768]{2,1,0:T(8,128)(2,1)}) %all-gather.23.cloned.1.call-update) | async-done | bytes 1769488 | tf_op jit(solution)/shard_map/all_gather | solution.py:136
  535.1 7.1 fusion.274
  545.2 17.5 %multiply_convert_fusion.3 = (bf16[2,576,1536]{2,1,0:T(8,128)(2,1)}, f32[2,576,1536]{2,1,0:T(8,128)}) fusion(f32[2,576,1536]{2,1,0:T(8,128)S(1)} %get-tuple-element.353, f32[1536]{0:T(1024)S(1)} %copy-done.102, u8[576,1536]{1,0:T(8,128)(4,1)S(1)} %get-tuple-element.61, u8[576,1536]{1,0:T(8,128)(4,1)S(1)} %get-tuple-element.60), kind=kLoop, calls=%fused_computation.91 | loop fusion | flops 125632512 | bytes 19470336 | tf_op jit(solution)/shard_map/convert_element_type | solution.py:142
  566.5 9.9 convert_reduce_fusion.3
  584.1 6.5 copy.159
  595.9 6.9 fusion.290
  602.8 6.5 copy.151
  614.4 9.7 fusion.162
  627.8 24.0 %multiply_convert_fusion = (bf16[8,196,1536]{2,1,0:T(8,128)(2,1)}, f32[8,196,1536]{2,1,0:T(8,128)}) fusion(f32[8,196,1536]{2,1,0:T(8,128)S(1)} %get-tuple-element.352, f32[1536]{0:T(1024)S(1)} %copy-done.102, u8[196,1536]{1,0:T(8,128)(4,1)S(1)} %get-tuple-element.55, u8[196,1536]{1,0:T(8,128)(4,1)S(1)} %get-tuple-element.54), kind=kLoop, calls=%fused_computation.28 | loop fusion | flops 170999808 | bytes 24692736 | tf_op jit(solution)/shard_map/convert_element_type | solution.py:142
  651.7 14.5 convert_reduce_fusion
  668.4 6.9 fusion.229
  680.5 6.4 reshape.346
  687.5 8.6 fusion.232
  701.3 6.3 reshape.338
  707.7 8.0 fusion.492
  756.9 6.7 all-reduce.7
  763.6 21.9 %reduce-scatter.41.cloned.1.call-done = bf16[384,1568]{1,0:T(8,128)(2,1)} async-done(((bf16[768,1568]{1,0:T(8,128)(2,1)}), bf16[384,1568]{1,0:T(8,128)(2,1)}) %reduce-scatter.41.cloned.1.call-update) | async-done | bytes 1204240
  838.9 19.6 %all-gather.33.cloned.1.call-done = bf16[2,576,768]{2,1,0:T(8,128)(2,1)} async-done(((bf16[2,576,384]{2,1,0:T(8,128)(2,1)}), bf16[2,576,768]{2,1,0:T(8,128)(2,1)}) %all-gather.33.cloned.1.call-update) | async-done | bytes 1769488 | tf_op jit(solution)/shard_map/all_gather | solution.py:195
  858.5 10.9 convert_reduce_fusion.4
  877.1 6.6 copy.161
  898.0 14.5 convert_reduce_fusion.1
  914.8 6.9 fusion.223
  926.7 6.3 reshape.348
  936.5 6.9 fusion.491
  989.5 6.7 convert_reduce_fusion.7
  1009.7 7.5 all-reduce.4
  1036.7 19.2 %all-gather.35.cloned.1.call-done = bf16[2,576,768]{2,1,0:T(8,128)(2,1)} async-done(((bf16[2,576,384]{2,1,0:T(8,128)(2,1)}), bf16[2,576,768]{2,1,0:T(8,128)(2,1)}) %all-gather.35.cloned.1.call-update) | async-done | bytes 1769488 | tf_op jit(solution)/shard_map/all_gather | solution.py:195
  1055.9 9.9 convert_reduce_fusion.5
  1073.5 6.5 copy.163
  1094.7 13.9 convert_reduce_fusion.2
  1120.4 6.5 reshape.350
  1133.9 7.5 fusion.490
  1183.9 6.8 convert_reduce_fusion.8
  1207.1 7.8 all-reduce.2
  1239.7 44.3 %all-reduce = (f32[1,384]{1,0:T(1,128)}, f32[1,384]{1,0:T(1,128)}, f32[1,384]{1,0:T(1,128)}, f32[1,196]{1,0:T(1,128)}, f32[1,196]{1,0:T(1,128)}, /*index=5*/f32[...) all-reduce(f32[1,384]{1,0:T(1,128)} %stack.262, ...), channel_id=1, replica_groups=mesh['dp'=16,'mp'=2] {'dp','mp'}, use_global_device_ids=true, to_apply=%region_146.0 | all-reduce | flops 4620 | bytes 36960 | tf_op jit(solution)/shard_map/psum | solution.py:274
  1286.5 57.2 %all-reduce.14 = (bf16[1,2,384]{2,1,0:T(2,128)(2,1)}, bf16[1,2,384]{2,1,0:T(2,128)(2,1)}, bf16[1,2,384]{2,1,0:T(2,128)(2,1)}, bf16[1,2,384]{2,1,0:T(2,128)(2,1)}...) all-reduce(bf16[1,2,384]{2,1,0:T(2,128)(2,1)} %maximum_bitcast_fusi, ...), channel_id=1, replica_groups=mesh['dp'=16,'mp'=2] {'dp'}, use_global_device_ids=true, to_apply=%region_122.0 | all-reduce | flops 10368 | bytes 41472 | tf_op jit(solution)/shard_map/psum | solution.py:292
  1358.3 74.4 %all-reduce.21.cloned.1.call-done = (bf16[1,768,1536]{2,1,0:T(8,128)(2,1)}, bf16[1,768,1536]{2,1,0:T(8,128)(2,1)}, bf16[1,768,1536]{2,1,0:T(8,128)(2,1)}, bf16[1...) async-done(((bf16[1,768,1536]{2,1,0:T(8,128)(2,1)}, bf16[1,768,1536]{2,1,0:T(8,128)(2,1)}, bf16[1,768,1536]{2,1,0:T(8,128)(2,1)}, ...) | async-done | bytes 14155792 | tf_op jit(solution)/shard_map/psum | solution.py:288
  1432.7 9.6 maximum_convert_fusion
  1442.4 6.8 maximum_convert_fusion.1
  1449.1 165.0 %all-reduce.19.cloned.1.call-done = (f32[1,196,384]{2,1,0:T(8,128)}, f32[1,196,384]{2,1,0:T(8,128)}, f32[1,196,384]{2,1,0:T(8,128)}, f32[1,384,196]{1,2,0:T(8,12...) async-done(((f32[1,196,384]{2,1,0:T(8,128)}, ...) | async-done | bytes 7114768 | tf_op jit(solution)/shard_map/psum | solution.py:274
  (754 shorter events, 563.3 us)
Async XLA Ops:
  7.2 88.2 %all-gather.19.cloned.1.call-start = ((), (), s32[]{:S(2)}) async-start(), calls=%async_computation.15 | async-start | bytes 2654208 | tf_op jit(solution)/shard_map/all_gather | solution.py:136
  10.0 29.7 %copy-start.170 = (f32[384]{0:T(512)}, f32[384]{0:T(512)S(1)}, u32[]{:S(2)}) copy-start(f32[384]{0:T(512)S(1)} %get-tuple-element.157) | copy-start | bytes 4612
  10.0 235.4 %copy-start.172 = (f32[384]{0:T(512)}, f32[384]{0:T(512)S(1)}, u32[]{:S(2)}) copy-start(f32[384]{0:T(512)S(1)} %get-tuple-element.158) | copy-start | bytes 4612
  17.9 24.5 %copy-start.139 = (f32[384]{0:T(512)}, f32[384]{0:T(512)S(1)}, u32[]{:S(2)}) copy-start(f32[384]{0:T(512)S(1)} %get-tuple-element.385) | copy-start | bytes 4612
  17.9 24.5 %copy-start.177 = (f32[384]{0:T(512)}, f32[384]{0:T(512)S(1)}, u32[]{:S(2)}) copy-start(f32[384]{0:T(512)S(1)} %get-tuple-element.148) | copy-start | bytes 4612
  17.9 43.0 %copy-start.84 = (f32[384]{0:T(512)}, f32[384]{0:T(512)S(1)}, u32[]{:S(2)}) copy-start(f32[384]{0:T(512)S(1)} %get-tuple-element.386) | copy-start | bytes 4612
  17.9 244.5 %copy-start.131 = (f32[384]{0:T(512)}, f32[384]{0:T(512)S(1)}, u32[]{:S(2)}) copy-start(f32[384]{0:T(512)S(1)} %get-tuple-element.387) | copy-start | bytes 4612
  17.9 244.5 %copy-start.179 = (f32[384]{0:T(512)}, f32[384]{0:T(512)S(1)}, u32[]{:S(2)}) copy-start(f32[384]{0:T(512)S(1)} %get-tuple-element.146) | copy-start | bytes 4612
  25.1 14.6 copy-start.113
  25.1 14.6 copy-start.115
  25.1 17.3 %copy-start.118 = (f32[2,576]{1,0:T(2,128)}, f32[2,576]{1,0:T(2,128)S(1)}, u32[]{:S(2)}) copy-start(f32[2,576]{1,0:T(2,128)S(1)} %get-tuple-element.329) | copy-start | bytes 13828
  25.1 17.3 %copy-start.120 = (f32[2,576]{1,0:T(2,128)}, f32[2,576]{1,0:T(2,128)S(1)}, u32[]{:S(2)}) copy-start(f32[2,576]{1,0:T(2,128)S(1)} %get-tuple-element.330) | copy-start | bytes 13828
  25.1 14.6 copy-start.47
  42.4 194.4 %copy-start.4 = (f32[8,196,384]{2,1,0:T(8,128)}, f32[8,196,384]{2,1,0:T(8,128)S(1)}, u32[]{:S(2)}) copy-start(f32[8,196,384]{2,1,0:T(8,128)S(1)} %get-tuple-element.337) | copy-start | bytes 7225348
  60.7 78.5 %all-gather.13.cloned.1.call-start = ((), (), s32[]{:S(2)}) async-start(), calls=%async_computation.12 | async-start | bytes 3686400 | tf_op jit(solution)/shard_map/all_gather | solution.py:131
  63.0 130.3 %reduce-scatter.43.cloned.1.call-start = ((), (), s32[]{:S(2)}) async-start(), calls=%async_computation.27 | async-start | bytes 2654208
  64.1 84.4 %copy-start.98 = (f32[1536]{0:T(1024)}, f32[1536]{0:T(1024)S(1)}, u32[]{:S(2)}) copy-start(f32[1536]{0:T(1024)S(1)} %get-tuple-element.133) | copy-start | bytes 18436
  64.1 304.5 %copy-start.100 = (f32[1536]{0:T(1024)}, f32[1536]{0:T(1024)S(1)}, u32[]{:S(2)}) copy-start(f32[1536]{0:T(1024)S(1)} %get-tuple-element.134) | copy-start | bytes 18436
  102.6 17.4 %copy-start.39 = (f32[2,576,1536]{2,1,0:T(8,128)}, f32[2,576,1536]{2,1,0:T(8,128)S(1)}, u32[]{:S(2)}) copy-start(f32[2,576,1536]{2,1,0:T(8,128)S(1)} %get-tuple-element.341) | copy-start | bytes 21233668
  139.0 90.4 %reduce-scatter.37.cloned.1.call-start = ((), (), s32[]{:S(2)}) async-start(), calls=%async_computation.24 | async-start | bytes 3833856
  148.5 23.5 %copy-start.31 = (f32[8,196,1536]{2,1,0:T(8,128)}, f32[8,196,1536]{2,1,0:T(8,128)S(1)}, u32[]{:S(2)}) copy-start(f32[8,196,1536]{2,1,0:T(8,128)S(1)} %get-tuple-element.340) | copy-start | bytes 28901380
  192.4 123.2 %all-gather.21.cloned.1.call-start = ((), (), s32[]{:S(2)}) async-start(), calls=%async_computation.16 | async-start | bytes 2654208 | tf_op jit(solution)/shard_map/all_gather | solution.py:136
  245.3 14.3 copy-start.103
  245.4 14.3 copy-start.106
  245.4 14.3 copy-start.11
  262.3 194.7 %copy-start = (f32[8,196,384]{2,1,0:T(8,128)}, f32[8,196,384]{2,1,0:T(8,128)S(1)}, u32[]{:S(2)}) copy-start(f32[8,196,384]{2,1,0:T(8,128)S(1)} %get-tuple-element.343) | copy-start | bytes 7225348
  281.9 77.4 %all-gather.15.cloned.1.call-start = ((), (), s32[]{:S(2)}) async-start(), calls=%async_computation.13 | async-start | bytes 3686400 | tf_op jit(solution)/shard_map/all_gather | solution.py:131
  284.2 128.7 %reduce-scatter.45.cloned.1.call-start = ((), (), s32[]{:S(2)}) async-start(), calls=%async_computation.28 | async-start | bytes 2654208
  322.7 17.4 %copy-start.40 = (f32[2,576,1536]{2,1,0:T(8,128)}, f32[2,576,1536]{2,1,0:T(8,128)S(1)}, u32[]{:S(2)}) copy-start(f32[2,576,1536]{2,1,0:T(8,128)S(1)} %get-tuple-element.347) | copy-start | bytes 21233668
  359.1 90.5 %reduce-scatter.39.cloned.1.call-start = ((), (), s32[]{:S(2)}) async-start(), calls=%async_computation.25 | async-start | bytes 3833856
  368.6 23.5 %copy-start.32 = (f32[8,196,1536]{2,1,0:T(8,128)}, f32[8,196,1536]{2,1,0:T(8,128)S(1)}, u32[]{:S(2)}) copy-start(f32[8,196,1536]{2,1,0:T(8,128)S(1)} %get-tuple-element.346) | copy-start | bytes 28901380
  412.6 122.5 %all-gather.23.cloned.1.call-start = ((), (), s32[]{:S(2)}) async-start(), calls=%async_computation.17 | async-start | bytes 2654208 | tf_op jit(solution)/shard_map/all_gather | solution.py:136
  465.6 14.4 copy-start.109
  465.6 14.3 copy-start.111
  465.6 14.3 copy-start.15
  465.6 14.3 copy-start.156
  501.4 65.1 %all-gather.31.cloned.1.call-start = ((), (), s32[]{:S(2)}) async-start(), calls=%async_computation.21 | async-start | bytes 2654208 | tf_op jit(solution)/shard_map/all_gather | solution.py:195
  504.1 110.3 %all-gather.17.cloned.1.call-start = ((), (), s32[]{:S(2)}) async-start(), calls=%async_computation.14 | async-start | bytes 3686400 | tf_op jit(solution)/shard_map/all_gather | solution.py:131
  505.7 29.4 %copy-start.102 = (f32[1536]{0:T(1024)S(1)}, f32[1536]{0:T(1024)}, u32[]{:S(2)}) copy-start(f32[1536]{0:T(1024)} %get-tuple-element.132) | copy-start | bytes 18436
  505.8 146.0 %all-gather.25.cloned.1.call-start = ((), (), s32[]{:S(2)}) async-start(), calls=%async_computation.18 | async-start | bytes 3686400 | tf_op jit(solution)/shard_map/all_gather | solution.py:194
  509.3 220.3 %reduce-scatter.55.cloned.1.call-start = ((), (), s32[]{:S(2)}) async-start(), calls=%async_computation.33 | async-start | bytes 2654208
  595.7 140.9 %reduce-scatter.47.cloned.1.call-start = ((), (), s32[]{:S(2)}) async-start(), calls=%async_computation.29 | async-start | bytes 2654208
  614.3 132.5 %reduce-scatter.49.cloned.1.call-start = ((), (), s32[]{:S(2)}) async-start(), calls=%async_computation.30 | async-start | bytes 3833856
  686.9 98.5 %reduce-scatter.41.cloned.1.call-start = ((), (), s32[]{:S(2)}) async-start(), calls=%async_computation.26 | async-start | bytes 3833856
  707.6 150.9 %all-gather.33.cloned.1.call-start = ((), (), s32[]{:S(2)}) async-start(), calls=%async_computation.22 | async-start | bytes 2654208 | tf_op jit(solution)/shard_map/all_gather | solution.py:195
  707.7 12.8 slice-start.4
  763.6 29.3 %copy-start.141 = (f32[384]{0:T(512)S(1)}, f32[384]{0:T(512)}, u32[]{:S(2)}) copy-start(f32[384]{0:T(512)} %get-tuple-element.153) | copy-start | bytes 4612
  826.0 72.0 %all-gather.27.cloned.1.call-start = ((), (), s32[]{:S(2)}) async-start(), calls=%async_computation.19 | async-start | bytes 3686400 | tf_op jit(solution)/shard_map/all_gather | solution.py:194
  836.3 22.1 %copy-start.101 = (f32[1536]{0:T(1024)S(1)}, f32[1536]{0:T(1024)}, u32[]{:S(2)}) copy-start(f32[1536]{0:T(1024)} %copy-done.100) | copy-start | bytes 18436
  838.8 118.7 %reduce-scatter.57.cloned.1.call-start = ((), (), s32[]{:S(2)}) async-start(), calls=%async_computation.34 | async-start | bytes 2654208
  888.7 81.4 %reduce-scatter.51.cloned.1.call-start = ((), (), s32[]{:S(2)}) async-start(), calls=%async_computation.31 | async-start | bytes 3833856
  933.1 122.8 %all-gather.35.cloned.1.call-start = ((), (), s32[]{:S(2)}) async-start(), calls=%async_computation.23 | async-start | bytes 2654208 | tf_op jit(solution)/shard_map/all_gather | solution.py:195
  936.5 11.6 slice-start.2
  1022.3 72.4 %all-gather.29.cloned.1.call-start = ((), (), s32[]{:S(2)}) async-start(), calls=%async_computation.20 | async-start | bytes 3686400 | tf_op jit(solution)/shard_map/all_gather | solution.py:194
  1032.5 23.4 %copy-start.99 = (f32[1536]{0:T(1024)S(1)}, f32[1536]{0:T(1024)}, u32[]{:S(2)}) copy-start(f32[1536]{0:T(1024)} %copy-done.98) | copy-start | bytes 18436
  1036.5 118.9 %reduce-scatter.59.cloned.1.call-start = ((), (), s32[]{:S(2)}) async-start(), calls=%async_computation.35 | async-start | bytes 2654208
  1085.0 79.8 %reduce-scatter.53.cloned.1.call-start = ((), (), s32[]{:S(2)}) async-start(), calls=%async_computation.32 | async-start | bytes 3833856
  1126.9 305.9 %all-reduce.21.cloned.1.call-start = ((), (), s32[]{:S(2)}) async-start(), calls=%async_computation.37 | async-start | bytes 28311552 | tf_op jit(solution)/shard_map/psum | solution.py:288
  1133.9 12.2 slice-start
  1155.3 458.8 %all-reduce.19.cloned.1.call-start = ((), (), s32[]{:S(2)}) async-start(), calls=%async_computation.36 | async-start | bytes 14303232 | tf_op jit(solution)/shard_map/psum | solution.py:274
  1203.7 12.8 copy-start.178
  1230.9 55.6 %copy-start.117 = (bf16[1,1536]{1,0:T(2,128)(2,1)S(1)}, bf16[1,1536]{1,0:T(2,128)(2,1)}, u32[]{:S(2)}) copy-start(bf16[1,1536]{1,0:T(2,128)(2,1)} %stack.295) | copy-start | bytes 9220
  1230.9 124.7 %copy-start.29 = (f32[2,576,384]{2,1,0:T(8,128)S(1)}, f32[2,576,384]{2,1,0:T(8,128)}, u32[]{:S(2)}) copy-start(f32[2,576,384]{2,1,0:T(8,128)} %copy-done.28) | copy-start | bytes 5308420
  1230.9 124.7 %copy-start.44 = (f32[2,384,576]{1,2,0:T(8,128)S(1)}, f32[2,384,576]{1,2,0:T(8,128)}, u32[]{:S(2)}) copy-start(f32[2,384,576]{1,2,0:T(8,128)} %copy-done.43) | copy-start | bytes 5308420
  (185 other events, 919.7 us)
Sparse Core Ops, SparseCore 0:
  60.9 34.5 all-gather.18
  97.6 37.1 all-gather.12
  139.1 28.2 reduce-scatter.42
  192.5 36.8 reduce-scatter.36
  282.0 33.4 all-gather.20
  317.5 37.1 all-gather.14
  359.2 28.2 reduce-scatter.44
  412.7 36.8 reduce-scatter.38
  501.6 33.4 all-gather.22
  537.1 29.4 all-gather.30
  568.6 37.1 all-gather.16
  607.3 37.1 all-gather.24
  646.7 28.2 reduce-scatter.54
  677.2 28.2 reduce-scatter.46
  708.2 36.8 reduce-scatter.48
  747.8 37.5 reduce-scatter.40
  826.1 32.3 all-gather.32
  859.9 37.1 all-gather.26
  899.4 28.2 reduce-scatter.56
  933.2 36.9 reduce-scatter.50
  1022.4 33.4 all-gather.34
  1057.5 37.1 all-gather.28
  1096.9 28.2 reduce-scatter.58
  1128.0 36.8 reduce-scatter.52
  1171.1 261.5 all-reduce.20
  1440.1 173.9 all-reduce.18
where the time goes:
time: 1640 us; the launch traced here: 1630 us
  waiting for transfers between devices  457 us (28%)
  matrix products  428 us (26%)
  local copies, waits for them, and re-layouts  280 us (17%)
  other arithmetic  269 us (16%)
  blocking collectives  177 us (11%)
  between operations  17.2 us (1%)
    unnamed x496, local copies, waits for them, and re-layouts  260 us
    psum x1, waiting for transfers between devices, body(): lax.psum((token_terms[0], token_terms[1], token_terms[2], token_terms[3],...  165 us
    convert_element_type x6, other arithmetic, body(): hidden_low = [gelu_exact(hidden[k]).astype(B16) for k in range(2)]  123 us
    all_gather x3, waiting for transfers between devices, body(): lax.all_gather(normed_rows[1], 'mp', axis=2, tiled=True)  88.4 us
    unnamed x38, waiting for transfers between devices  80.6 us
    psum x1, waiting for transfers between devices, body(): lax.psum(chan_local[0].astype(jnp.bfloat16), 'dp').astype(jnp.float32)  74.4 us
    dot_general x6, matrix products, body(): jnp.einsum('nsc,fc->nsf', gathered_grad[k], chan_out[layer_pos], preferre...  73.6 us
    dot_general x6, matrix products, body(): jnp.einsum('nsc,sh->nhc', normed_low, token_in[layer_pos], preferred_elem...  61.3 us
  transfers between devices with their start and end apart: 26, of which 14 were waited for; matrix products, arithmetic and copies ran while one was open for 46% of the time, Pallas kernels for 0%

commit v1 on v0

--- a/solution.py
+++ b/solution.py
@@ -1,6 +1,10 @@
+import functools
+
 import jax
 import jax.numpy as jnp
 from jax import lax
+from jax.experimental import pallas as pl
+from jax.experimental.pallas import tpu as pltpu
 from jax.sharding import PartitionSpec as P
 
 EPS = 1e-06
@@ -64,7 +68,7 @@
     return (back_list, gain_grad, shift_grad)
 
 
-def body(
+def split_body(
     image_small,
     image_large,
     image_counts,
@@ -318,6 +322,946 @@
     )
 
 
+LANES = 128
+SIDE, CORE, QUARTER, PLACE = range(4)
+VMEM_LIMIT = 56 << 20
+COST_SCALE = 200
+
+
+def gelu_pair(point):
+    below = 0.5 + 0.5 * lax.erf(point * 0.7071067811865476)
+    bell = jnp.exp(point * point * -0.5) * 0.3989422804014327
+    return point * below, below + point * bell
+
+
+def kernel_call(
+    kernel, grid, in_specs, out_specs, out_shape, scratch=(), cost=None, aliases=None, prefetch=0
+):
+    return pl.pallas_call(
+        kernel,
+        grid_spec=pltpu.PrefetchScalarGridSpec(
+            num_scalar_prefetch=prefetch,
+            grid=grid,
+            in_specs=in_specs,
+            out_specs=out_specs,
+            scratch_shapes=list(scratch),
+        ),
+        out_shape=out_shape,
+        compiler_params=pltpu.CompilerParams(vmem_limit_bytes=VMEM_LIMIT),
+        cost_estimate=cost,
+        input_output_aliases=aliases or {},
+    )
+
+
+def cost_of(flops, nbytes):
+    return pl.CostEstimate(
+        flops=int(COST_SCALE * flops), bytes_accessed=int(COST_SCALE * nbytes), transcendentals=0
+    )
+
+
+def mark_spec():
+    return pl.BlockSpec(memory_space=pltpu.SMEM), jax.ShapeDtypeStruct((1, 1), F32)
+
+
+def column(row, size):
+    pad = -row.shape[1] % LANES
+    if pad:
+        row = jnp.concatenate([row, jnp.zeros((1, pad), F32)], 1)
+    return jnp.broadcast_to(row, (8, row.shape[1])).T[:size, 0:1]
+
+
+def pad_rows(value, size):
+    if value.shape[0] == size:
+        return value
+    return jnp.concatenate([value, jnp.zeros((size - value.shape[0], value.shape[1]), value.dtype)], 0)
+
+
+def dims_nt(left, right):
+    return lax.dot_general(left, right, (((1,), (1,)), ((), ())), preferred_element_type=F32)
+
+
+def dims_tn(left, right):
+    return lax.dot_general(left, right, (((0,), (0,)), ((), ())), preferred_element_type=F32)
+
+
+def dims_nn(left, right):
+    return jnp.dot(left, right, preferred_element_type=F32)
+
+
+def norm_block(field):
+    centred = field - jnp.mean(field, -1, keepdims=True)
+    scale = lax.rsqrt(jnp.mean(centred * centred, -1, keepdims=True) + EPS)
+    return centred * scale, scale
+
+
+def token_forward_kernel(x_ref, norm_ref, in_ref, bias_ref, out_ref, obias_ref, *rest):
+    (
+        mixed_ref,
+        rows_ref,
+        low_ref,
+        act_ref,
+        slope_ref,
+        vhat_one_ref,
+        vhat_two_ref,
+        scale_ref,
+        mark_ref,
+    ) = rest[-9:]
+    x = x_ref[...]
+    size = x.shape[0]
+    vhat, scale = norm_block(x)
+    vhat_one_ref[...] = vhat.astype(B16)
+    low = (vhat * norm_ref[0:1, :] + norm_ref[2:3, :]).astype(B16)
+    low_ref[...] = low
+    point = dims_tn(pad_rows(in_ref[...], size), low) + column(bias_ref[...], act_ref.shape[0])
+    act, slope = gelu_pair(point)
+    act = act.astype(B16)
+    act_ref[...] = act
+    slope_ref[...] = slope.astype(B16)
+    mixed = x + dims_nn(pad_rows(out_ref[...], size), act) + column(obias_ref[...], size)
+    mixed_ref[...] = mixed
+    vhat, scale_two = norm_block(mixed)
+    vhat_two_ref[...] = vhat.astype(B16)
+    rows_ref[...] = (vhat * norm_ref[1:2, :] + norm_ref[3:4, :]).astype(B16)
+    scale_ref[:, 0:1] = scale
+    scale_ref[:, 1:2] = scale_two
+    mark_ref[0, 0] = 0.0
+
+
+def row_block(patches, width, offset):
+    return pl.BlockSpec(
+        (pl.Element(patches), pl.Element(width)),
+        lambda i: ((offset // 16 + i * (patches // 16)) * 16, 0),
+    )
+
+
+def whole_spec(array):
+    return pl.BlockSpec(array.shape, lambda *i: (0, 0))
+
+
+def free_specs(arrays):
+    return [pl.BlockSpec(memory_space=pl.ANY)] * len(arrays)
+
+
+def layer_spec(array, pos):
+    return pl.BlockSpec(
+        (None,) + array.shape[1:], lambda *i: (pos,) + (0,) * (array.ndim - 1)
+    )
+
+
+def token_forward(x, pos, params, images, patches, offset, base, after=()):
+    total, width = x.shape
+    hidden = params[1].shape[2]
+    rows = images * patches
+    block = lambda size, lanes: pl.BlockSpec((size, lanes), lambda i: (i, 0))
+    placed = row_block(patches, width, offset)
+    shape = jax.ShapeDtypeStruct
+    mark = mark_spec()
+    return kernel_call(
+        token_forward_kernel,
+        (images,),
+        [placed] + [layer_spec(a, pos) for a in params] + free_specs(base + after),
+        [placed, placed]
+        + [block(patches, width)]
+        + [block(hidden, width)] * 2
+        + [block(patches, width)] * 2
+        + [block(patches, LANES), mark[0]],
+        [
+            shape((total, width), F32),
+            shape((total, width), B16),
+            shape((rows, width), B16),
+            shape((images * hidden, width), B16),
+            shape((images * hidden, width), B16),
+            shape((rows, width), B16),
+            shape((rows, width), B16),
+            shape((rows, LANES), F32),
+            mark[1],
+        ],
+        aliases={6 + i: i for i in range(len(base))},
+        cost=cost_of(4 * rows * hidden * width, 30 * rows * width),
+    )(x, *params, *base, *after)
+
+
+def join_kernel(info_ref, own_ref, got_ref, live_ref, joined_ref, mark_ref):
+    own, got = own_ref[...].astype(F32), got_ref[...].astype(F32)
+    first = info_ref[SIDE] == 0
+    live = live_ref[:, 0:1]
+    half = own.shape[1]
+    joined_ref[:, :half] = jnp.where(first, own, got) * live
+    joined_ref[:, half:] = jnp.where(first, got, own) * live
+    mark_ref[0, 0] = 0.0
+
+
+def join_features(info, own, got, live, tiles=4):
+    rows, half = own.shape
+    block = lambda lanes: pl.BlockSpec((rows // tiles, lanes), lambda i, _: (i, 0))
+    mark = mark_spec()
+    return kernel_call(
+        join_kernel,
+        (tiles,),
+        [block(half), block(half), block(LANES)],
+        [block(2 * half), mark[0]],
+        [jax.ShapeDtypeStruct((rows, 2 * half), F32), mark[1]],
+        prefetch=1,
+        cost=cost_of(0, 12 * rows * half),
+    )(info, own, got, live)
+
+
+def chan_forward_kernel(
+    part,
+    info_ref,
+    rows_ref,
+    mixed_ref,
+    in_own_ref,
+    out_own_ref,
+    in_near_ref,
+    in_far_ref,
+    out_near_ref,
+    out_far_ref,
+    bias_ref,
+    obias_ref,
+    *rest,
+):
+    quant_ref, slope_ref, total_ref, in_other_ref, out_other_ref, mark_ref = rest[-6:]
+    mark_ref[0, 0] = 0.0
+
+    @pl.when(pl.program_id(0) == 0)
+    def _():
+        place = info_ref[QUARTER]
+        for pieces, other_ref in (
+            ((in_near_ref, in_far_ref), in_other_ref),
+            ((out_near_ref, out_far_ref), out_other_ref),
+        ):
+            size = pieces[0].shape[1]
+            for k in range(4):
+                at = pl.multiple_of((place ^ k) * size, size)
+                other_ref[pl.ds(at, size), :] = pieces[k // 2][k % 2]
+
+    rows = rows_ref[...]
+    total = mixed_ref[...] + obias_ref[...]
+    units = in_own_ref.shape[1]
+    for side, (in_ref, out_ref) in enumerate(
+        ((in_own_ref, out_own_ref), (in_other_ref, out_other_ref))
+    ):
+        for at in range(0, units, part):
+            lanes = slice(at, at + part)
+            place = slice(side * units + at, side * units + at + part)
+            point = dims_nn(rows, in_ref[:, lanes]) + bias_ref[:, place]
+            quant, slope = gelu_pair(point)
+            quant = quant.astype(B16)
+            quant_ref[:, place] = quant
+            slope_ref[:, place] = slope.astype(B16)
+            total = total + dims_nn(quant, out_ref[lanes, :])
+    total_ref[...] = total
+
+
+def chan_forward(info, rows, mixed, own, found, layer, bias, obias, tile, part, after=()):
+    pos, at = layer
+    count, width = rows.shape
+    units = bias.shape[2]
+    half = units // 2
+    mark = mark_spec()
+    tiled = pl.BlockSpec((tile, width), lambda i, _: (i, 0))
+    lanes = pl.BlockSpec((tile, units), lambda i, _: (i, 0))
+    once = lambda rows, cols: pl.BlockSpec((rows, cols), lambda i, _: (0, 0))
+    layered = lambda a: pl.BlockSpec((None,) + a.shape[1:], lambda i, _: (pos, 0, 0))
+    pieces = lambda a: pl.BlockSpec(
+        (a.shape[0], None) + a.shape[2:], lambda i, _: (0, at, 0, 0)
+    )
+    return kernel_call(
+        functools.partial(chan_forward_kernel, part),
+        (count // tile,),
+        [tiled, tiled]
+        + [layered(a) for a in own]
+        + [pieces(a) for a in found]
+        + [layered(bias), layered(obias)]
+        + free_specs(after),
+        [lanes, lanes, tiled, once(width, half), once(half, width), mark[0]],
+        [
+            jax.ShapeDtypeStruct((count, units), B16),
+            jax.ShapeDtypeStruct((count, units), B16),
+            jax.ShapeDtypeStruct((count, width), F32),
+            jax.ShapeDtypeStruct((width, half), B16),
+            jax.ShapeDtypeStruct((half, width), B16),
+            mark[1],
+        ],
+        prefetch=1,
+        cost=cost_of(4 * count * units * width, 4 * count * units + 10 * count * width),
+    )(info, rows, mixed, *own, *found, bias, obias, *after)
+
+
+def chan_backward_kernel(
+    blocks,
+    first,
+    info_ref,
+    grad_ref,
+    rows_ref,
+    quant_ref,
+    slope_ref,
+    in_own_ref,
+    out_own_ref,
+    in_other_ref,
+    out_other_ref,
+    *rest,
+):
+    sum_ref, small_ref, back_ref, mark_ref, low_ref = rest[-5:]
+    mark_ref[0, 0] = 0.0
+    step = pl.program_id(0)
+
+    @pl.when(step == 0)
+    def _():
+        low = grad_ref[...].astype(B16)
+        low_ref[...] = low
+        small_ref[...] = jnp.zeros_like(small_ref)
+        if first:
+            small_ref[0:1, :] = jnp.sum(low.astype(F32), 0, keepdims=True)
+            back_ref[...] = jnp.zeros_like(back_ref)
+        else:
+            back_ref[...] = rest[0][...]
+
+    def body(other, in_ref, out_ref):
+        low = low_ref[...]
+        hidden = (dims_nt(low, out_ref[...]) * slope_ref[...].astype(F32)).astype(B16)
+        core = 1 - info_ref[CORE] if first else info_ref[CORE]
+        row = 1 + 2 * (info_ref[SIDE] ^ other) + core
+        small_ref[pl.ds(row, 1), :] = jnp.sum(hidden.astype(F32), 0, keepdims=True)
+        for item, grads in enumerate(
+            (dims_tn(hidden, rows_ref[...]), dims_tn(quant_ref[...], low))
+        ):
+            place = info_ref[PLACE]
+            size = grads.shape[0] // blocks
+            for k in range(blocks):
+                part = grads[k * size : (k + 1) * size, :].astype(B16)
+                sum_ref[item, k ^ place] = part
+        back_ref[...] += dims_nt(hidden, in_ref[...])
+
+    pl.when(step == 0)(lambda: body(1, in_other_ref, out_other_ref))
+    pl.when(step == 1)(lambda: body(0, in_own_ref, out_own_ref))
+
+
+def chan_backward(
+    info, grad, rows, quant, slope, own, other, pos, back, blocks, after=()
+):
+    count, width = rows.shape
+    chunk = own[0].shape[2] // 2
+    first = back is None
+    core = lambda info: 1 - info[CORE] if first else info[CORE]
+    lanes = pl.BlockSpec((count, chunk), lambda s, info: (0, 2 * (1 - s) + core(info)))
+    once = lambda rows, cols: pl.BlockSpec((rows, cols), lambda s, _: (0, 0))
+    part = (None, 2, blocks, chunk // blocks, width)
+    sums = pl.BlockSpec(part, lambda s, _: (s,) + (0,) * (len(part) - 1))
+    extra = () if first else (back,)
+    mark = mark_spec()
+    return kernel_call(
+        functools.partial(chan_backward_kernel, blocks, first),
+        (2,),
+        [once(count, width), once(count, width), lanes, lanes]
+        + [
+            pl.BlockSpec((None, width, chunk), lambda s, info: (pos, 0, core(info))),
+            pl.BlockSpec((None, chunk, width), lambda s, info: (pos, core(info), 0)),
+            pl.BlockSpec((width, chunk), lambda s, info: (0, core(info))),
+            pl.BlockSpec((chunk, width), lambda s, info: (core(info), 0)),
+        ]
+        + [once(count, width)] * len(extra)
+        + free_specs(after),
+        [sums, once(8, width), once(count, width), mark[0]],
+        [
+            jax.ShapeDtypeStruct((2,) + part[1:], B16),
+            jax.ShapeDtypeStruct((8, width), F32),
+            jax.ShapeDtypeStruct((count, width), F32),
+            mark[1],
+        ],
+        scratch=[pltpu.VMEM((count, width), B16)],
+        prefetch=1,
+        cost=cost_of(16 * count * chunk * width, 8 * count * chunk + 16 * count * width),
+    )(info, grad, rows, quant, slope, *own, *other, *extra, *after)
+
+
+def assemble_kernel(places, size, all_ref, *rest):
+    in_ref, out_ref, mark_ref, scratch = rest[-4:]
+    mark_ref[0, 0] = 0.0
+
+    def body(core):
+        for i, (in_place, out_place) in enumerate(places):
+            if i % 2 == core:
+                at = slice(in_place * size, (in_place + 1) * size)
+                scratch[at, :] = all_ref[i, 0:size, :].astype(F32)
+                at = slice(out_place * size, (out_place + 1) * size)
+                out_ref[at, :] = all_ref[i, size : 2 * size, :].astype(F32)
+        in_ref[...] = scratch[...].T
+
+    pl.when(pl.program_id(0) == 0)(lambda: body(0))
+    pl.when(pl.program_id(0) == 1)(lambda: body(1))
+
+
+def assemble(gathered, places, pos, layers, size, base):
+    count, _, width = gathered.shape
+    chunk = count // 2 * size
+    mark = mark_spec()
+    return kernel_call(
+        functools.partial(assemble_kernel, places, size),
+        (2,),
+        [pl.BlockSpec(gathered.shape, lambda s: (0, 0, 0))] + free_specs(base),
+        [
+            pl.BlockSpec((None, width, chunk), lambda s: (pos, 0, s)),
+            pl.BlockSpec((None, chunk, width), lambda s: (pos, s, 0)),
+            mark[0],
+        ],
+        [
+            jax.ShapeDtypeStruct((layers, width, 2 * chunk), F32),
+            jax.ShapeDtypeStruct((layers, 2 * chunk, width), F32),
+            mark[1],
+        ],
+        scratch=[pltpu.VMEM((chunk, width), F32)],
+        aliases={1 + i: i for i in range(len(base))},
+        cost=cost_of(0, 24 * chunk * width),
+    )(gathered, *base)
+
+
+def mark_kernel(*refs):
+    refs[-1][0, 0] = 0.0
+
+
+def mark_after(*arrays):
+    mark = mark_spec()
+    return kernel_call(mark_kernel, (1,), free_specs(arrays), mark[0], mark[1])(*arrays)
+
+
+def norm_block_back(grad, vhat, scale, gain):
+    scaled = grad * gain
+    inner = (
+        scaled
+        - jnp.mean(scaled, -1, keepdims=True)
+        - vhat * jnp.mean(scaled * vhat, -1, keepdims=True)
+    )
+    return scale * inner, jnp.sum(grad * vhat, 0, keepdims=True), jnp.sum(grad, 0, keepdims=True)
+
+
+def token_backward_kernel(
+    grad_ref,
+    back_ref,
+    vhat_two_ref,
+    scale_ref,
+    act_ref,
+    slope_ref,
+    low_ref,
+    vhat_one_ref,
+    norm_ref,
+    in_ref,
+    out_ref,
+    *rest,
+):
+    next_ref, grads_ref, small_ref, mark_ref = rest[-4:]
+    mark_ref[0, 0] = 0.0
+    first = pl.program_id(0) == 0
+
+    def add(ref, where, value):
+        @pl.when(first)
+        def _():
+            ref[where] = value
+
+        @pl.when(jnp.logical_not(first))
+        def _():
+            ref[where] += value
+
+    patches, width = low_ref.shape
+    hidden = act_ref.shape[0]
+    ones = jnp.ones((8, width), B16)
+    pl.when(first)(lambda: small_ref.__setitem__((Ellipsis,), jnp.zeros_like(small_ref)))
+    dv, gain_two, shift_two = norm_block_back(
+        back_ref[...], vhat_two_ref[...].astype(F32), scale_ref[:, 1:2], norm_ref[1:2, :]
+    )
+    mid = grad_ref[...].astype(F32) + dv
+    low = mid.astype(B16)
+    small_ref[5:6, :patches] += dims_nt(ones, low)[0:1, :]
+    add(grads_ref, (slice(None), slice(hidden, None)), dims_nt(low, act_ref[...]))
+    point = (dims_tn(pad_rows(out_ref[...], patches), low) * slope_ref[...].astype(F32)).astype(B16)
+    small_ref[4:5, :hidden] += dims_nt(ones, point)[0:1, :]
+    add(grads_ref, (slice(None), slice(0, hidden)), dims_nt(low_ref[...], point))
+    dv, gain_one, shift_one = norm_block_back(
+        dims_nn(pad_rows(in_ref[...], patches), point),
+        vhat_one_ref[...].astype(F32),
+        scale_ref[:, 0:1],
+        norm_ref[0:1, :],
+    )
+    next_ref[...] = mid + dv
+    for i, value in enumerate((gain_one, gain_two, shift_one, shift_two)):
+        small_ref[i : i + 1, :] += value
+
+
+def token_backward(grad, back, kept, pos, params, images, patches, offset, base, after=()):
+    low, act, slope, vhat_one, vhat_two, scale = kept
+    norm, w_in, _, w_out, _ = params
+    total, width = grad.shape
+    hidden = w_in.shape[2]
+    rows = images * patches
+    block = lambda size, lanes: pl.BlockSpec((size, lanes), lambda i: (i, 0))
+    placed = row_block(patches, width, offset)
+    shape = lambda r, c: jax.ShapeDtypeStruct((r, c), F32)
+    outs = [shape(patches, 2 * hidden), shape(8, width)]
+    mark = mark_spec()
+    return kernel_call(
+        token_backward_kernel,
+        (images,),
+        [placed, placed, block(patches, width), block(patches, LANES)]
+        + [block(hidden, width)] * 2
+        + [block(patches, width)] * 2
+        + [layer_spec(a, pos) for a in (norm, w_in, w_out)]
+        + free_specs(base + after),
+        [placed] + [whole_spec(a) for a in outs] + [mark[0]],
+        [shape(total, width)] + outs + [mark[1]],
+        aliases={11 + i: i for i in range(len(base))},
+        cost=cost_of(8 * rows * hidden * width, 30 * rows * width),
+    )(grad, back, vhat_two, scale, act, slope, low, vhat_one, norm, w_in, w_out, *base, *after)
+
+
+def image_split(mesh):
+    dp = mesh.shape["dp"]
+    return mesh.shape["mp"] == 2 and dp >= 8 and dp & (dp - 1) == 0
+
+
+def exchange(value, mask, over_mp):
+    count = lax.axis_size("dp")
+    if not mask:
+        return lax.ppermute(value, "mp", [(0, 1), (1, 0)])
+    if not over_mp:
+        return lax.ppermute(value, "dp", [(i, i ^ mask) for i in range(count)])
+    return lax.ppermute(
+        value, ("dp", "mp"), [(i, i ^ (2 * mask + 1)) for i in range(2 * count)]
+    )
+
+
+def dp_bit(bit):
+    return (lax.axis_index("dp") >> bit) & 1
+
+
+def join(value, other, flag, axis=0):
+    return jnp.where(
+        flag == 0,
+        jnp.concatenate([value, other], axis),
+        jnp.concatenate([other, value], axis),
+    )
+
+
+class Transfers:
+    def __init__(self):
+        self.flows = []
+        self.mark = None
+
+    def start(self, steps, first=False):
+        flow = {"steps": steps, "got": None}
+        self.flows.insert(0 if first else len(self.flows), flow)
+        return flow
+
+    def step(self, flow):
+        try:
+            if flow["got"] is None:
+                sends = next(flow["steps"])
+            else:
+                sends = flow["steps"].send(flow["got"])
+        except StopIteration:
+            self.flows.remove(flow)
+            return []
+        flow["got"] = [exchange(value, *masks) for value, *masks in sends]
+        return [send[0] for send in sends]
+
+    def tick(self):
+        ties = []
+        for flow in list(self.flows):
+            ties += self.step(flow)
+        return tuple(ties)
+
+    def finish(self, flow):
+        self.step(flow)
+
+    def arrived(self):
+        self.mark = mark_after(*[got for flow in self.flows for got in flow["got"]])
+
+    def zero(self):
+        return self.mark[0, 0]
+
+    def gate(self, value):
+        return value if self.mark is None else value + self.zero().astype(value.dtype)
+
+    def add(self, *values):
+        total = values[0].astype(F32)
+        for value in values[1:]:
+            total = total + value.astype(F32)
+        return (total + self.zero()).astype(B16)
+
+
+def one_step(line, value, found, delay=0):
+    for _ in range(delay):
+        yield []
+    (got,) = yield [(line.gate(value), 0, 1)]
+    found.append(got)
+
+
+def fetch_steps(line, weights, pos, found):
+    part = dp_bit(0) * 2 + dp_bit(1)
+    sends = []
+    for weight in weights:
+        size = weight.shape[1] // 4
+        quarter = lax.dynamic_slice(weight, (pos, part * size, 0), (1, size, weight.shape[2]))
+        sends.append(line.gate(quarter))
+    near = yield [(s, 0, 1) for s in sends]
+    got = yield [(line.gate(s), 2, 0) for s in near]
+    pairs = [line.gate(jnp.stack(p)) for p in zip(near, got)]
+    far = yield [(s, 1, 0) for s in pairs]
+    found += [pairs[0], far[0], pairs[1], far[1]]
+
+
+def far_blocks(line, value):
+    sends = [(value[k], k << 2, 0) for k in range(1, len(value))]
+    return value[0], sends
+
+
+def plain_sum(*values):
+    total = values[0].astype(F32)
+    for value in values[1:]:
+        total = total + value.astype(F32)
+    return total.astype(B16)
+
+
+def upper_grad_steps(line, send, keep, found):
+    (got,) = yield [(send, 1, 0)]
+    keep = keep[0]
+    half = keep.shape[2] // 2
+    low, high = slice(half), slice(half, None)
+    sum_of = lambda side, blocks: line.add(keep[side, :, blocks], got[side, :, blocks])
+    own = [sum_of(1, low), sum_of(1, high)]
+    other = [sum_of(0, low), sum_of(0, high)]
+    (got,) = yield [(other[1], 0, 1)]
+    own[1] = line.add(own[1], got)
+    got = yield [(other[0], 0, 1), (own[1], 2, 0)]
+    own = line.add(own[0], *got)
+    own = jnp.concatenate([own[0], own[1]], 1)
+    mine, sends = far_blocks(line, own)
+    got = yield sends
+    found.append(plain_sum(mine, *got))
+
+
+def lowest_grad_steps(line, send, keep, found):
+    (got,) = yield [(send, 1, 0)]
+    keep = keep[0]
+    half = keep.shape[2] // 2
+    low, high, every = slice(half), slice(half, None), slice(None)
+    sum_of = lambda side, item, blocks: line.add(keep[side, item, blocks], got[side, item, blocks])
+    in_other, in_low, in_high = sum_of(0, 0, every), sum_of(1, 0, low), sum_of(1, 0, high)
+    out_away = sum_of(every, 1, high)
+    out_own, out_other = sum_of(1, 1, low), sum_of(0, 1, low)
+    got = yield [(in_other, 0, 1), (out_away, 2, 0)]
+    in_low, in_high = line.add(in_low, got[0][:half]), line.add(in_high, got[0][half:])
+    out_other, out_own = line.add(out_other, got[1][0]), line.add(out_own, got[1][1])
+    got = yield [(in_high, 2, 0), (out_other, 0, 1)]
+    own = jnp.concatenate([line.add(in_low, got[0]), line.add(out_own, got[1])], 1)
+    mine, sends = far_blocks(line, own)
+    got = yield sends
+    found.append(plain_sum(mine, *got))
+
+
+def pack_sum_steps(line, pack, at_once, found):
+    count = lax.axis_size("dp")
+    here = lax.axis_index("dp")
+    pack = pack.reshape(count // 4, 2, 2, -1, pack.shape[1])
+    near = lambda value, bit, k, axis: lax.dynamic_index_in_dim(value, dp_bit(bit) ^ k, axis, False)
+    (got,) = yield [(line.gate(near(pack, 0, 1, 2)), 1, 0)]
+    pack = line.add(near(pack, 0, 0, 2), got)
+    mine, away = near(pack, 1, 0, 1), near(pack, 1, 1, 1)
+    if at_once:
+        got = yield [(mine, 0, 1), (away, 2, 0), (away, 2, 1)]
+        mine = line.add(mine, *got)
+    else:
+        (got,) = yield [(away, 2, 0)]
+        mine = line.add(mine, got)
+        (got,) = yield [(mine, 0, 1)]
+        mine = line.add(mine, got)
+    far = lambda k: lax.dynamic_index_in_dim(mine, (here >> 2) ^ k, 0, False)
+    mine, sends = far_blocks(line, [far(k) for k in range(count // 4)])
+    got = yield sends
+    found.append(line.add(mine, *got))
+
+
+def pack_all_steps(line, pack, sums, found):
+    mine = []
+    yield from pack_sum_steps(line, pack, True, mine)
+    mine = jnp.stack(mine + [s[0] for s in sums])
+    got = yield [(mine, k << 2, 0) for k in range(1, lax.axis_size("dp") // 4)]
+    parts = line.gate(jnp.stack([mine, *got]))
+    (got,) = yield [(parts, 2, 0)]
+    parts = line.gate(jnp.stack([parts, got], 1))
+    (got,) = yield [(parts, 1, 0)]
+    parts = jnp.stack([parts, got], 2)
+    parts = parts.reshape((-1,) + parts.shape[3:])
+    here = lax.axis_index("dp")
+    whole = [lax.dynamic_index_in_dim(parts, here ^ k, 0) for k in range(parts.shape[0])]
+    found.append(jnp.concatenate(whole))
+
+
+def block_place(index, bits):
+    low = index >> 1
+    return (low & 1) << (bits - 2) | low >> 1
+
+
+def image_body(
+    image_small,
+    image_large,
+    image_counts,
+    norm_gain,
+    norm_shift,
+    mix_in_small,
+    mix_bias_small,
+    mix_out_small,
+    mix_obias_small,
+    mix_in_large,
+    mix_bias_large,
+    mix_out_large,
+    mix_obias_large,
+    chan_in,
+    chan_bias,
+    chan_out,
+    chan_obias,
+    cot_small,
+    cot_large,
+):
+    layers = norm_gain.shape[0]
+    own_width = norm_gain.shape[2]
+    width = 2 * own_width
+    units = chan_bias.shape[1]
+    side = lax.axis_index("mp")
+    counts = (image_small.shape[0] // 2, image_large.shape[0] // 2)
+    patches = (image_small.shape[1], image_large.shape[1])
+    padded = tuple(-(-p // 16) * 16 for p in patches)
+    offsets = (0, counts[0] * padded[0])
+
+    def pad_patches(field, k, axis):
+        widths = [(0, 0)] * field.ndim
+        widths[axis] = (0, padded[k] - patches[k])
+        return jnp.pad(field, widths)
+
+    def pick(fields, flag):
+        parts = []
+        for k in range(2):
+            part = lax.dynamic_slice_in_dim(fields[k], flag * counts[k], counts[k], 0)
+            parts.append(pad_patches(part, k, 1).reshape(-1, own_width))
+        return jnp.concatenate(parts, 0)
+
+    def to_features(own, got):
+        outs = []
+        for k in range(2):
+            pair = []
+            for v in (own, got):
+                v = v[offsets[k] : offsets[k] + counts[k] * padded[k]]
+                pair.append(v.reshape(counts[k], padded[k], own_width)[:, : patches[k]])
+            outs.append(join(pair[0], pair[1], side, 0))
+        return outs
+
+    def features(rows, flag):
+        return lax.dynamic_slice_in_dim(rows, flag * own_width, own_width, 1)
+
+    count = lax.axis_size("dp")
+    bits = count.bit_length() - 1
+    place = block_place(lax.axis_index("dp"), bits)
+    info = jnp.stack([side, dp_bit(0), dp_bit(0) * 2 + dp_bit(1), place]).astype(jnp.int32)
+    places = [(block_place(i, bits),) * 2 for i in range(count)]
+
+    line = Transfers()
+    vectors = jnp.concatenate(
+        [norm_gain.reshape(layers, -1), norm_shift.reshape(layers, -1), chan_obias, chan_bias], 1
+    )
+    live = []
+    for k in range(2):
+        slot = side * counts[k] + jnp.arange(counts[k], dtype=jnp.int32)
+        alive = (slot < image_counts[0, k]).astype(F32)
+        live.append(jnp.repeat(alive, padded[k]))
+    live = jnp.broadcast_to(jnp.concatenate(live)[:, None], (sum(c * p for c, p in zip(counts, padded)), LANES))
+    own = (chan_in, chan_out)
+    images = (image_small, image_large)
+    cots = (cot_small, cot_large)
+    vectors_found, images_found, cot_found, out_found = [], [], [], []
+    found = [[] for _ in range(layers)]
+    fetches = {0: line.start(fetch_steps(line, own, 0, found[0]))}
+    line.tick()
+    line.arrived()
+    images_flow = line.start(one_step(line, pick(images, 1 - side), images_found))
+    vectors_flow = line.start(one_step(line, vectors, vectors_found))
+    line.tick()
+    line.finish(images_flow)
+    line.finish(vectors_flow)
+    other_vectors = vectors_found[0]
+    line.mark = mark_after(images_found[0])
+    if layers > 1:
+        fetches[1] = line.start(fetch_steps(line, own, 1, found[1]))
+    ties = line.tick()
+    stream, line.mark = join_features(
+        info, pick(images, side), images_found[0], jnp.ones_like(live)
+    )
+
+    mine, theirs = (v[:, : 5 * own_width].reshape(layers, 5, own_width) for v in (vectors, other_vectors))
+    whole = join(mine, theirs, side, 2)
+    norms, obias_all = whole[:, :4], whole[:, 4:]
+    bias_all = jnp.concatenate([chan_bias, other_vectors[:, 5 * own_width :]], 1)[:, None]
+    line_of = lambda b: b[:, None, :]
+    token_params = (
+        (
+            norms,
+            mix_in_small,
+            line_of(mix_bias_small),
+            jnp.swapaxes(mix_out_small, 1, 2),
+            line_of(mix_obias_small),
+        ),
+        (
+            norms,
+            mix_in_large,
+            line_of(mix_bias_large),
+            jnp.swapaxes(mix_out_large, 1, 2),
+            line_of(mix_obias_large),
+        ),
+    )
+
+    kept = []
+    for pos in range(layers):
+        if pos > 0:
+            if pos == layers - 1:
+                line.start(one_step(line, pick(cots, 1 - side), cot_found))
+            ties = line.tick()
+        parts, base = [], ()
+        for k in range(2):
+            mixed, rows, *rest, line.mark = token_forward(
+                stream, pos, token_params[k], counts[k], padded[k], offsets[k], base, ties
+            )
+            ties = ()
+            base = (mixed, rows)
+            parts.append(rest)
+        line.finish(fetches[pos])
+        if pos + 2 < layers:
+            fetches[pos + 2] = line.start(fetch_steps(line, own, pos + 2, found[pos + 2]))
+            ties = line.tick()
+        quant, slope, stream, *other, line.mark = chan_forward(
+            info, rows, mixed, own, found[pos], (pos, 0), bias_all, obias_all, 352, 256, ties
+        )
+        ties = ()
+        kept.append((parts, rows, quant, slope, other))
+    if not cot_found:
+        if layers == 1:
+            line.start(one_step(line, pick(cots, 1 - side), cot_found))
+            line.tick()
+        line.tick()
+    out = (stream * live[:, 0:1]).astype(B16)
+    grad, line.mark = join_features(info, pick(cots, side), cot_found[0], live)
+
+    block = units // count
+    grads_found = [[] for _ in range(layers)]
+    pack_found = [[] for _ in range(layers)]
+    gathered = [None] * layers
+    chan_grads = ()
+
+    def gather_ready():
+        for pos in reversed(range(layers)):
+            if gathered[pos] is None and grads_found[pos]:
+                payload = grads_found[pos][0]
+                if pos + 1 < layers:
+                    payload = payload + mark_after(gathered[pos + 1])[0, 0].astype(B16)
+                gathered[pos] = lax.all_gather(payload, "dp")
+
+    for pos in reversed(range(layers)):
+        parts, rows, quant, slope, other = kept[pos]
+        back, small, keep = None, 0.0, []
+        for half in range(2):
+            ties = line.tick()
+            gather_ready()
+            value, part_small, back, line.mark = chan_backward(
+                info, grad, rows, quant, slope, own, other, pos, back, count // 2, ties
+            )
+            small = small + part_small
+            if half == 0:
+                steps = upper_grad_steps if pos > 0 else lowest_grad_steps
+                line.start(steps(line, value, keep, grads_found[pos]))
+            else:
+                keep.append(value)
+        ties = line.tick()
+        gather_ready()
+        base, token_grads, smalls = (), [], []
+        for k in range(2):
+            following, token_grad, token_small, line.mark = token_backward(
+                grad,
+                back,
+                parts[k],
+                pos,
+                token_params[k],
+                counts[k],
+                padded[k],
+                offsets[k],
+                base,
+                ties,
+            )
+            ties = ()
+            base = (following,)
+            token_grads.append(token_grad)
+            smalls.append(token_small)
+        grad = following
+        pieces = token_grads + smalls + [small]
+        size = sum(p.shape[0] for p in pieces)
+        fill = jnp.zeros((-size % (8 * count), width), F32)
+        pack = jnp.concatenate(pieces + [fill], 0).astype(B16)
+        if pos > 0:
+            line.start(pack_sum_steps(line, pack, False, pack_found[pos]), first=True)
+        else:
+            line.start(pack_all_steps(line, pack, pack_found[1:], pack_found[0]))
+
+    grad_found = []
+    line.start(one_step(line, features(grad, 1 - side).astype(B16), grad_found, 2))
+    line.start(one_step(line, features(out, 1 - side), out_found, 3))
+    done = layers
+    while line.flows:
+        line.tick()
+        gather_ready()
+        if done > 1 and (done == layers or gathered[done - 2] is not None):
+            done -= 1
+            *chan_grads, line.mark = assemble(
+                gathered[done], places, done, layers, block, tuple(chan_grads)
+            )
+        if any(flow["got"] for flow in line.flows):
+            line.arrived()
+    outs = to_features(features(out, side), out_found[0])
+    grads = to_features(features(grad, side), grad_found[0].astype(F32))
+    while done:
+        done -= 1
+        *chan_grads, _ = assemble(gathered[done], places, done, layers, block, tuple(chan_grads))
+    pack_rows = pack.shape[0]
+    pack = jnp.swapaxes(pack_found[0][0], 0, 1).reshape(layers, pack_rows, width)
+    hidden_tok = mix_bias_small.shape[1]
+    token_parts = []
+    at = 0
+    for k in range(2):
+        block = pack[:, at : at + patches[k]].astype(F32)
+        token_parts.append((block[:, :, :hidden_tok], jnp.swapaxes(block[:, :, hidden_tok:], 1, 2)))
+        at += padded[k]
+    small = pack[:, at : at + 24].astype(F32)
+    mine = lax.dynamic_slice_in_dim(small, side * own_width, own_width, 2)
+    norm_g = mine[:, 0:4] + mine[:, 8:12]
+    cbias = lax.dynamic_slice_in_dim(small[:, 17:21].reshape(layers, -1), side * units, units, 1)
+    return (
+        outs[0],
+        outs[1],
+        grads[0],
+        grads[1],
+        norm_g[:, 0:2],
+        norm_g[:, 2:4],
+        token_parts[0][0],
+        small[:, 4, :hidden_tok],
+        token_parts[0][1],
+        small[:, 5, : patches[0]],
+        token_parts[1][0],
+        small[:, 12, :hidden_tok],
+        token_parts[1][1],
+        small[:, 13, : patches[1]],
+        chan_grads[0],
+        cbias,
+        chan_grads[1],
+        mine[:, 16],
+    )
+
+
 def solution(mesh):
     in_specs = (
         P("dp", None, "mp"),
@@ -360,4 +1304,5 @@
         P(None, "mp", None),
         P(None, "mp"),
     )
+    body = image_body if image_split(mesh) else split_body
     return jax.shard_map(body, mesh=mesh, in_specs=in_specs, out_specs=out_specs, check_vma=False)

time: 1640 us -> 820 us (0.50)
  matrix products: 428 us -> 0 us
  Pallas kernels: 0 us -> 376 us
  waiting for transfers between devices: 457 us -> 123 us
  local copies, waits for them, and re-layouts: 280 us -> 60.1 us
  blocking collectives: 177 us -> 0 us
  other arithmetic: 269 us -> 142 us
  starting transfers between devices: 2.49 us -> 85.1 us
    dot_general x72 -> x0, matrix products: 428 us -> none  [the longest x6 73.6 us: body(): jnp.einsum('nsc,fc->nsf', gathered_grad[k], chan_out[layer_pos], preferre...]
    pallas_call x0 -> x35, Pallas kernels: none -> 376 us  [the longest x6 160 us: chan_backward(): kernel_call(functools.partial(chan_backward_kernel, blocks, first), (2,),...]
    unnamed x496 -> x228, local copies, waits for them, and re-layouts: 260 us -> 18 us
    psum x2 -> x0, waiting for transfers between devices: 239 us -> none  [the longest x1 165 us: body(): lax.psum((token_terms[0], token_terms[1], token_terms[2], token_terms[3],...]
    psum x14 -> x0, blocking collectives: 177 us -> none  [the longest x1 57.2 us: body(): lax.psum(chan_local[4].astype(jnp.bfloat16), 'dp').astype(jnp.float32)]
    all_gather x12 -> x3, waiting for transfers between devices: 137 us -> 0.01 us  [gather_ready(): gathered[pos] = lax.all_gather(payload, 'dp')]
    ppermute x0 -> x69, waiting for transfers between devices: none -> 123 us  [the longest x48 88.6 us: exchange(): return lax.ppermute(value, 'dp', [(i, i ^ mask) for i in range(count)])]
    ppermute x0 -> x69, starting transfers between devices: none -> 85 us  [the longest x48 68.5 us: exchange(): return lax.ppermute(value, 'dp', [(i, i ^ mask) for i in range(count)])]
  transfers between devices with their start and end apart: 26 -> 72, of which waited for: 14 -> 11; matrix products, arithmetic and copies ran while one was open for 46% -> 22% of each run, Pallas kernels for 0% -> 39%
where the time goes in v1:
time: 820 us; the launch traced here: 812 us
  Pallas kernels  376 us (46%)
  other arithmetic  142 us (17%)
  waiting for transfers between devices  123 us (15%)
  starting transfers between devices  85.1 us (10%)
  local copies, waits for them, and re-layouts  60.1 us (7%)
  between operations  26 us (3%)
    pallas_call x6, Pallas kernels, chan_backward(): kernel_call(functools.partial(chan_backward_kernel, blocks, first), (2,),...  160 us
    ppermute x48, waiting for transfers between devices, exchange(): return lax.ppermute(value, 'dp', [(i, i ^ mask) for i in range(count)])  88.6 us
    pallas_call x3, Pallas kernels, chan_forward(): kernel_call(functools.partial(chan_forward_kernel, part), (count // tile,...  74.7 us
    ppermute x48, starting transfers between devices, exchange(): return lax.ppermute(value, 'dp', [(i, i ^ mask) for i in range(count)])  68.5 us
    pallas_call x6, Pallas kernels, token_backward(): kernel_call(token_backward_kernel, (images,), [placed, placed, block(patc...  62.3 us
    convert_element_type x18, other arithmetic, add(): return (total + self.zero()).astype(B16)  58.4 us
    pallas_call x6, Pallas kernels, token_forward(): kernel_call(token_forward_kernel, (images,), [placed] + [layer_spec(a, po...  44.4 us
    add x28, other arithmetic, gate(): value + self.zero().astype(value.dtype)  41.4 us
  transfers between devices with their start and end apart: 72, of which 11 were waited for; matrix products, arithmetic and copies ran while one was open for 22% of the time, Pallas kernels for 39%

profile of v1, /device:TPU:1, one launch (start us, length us, event | category | flops | bytes accessed | tf_op | source)
XLA Modules:
  0.0 812.4 jit_solution(9711353573274975586)
XLA Ops:
  13.1 4.5 constant_dynamic-slice_fusion.8
  32.2 4.9 collective-permute-done.1.refs_1_
  45.8 20.1 %collective-permute-done.3 = f32[3,3456]{1,0:T(4,128)S(1)} collective-permute-done((f32[3,3456]{1,0:T(4,128)S(1)}, f32[3,3456]{1,0:T(4,128)S(1)}, u32[]{:S(2)}, u32[]{:S(2)}) %collective-permute-start.3) | collective-permute-done | bytes 41504 | tf_op jit(solution)/shard_map/ppermute | solution.py:825
  82.9 5.3 shard_map.323
  88.2 8.6 %shard_map.325 = (f32[1408,768]{1,0:T(8,128)}, bf16[1408,768]{1,0:T(8,128)(2,1)}, bf16[832,768]{1,0:T(8,128)(2,1)}, bf16[1536,768]{1,0:T(8,128)(2,1)}, bf16[1536...) custom-call(f32[1408,768]{1,0:T(8,128)} %get-tuple-element.136.x_ref, ...), custom_call_target="tpu_custom_call" | custom-call | flops 196293427200 | bytes 3833856000 | tf_op jit(solution)/shard_map/pallas_call | solution.py:459
  96.9 6.0 shard_map.326
  114.4 24.5 %shard_map.327 = (bf16[1408,3072]{1,0:T(8,128)(2,1)}, bf16[1408,3072]{1,0:T(8,128)(2,1)}, f32[1408,768]{1,0:T(8,128)}, bf16[768,1536]{1,0:T(8,128)(2,1)}, bf16[1536,768]{1,0:T(8,128)(2,1)}, /*index=5*/f32[1,1]{1,0:T(1,128)}) custom-call(s32[4]{0:T(128)} %pad_add_fusion.info_ref, bf16[1408,768]{1,0:T(8,128)(2,1)} %get-tuple-element.139.rows_ref, ...), custom_call_target="tpu_custom_call" | custom-call | flops 2657511014400 | bytes 5622988800 | tf_op jit(solution)/shard_map/pallas_call | solution.py:570
  139.5 2.4 maximum_add_fusion.4.rest_0_.in_near_ref
  144.0 2.4 maximum_add_fusion.5.rest_1_.out_near_ref
  151.7 9.1 %shard_map.328 = (f32[1408,768]{1,0:T(8,128)}, bf16[1408,768]{1,0:T(8,128)(2,1)}, bf16[832,768]{1,0:T(8,128)(2,1)}, bf16[1536,768]{1,0:T(8,128)(2,1)}, bf16[1536...) custom-call(f32[1408,768]{1,0:T(8,128)} %get-tuple-element.142.x_ref, ...), custom_call_target="tpu_custom_call" | custom-call | flops 196293427200 | bytes 3833856000 | tf_op jit(solution)/shard_map/pallas_call | solution.py:459
  160.9 6.0 shard_map.329
  166.9 25.1 %shard_map.330 = (bf16[1408,3072]{1,0:T(8,128)(2,1)}, bf16[1408,3072]{1,0:T(8,128)(2,1)}, f32[1408,768]{1,0:T(8,128)}, bf16[768,1536]{1,0:T(8,128)(2,1)}, bf16[1536,768]{1,0:T(8,128)(2,1)}, /*index=5*/f32[1,1]{1,0:T(1,128)}) custom-call(s32[4]{0:T(128)} %pad_add_fusion.info_ref, bf16[1408,768]{1,0:T(8,128)(2,1)} %get-tuple-element.146.rows_ref, ...), custom_call_target="tpu_custom_call" | custom-call | flops 2657511014400 | bytes 5622988800 | tf_op jit(solution)/shard_map/pallas_call | solution.py:570
  192.7 2.4 maximum_add_fusion.6.rest_0_.in_near_ref
  196.1 2.4 maximum_add_fusion.7.rest_1_.out_near_ref
  201.0 8.7 %shard_map.331 = (f32[1408,768]{1,0:T(8,128)}, bf16[1408,768]{1,0:T(8,128)(2,1)}, bf16[832,768]{1,0:T(8,128)(2,1)}, bf16[1536,768]{1,0:T(8,128)(2,1)}, bf16[1536...) custom-call(f32[1408,768]{1,0:T(8,128)} %get-tuple-element.148.x_ref, ...), custom_call_target="tpu_custom_call" | custom-call | flops 196293427200 | bytes 3833856000 | tf_op jit(solution)/shard_map/pallas_call | solution.py:459
  209.7 6.0 shard_map.332
  215.7 9.5 %collective-permute-done.20.got_ref = bf16[1408,384]{1,0:T(8,128)(2,1)} collective-permute-done((bf16[1408,384]{1,0:T(8,128)(2,1)}, bf16[1408,384]{1,0:T(8,128)(2,1)}, u32[]{:S(2)}, u32[]{:S(2)}) %collective-permute-start.20) | collective-permute-done | bytes 1081376 | tf_op jit(solution)/shard_map/ppermute | solution.py:825
  226.3 5.3 shard_map.334
  231.6 25.2 %shard_map.333 = (bf16[1408,3072]{1,0:T(8,128)(2,1)}, bf16[1408,3072]{1,0:T(8,128)(2,1)}, f32[1408,768]{1,0:T(8,128)}, bf16[768,1536]{1,0:T(8,128)(2,1)}, bf16[1536,768]{1,0:T(8,128)(2,1)}, /*index=5*/f32[1,1]{1,0:T(1,128)}) custom-call(s32[4]{0:T(128)} %pad_add_fusion.info_ref, bf16[1408,768]{1,0:T(8,128)(2,1)} %get-tuple-element.152.rows_ref, ...), custom_call_target="tpu_custom_call" | custom-call | flops 2657511014400 | bytes 5622988800 | tf_op jit(solution)/shard_map/pallas_call | solution.py:570
  256.8 26.2 %shard_map.335 = (bf16[2,2,8,96,768]{4,3,2,1,0:T(8,128)(2,1)}, f32[8,768]{1,0:T(8,128)}, f32[1408,768]{1,0:T(8,128)}, f32[1,1]{1,0:T(1,128)}) custom-call(s32[4]{0:T(128)} %pad_add_fusion.info_ref, f32[1408,768]{1,0:T(8,128)} %get-tuple-element.155.grad_ref, bf16[1408,768]{1,0:T(8,128)(2,1)} %get-tuple-element.152.rows_ref, ...), custom_call_target="tpu_custom_call" | custom-call | flops 2657511014400 | bytes 5190451200 | tf_op jit(solution)/shard_map/pallas_call | solution.py:654
  284.3 27.0 %shard_map.336 = (bf16[2,2,8,96,768]{4,3,2,1,0:T(8,128)(2,1)}, f32[8,768]{1,0:T(8,128)}, f32[1408,768]{1,0:T(8,128)}, f32[1,1]{1,0:T(1,128)}) custom-call(s32[4]{0:T(128)} %pad_add_fusion.info_ref, f32[1408,768]{1,0:T(8,128)} %get-tuple-element.155.grad_ref, bf16[1408,768]{1,0:T(8,128)(2,1)} %get-tuple-element.152.rows_ref, ...), custom_call_target="tpu_custom_call" | custom-call | flops 2657511014400 | bytes 5190451200 | tf_op jit(solution)/shard_map/pallas_call | solution.py:654
  311.4 5.1 fusion.17
  317.7 12.3 %shard_map.337 = (f32[1408,768]{1,0:T(8,128)}, f32[208,768]{1,0:T(8,128)}, f32[8,768]{1,0:T(8,128)}, f32[1,1]{1,0:T(1,128)}) custom-call(f32[1408,768]{1,0:T(8,128)} %get-tuple-element.155.grad_ref, f32[1408,768]{1,0:T(8,128)} %get-tuple-element.162.back_ref, bf16[832,768]{1,0:T(8,128)(2,1)} %get-tuple-element.169.vhat_two_ref, ...), custom_call_target="tpu_custom_call" | custom-call | flops 392586854400 | bytes 3833856000 | tf_op jit(solution)/shard_map/pallas_call | solution.py:802
  331.8 8.5 %shard_map.338 = (f32[1408,768]{1,0:T(8,128)}, f32[576,768]{1,0:T(8,128)}, f32[8,768]{1,0:T(8,128)}, f32[1,1]{1,0:T(1,128)}) custom-call(f32[1408,768]{1,0:T(8,128)} %get-tuple-element.155.grad_ref, f32[1408,768]{1,0:T(8,128)} %get-tuple-element.162.back_ref, bf16[576,768]{1,0:T(8,128)(2,1)} %get-tuple-element.163.vhat_two_ref, ...), custom_call_target="tpu_custom_call", output_to_operand_aliasing={{0}: (11, {})} | custom-call | flops 271790899200 | bytes 2654208000 | tf_op jit(solution)/shard_map/pallas_call | solution.py:802
  347.1 4.9 fusion.9.rest_2_
  353.1 25.9 %shard_map.339 = (bf16[2,2,8,96,768]{4,3,2,1,0:T(8,128)(2,1)}, f32[8,768]{1,0:T(8,128)}, f32[1408,768]{1,0:T(8,128)}, f32[1,1]{1,0:T(1,128)}) custom-call(s32[4]{0:T(128)} %pad_add_fusion.info_ref, f32[1408,768]{1,0:T(8,128)} %get-tuple-element.178.grad_ref, bf16[1408,768]{1,0:T(8,128)(2,1)} %get-tuple-element.146.rows_ref, ...), custom_call_target="tpu_custom_call" | custom-call | flops 2657511014400 | bytes 5190451200 | tf_op jit(solution)/shard_map/pallas_call | solution.py:654
  383.3 4.4 fusion.7
  389.5 3.3 collective-permute-start.68
  393.1 27.1 %shard_map.340 = (bf16[2,2,8,96,768]{4,3,2,1,0:T(8,128)(2,1)}, f32[8,768]{1,0:T(8,128)}, f32[1408,768]{1,0:T(8,128)}, f32[1,1]{1,0:T(1,128)}) custom-call(s32[4]{0:T(128)} %pad_add_fusion.info_ref, f32[1408,768]{1,0:T(8,128)} %get-tuple-element.178.grad_ref, bf16[1408,768]{1,0:T(8,128)(2,1)} %get-tuple-element.146.rows_ref, ...), custom_call_target="tpu_custom_call" | custom-call | flops 2657511014400 | bytes 5190451200 | tf_op jit(solution)/shard_map/pallas_call | solution.py:654
  420.2 2.5 fusion.41.rest_0_
  426.0 5.2 fusion.21
  431.4 12.3 %shard_map.341 = (f32[1408,768]{1,0:T(8,128)}, f32[208,768]{1,0:T(8,128)}, f32[8,768]{1,0:T(8,128)}, f32[1,1]{1,0:T(1,128)}) custom-call(f32[1408,768]{1,0:T(8,128)} %get-tuple-element.178.grad_ref, f32[1408,768]{1,0:T(8,128)} %get-tuple-element.193.back_ref, bf16[832,768]{1,0:T(8,128)(2,1)} %get-tuple-element.200.vhat_two_ref, ...), custom_call_target="tpu_custom_call" | custom-call | flops 392586854400 | bytes 3833856000 | tf_op jit(solution)/shard_map/pallas_call | solution.py:802
  445.5 8.5 %shard_map.342 = (f32[1408,768]{1,0:T(8,128)}, f32[576,768]{1,0:T(8,128)}, f32[8,768]{1,0:T(8,128)}, f32[1,1]{1,0:T(1,128)}) custom-call(f32[1408,768]{1,0:T(8,128)} %get-tuple-element.178.grad_ref, f32[1408,768]{1,0:T(8,128)} %get-tuple-element.193.back_ref, bf16[576,768]{1,0:T(8,128)(2,1)} %get-tuple-element.194.vhat_two_ref, ...), custom_call_target="tpu_custom_call", output_to_operand_aliasing={{0}: (11, {})} | custom-call | flops 271790899200 | bytes 2654208000 | tf_op jit(solution)/shard_map/pallas_call | solution.py:802
  466.2 4.9 fusion.4.rest_5_
  472.5 26.3 %shard_map.343 = (bf16[2,2,8,96,768]{4,3,2,1,0:T(8,128)(2,1)}, f32[8,768]{1,0:T(8,128)}, f32[1408,768]{1,0:T(8,128)}, f32[1,1]{1,0:T(1,128)}) custom-call(s32[4]{0:T(128)} %pad_add_fusion.info_ref, f32[1408,768]{1,0:T(8,128)} %get-tuple-element.209.grad_ref, bf16[1408,768]{1,0:T(8,128)(2,1)} %get-tuple-element.139.rows_ref, ...), custom_call_target="tpu_custom_call" | custom-call | flops 2657511014400 | bytes 5190451200 | tf_op jit(solution)/shard_map/pallas_call | solution.py:654
  502.6 4.4 fusion.2
  508.8 3.3 collective-permute-start.65
  512.5 27.0 %shard_map.344 = (bf16[2,2,8,96,768]{4,3,2,1,0:T(8,128)(2,1)}, f32[8,768]{1,0:T(8,128)}, f32[1408,768]{1,0:T(8,128)}, f32[1,1]{1,0:T(1,128)}) custom-call(s32[4]{0:T(128)} %pad_add_fusion.info_ref, f32[1408,768]{1,0:T(8,128)} %get-tuple-element.209.grad_ref, bf16[1408,768]{1,0:T(8,128)(2,1)} %get-tuple-element.139.rows_ref, ...), custom_call_target="tpu_custom_call" | custom-call | flops 2657511014400 | bytes 5190451200 | tf_op jit(solution)/shard_map/pallas_call | solution.py:654
  539.5 2.5 fusion.39.rest_0_
  545.5 3.6 fusion.25.rest_2_
  550.4 3.6 fusion.24.rest_1_
  555.3 12.3 %shard_map.345 = (f32[1408,768]{1,0:T(8,128)}, f32[208,768]{1,0:T(8,128)}, f32[8,768]{1,0:T(8,128)}, f32[1,1]{1,0:T(1,128)}) custom-call(f32[1408,768]{1,0:T(8,128)} %get-tuple-element.209.grad_ref, f32[1408,768]{1,0:T(8,128)} %get-tuple-element.224.back_ref, bf16[832,768]{1,0:T(8,128)(2,1)} %get-tuple-element.225.vhat_two_ref, ...), custom_call_target="tpu_custom_call" | custom-call | flops 392586854400 | bytes 3833856000 | tf_op jit(solution)/shard_map/pallas_call | solution.py:802
  567.7 8.4 %shard_map.346 = (f32[1408,768]{1,0:T(8,128)}, f32[576,768]{1,0:T(8,128)}, f32[8,768]{1,0:T(8,128)}, f32[1,1]{1,0:T(1,128)}) custom-call(f32[1408,768]{1,0:T(8,128)} %get-tuple-element.209.grad_ref, f32[1408,768]{1,0:T(8,128)} %get-tuple-element.224.back_ref, bf16[576,768]{1,0:T(8,128)(2,1)} %get-tuple-element.234.vhat_two_ref, ...), custom_call_target="tpu_custom_call", output_to_operand_aliasing={{0}: (11, {})} | custom-call | flops 271790899200 | bytes 2654208000 | tf_op jit(solution)/shard_map/pallas_call | solution.py:802
  581.4 3.5 fusion.31
  588.9 2.4 collective-permute-start.38
  594.7 4.2 collective-permute-done.39.refs_2_
  598.9 6.0 collective-permute-done.41.refs_3_
  607.1 4.7 add_convert_fusion.10
  618.3 2.3 collective-permute-start.48
  621.9 17.0 %collective-permute-done.48.refs_1_ = bf16[192,768]{1,0:T(8,128)(2,1)S(1)} collective-permute-done((bf16[192,768]{1,0:T(8,128)(2,1)}, bf16[192,768]{1,0:T(8,128)(2,1)S(1)}, u32[]{:S(2)}, u32[]{:S(2)}) %collective-permute-start.48) | collective-permute-done | bytes 294944 | tf_op jit(solution)/shard_map/ppermute | solution.py:827
  644.7 2.5 multiply_convert_fusion
  647.2 5.1 collective-permute-start.57
  652.4 5.4 collective-permute-start.56
  662.2 3.2 collective-permute-start.52
  681.0 4.3 collective-permute-start.60
  685.3 5.6 collective-permute-start.59
  691.1 25.1 %collective-permute-done.59.refs_1_ = bf16[3,56,768]{2,1,0:T(8,128)(2,1)S(1)} collective-permute-done((bf16[3,56,768]{2,1,0:T(8,128)(2,1)S(1)}, bf16[3,56,768]{2,1,0:T(8,128)(2,1)S(1)}, u32[]{:S(2)}, u32[]{:S(2)}) %collective-permute-start.59) | collective-permute-done | bytes 258080 | tf_op jit(solution)/shard_map/ppermute | solution.py:827
  721.1 32.8 %collective-permute-done.61.refs_0_ = bf16[4,3,56,768]{3,2,1,0:T(8,128)(2,1)S(1)} collective-permute-done((bf16[4,3,56,768]{3,2,1,0:T(8,128)(2,1)S(1)}, bf16[4,3,56,768]{3,2,1,0:T(8,128)(2,1)S(1)}, u32[]{:S(2)}, u32[]{:S(2)}) %collective-permute-start.61) | collective-permute-done | bytes 1032224 | tf_op jit(solution)/shard_map/ppermute | solution.py:827
  756.0 2.7 maximum_add_fusion.1
  760.5 6.7 shard_map.354
  772.3 2.3 maximum_select_fusion
  789.9 2.7 slice_bitcast_fusion
  792.7 6.5 shard_map.355
  799.2 6.5 shard_map.356
  (499 shorter events, 187.2 us)
Async XLA Ops:
  7.2 535.0 %all-gather.7.cloned.1.call-start = ((), (), s32[]{:S(2)}) async-start(), calls=%async_computation | async-start | bytes 5013504 | tf_op jit(solution)/shard_map/all_gather | solution.py:1164
  9.2 23.1 %collective-permute-start = (bf16[1,192,1536]{2,1,0:T(8,128)(2,1)}, bf16[1,192,1536]{2,1,0:T(8,128)(2,1)S(1)}, u32[]{:S(2)}, u32[]{:S(2)}) collective-permute-start(bf16[1,192,1536]{2,1,0:T(8,128)(2,1)} %constant_dynamic-slice_fusion.11), channel_id=1, source_target_pairs={{0,1},{1,0},{2,3},{3,2},{4,5},{5,4},{6,7},{7,6},{8,9},{9,8},{10,11... | collective-permute-start | bytes 1769480 | tf_op jit(solution)/shard_map/ppermute | solution.py:825
  13.1 24.0 %collective-permute-start.1 = (bf16[1,384,768]{2,1,0:T(8,128)(2,1)}, bf16[1,384,768]{2,1,0:T(8,128)(2,1)S(1)}, u32[]{:S(2)}, u32[]{:S(2)}) collective-permute-start(bf16[1,384,768]{2,1,0:T(8,128)(2,1)} %constant_dynamic-slice_fusion.10), channel_id=1, source_target_pairs={{0,1},{1,0},{2,3},{3,2},{4,5},{5,4},{6,7},{7,6},{8,9},{9,8},{10,11... | collective-permute-start | bytes 1769480 | tf_op jit(solution)/shard_map/ppermute | solution.py:825
  40.4 29.6 %collective-permute-start.2 = (bf16[1408,384]{1,0:T(8,128)(2,1)}, bf16[1408,384]{1,0:T(8,128)(2,1)S(1)}, u32[]{:S(2)}, u32[]{:S(2)}) collective-permute-start(bf16[1408,384]{1,0:T(8,128)(2,1)} %maximum_add_fusion.8), channel_id=1, source_target_pairs={{0,1},{1,0},{2,3},{3,2},{4,5},{5,4},{6,7},{7,6},{8,9},{9,8},{10,11... | collective-permute-start | bytes 3244040 | tf_op jit(solution)/shard_map/ppermute | solution.py:825
  42.2 23.7 %collective-permute-start.3 = (f32[3,3456]{1,0:T(4,128)S(1)}, f32[3,3456]{1,0:T(4,128)S(1)}, u32[]{:S(2)}, u32[]{:S(2)}) collective-permute-start(f32[3,3456]{1,0:T(4,128)S(1)} %maximum_add_fusion.12), channel_id=1, source_target_pairs={{0,1},{1,0},{2,3},{3,2},{4,5},{5,4},{6,7},{7,6},{8,9},{9,8},{10,11... | collective-permute-start | bytes 124424 | tf_op jit(solution)/shard_map/ppermute | solution.py:825
  43.5 28.7 %collective-permute-start.4 = (bf16[1,192,1536]{2,1,0:T(8,128)(2,1)}, bf16[1,192,1536]{2,1,0:T(8,128)(2,1)S(1)}, u32[]{:S(2)}, u32[]{:S(2)}) collective-permute-start(bf16[1,192,1536]{2,1,0:T(8,128)(2,1)} %broadcast_add_fusion.5), channel_id=1, source_target_pairs={{0,4},{2,6},{4,0},{6,2},{8,12},{10,14},{12,8},{14,10},{16,20},{18,... | collective-permute-start | bytes 1769480 | tf_op jit(solution)/shard_map/ppermute | solution.py:827
  45.5 33.9 %collective-permute-start.5 = (bf16[1,384,768]{2,1,0:T(8,128)(2,1)}, bf16[1,384,768]{2,1,0:T(8,128)(2,1)S(1)}, u32[]{:S(2)}, u32[]{:S(2)}) collective-permute-start(bf16[1,384,768]{2,1,0:T(8,128)(2,1)} %broadcast_add_fusion.4), channel_id=1, source_target_pairs={{0,4},{2,6},{4,0},{6,2},{8,12},{10,14},{12,8},{14,10},{16,20},{18,... | collective-permute-start | bytes 1769480 | tf_op jit(solution)/shard_map/ppermute | solution.py:827
  73.3 40.8 %collective-permute-start.6 = (bf16[2,1,192,1536]{3,2,1,0:T(8,128)(2,1)}, bf16[2,1,192,1536]{3,2,1,0:T(8,128)(2,1)}, u32[]{:S(2)}, u32[]{:S(2)}) collective-permute-start(bf16[2,1,192,1536]{3,2,1,0:T(8,128)(2,1)} %maximum_add_fusion.2.rest_0_.in_near_ref), channel_id=1, source_target_pairs={{0,2},{2,0},{4,6},{6,4},{8,10},{10,8},{12,14},{14,12},{16,18},{18,... | collective-permute-start | bytes 3538952 | tf_op jit(solution)/shard_map/ppermute | solution.py:827
  80.5 33.9 %collective-permute-start.7 = (bf16[2,1,384,768]{3,2,1,0:T(8,128)(2,1)}, bf16[2,1,384,768]{3,2,1,0:T(8,128)(2,1)}, u32[]{:S(2)}, u32[]{:S(2)}) collective-permute-start(bf16[2,1,384,768]{3,2,1,0:T(8,128)(2,1)} %maximum_add_fusion.3.rest_1_.out_near_ref), channel_id=1, source_target_pairs={{0,2},{2,0},{4,6},{6,4},{8,10},{10,8},{12,14},{14,12},{16,18},{18,... | collective-permute-start | bytes 3538952 | tf_op jit(solution)/shard_map/ppermute | solution.py:827
  80.5 28.2 %collective-permute-start.8 = (bf16[1,192,1536]{2,1,0:T(8,128)(2,1)}, bf16[1,192,1536]{2,1,0:T(8,128)(2,1)}, u32[]{:S(2)}, u32[]{:S(2)}) collective-permute-start(bf16[1,192,1536]{2,1,0:T(8,128)(2,1)} %dynamic-slice_add_fusion.4.rest_2_), channel_id=1, source_target_pairs={{0,1},{1,0},{2,3},{3,2},{4,5},{5,4},{6,7},{7,6},{8,9},{9,8},{10,11... | collective-permute-start | bytes 1769480 | tf_op jit(solution)/shard_map/ppermute | solution.py:825
  81.6 29.3 %collective-permute-start.9 = (bf16[1,384,768]{2,1,0:T(8,128)(2,1)}, bf16[1,384,768]{2,1,0:T(8,128)(2,1)}, u32[]{:S(2)}, u32[]{:S(2)}) collective-permute-start(bf16[1,384,768]{2,1,0:T(8,128)(2,1)} %dynamic-slice_add_fusion.3.rest_3_), channel_id=1, source_target_pairs={{0,1},{1,0},{2,3},{3,2},{4,5},{5,4},{6,7},{7,6},{8,9},{9,8},{10,11... | collective-permute-start | bytes 1769480 | tf_op jit(solution)/shard_map/ppermute | solution.py:825
  105.5 40.9 %collective-permute-start.12 = (bf16[1,192,1536]{2,1,0:T(8,128)(2,1)}, bf16[1,192,1536]{2,1,0:T(8,128)(2,1)}, u32[]{:S(2)}, u32[]{:S(2)}) collective-permute-start(bf16[1,192,1536]{2,1,0:T(8,128)(2,1)} %dynamic-slice_add_fusion.2.rest_2_), channel_id=1, source_target_pairs={{0,1},{1,0},{2,3},{3,2},{4,5},{5,4},{6,7},{7,6},{8,9},{9,8},{10,11... | collective-permute-start | bytes 1769480 | tf_op jit(solution)/shard_map/ppermute | solution.py:825
  108.7 40.8 %collective-permute-start.13 = (bf16[1,384,768]{2,1,0:T(8,128)(2,1)}, bf16[1,384,768]{2,1,0:T(8,128)(2,1)}, u32[]{:S(2)}, u32[]{:S(2)}) collective-permute-start(bf16[1,384,768]{2,1,0:T(8,128)(2,1)} %dynamic-slice_add_fusion.1.rest_3_), channel_id=1, source_target_pairs={{0,1},{1,0},{2,3},{3,2},{4,5},{5,4},{6,7},{7,6},{8,9},{9,8},{10,11... | collective-permute-start | bytes 1769480 | tf_op jit(solution)/shard_map/ppermute | solution.py:825
  110.9 28.6 %collective-permute-start.10 = (bf16[1,192,1536]{2,1,0:T(8,128)(2,1)}, bf16[1,192,1536]{2,1,0:T(8,128)(2,1)}, u32[]{:S(2)}, u32[]{:S(2)}) collective-permute-start(bf16[1,192,1536]{2,1,0:T(8,128)(2,1)} %broadcast_add_fusion.3.rest_0_), channel_id=1, source_target_pairs={{0,4},{2,6},{4,0},{6,2},{8,12},{10,14},{12,8},{14,10},{16,20},{18,... | collective-permute-start | bytes 1769480 | tf_op jit(solution)/shard_map/ppermute | solution.py:827
  114.1 30.0 %collective-permute-start.11 = (bf16[1,384,768]{2,1,0:T(8,128)(2,1)}, bf16[1,384,768]{2,1,0:T(8,128)(2,1)}, u32[]{:S(2)}, u32[]{:S(2)}) collective-permute-start(bf16[1,384,768]{2,1,0:T(8,128)(2,1)} %broadcast_add_fusion.2.rest_1_), channel_id=1, source_target_pairs={{0,4},{2,6},{4,0},{6,2},{8,12},{10,14},{12,8},{14,10},{16,20},{18,... | collective-permute-start | bytes 1769480 | tf_op jit(solution)/shard_map/ppermute | solution.py:827
  141.8 25.1 %collective-permute-start.14 = (bf16[2,1,192,1536]{3,2,1,0:T(8,128)(2,1)}, bf16[2,1,192,1536]{3,2,1,0:T(8,128)(2,1)}, u32[]{:S(2)}, u32[]{:S(2)}) collective-permute-start(bf16[2,1,192,1536]{3,2,1,0:T(8,128)(2,1)} %maximum_add_fusion.4.rest_0_.in_near_ref), channel_id=1, source_target_pairs={{0,2},{2,0},{4,6},{6,4},{8,10},{10,8},{12,14},{14,12},{16,18},{18,... | collective-permute-start | bytes 3538952 | tf_op jit(solution)/shard_map/ppermute | solution.py:827
  146.4 20.5 %collective-permute-start.15 = (bf16[2,1,384,768]{3,2,1,0:T(8,128)(2,1)}, bf16[2,1,384,768]{3,2,1,0:T(8,128)(2,1)}, u32[]{:S(2)}, u32[]{:S(2)}) collective-permute-start(bf16[2,1,384,768]{3,2,1,0:T(8,128)(2,1)} %maximum_add_fusion.5.rest_1_.out_near_ref), channel_id=1, source_target_pairs={{0,2},{2,0},{4,6},{6,4},{8,10},{10,8},{12,14},{14,12},{16,18},{18,... | collective-permute-start | bytes 3538952 | tf_op jit(solution)/shard_map/ppermute | solution.py:827
  148.3 44.4 %collective-permute-start.16 = (bf16[1,192,1536]{2,1,0:T(8,128)(2,1)}, bf16[1,192,1536]{2,1,0:T(8,128)(2,1)}, u32[]{:S(2)}, u32[]{:S(2)}) collective-permute-start(bf16[1,192,1536]{2,1,0:T(8,128)(2,1)} %broadcast_add_fusion.1.rest_2_), channel_id=1, source_target_pairs={{0,4},{2,6},{4,0},{6,2},{8,12},{10,14},{12,8},{14,10},{16,20},{18,... | collective-permute-start | bytes 1769480 | tf_op jit(solution)/shard_map/ppermute | solution.py:827
  151.5 44.7 %collective-permute-start.17 = (bf16[1,384,768]{2,1,0:T(8,128)(2,1)}, bf16[1,384,768]{2,1,0:T(8,128)(2,1)}, u32[]{:S(2)}, u32[]{:S(2)}) collective-permute-start(bf16[1,384,768]{2,1,0:T(8,128)(2,1)} %broadcast_add_fusion.rest_3_), channel_id=1, source_target_pairs={{0,4},{2,6},{4,0},{6,2},{8,12},{10,14},{12,8},{14,10},{16,20},{18,... | collective-permute-start | bytes 1769480 | tf_op jit(solution)/shard_map/ppermute | solution.py:827
  195.1 36.5 %collective-permute-start.18 = (bf16[2,1,192,1536]{3,2,1,0:T(8,128)(2,1)}, bf16[2,1,192,1536]{3,2,1,0:T(8,128)(2,1)}, u32[]{:S(2)}, u32[]{:S(2)}) collective-permute-start(bf16[2,1,192,1536]{3,2,1,0:T(8,128)(2,1)} %maximum_add_fusion.6.rest_0_.in_near_ref), channel_id=1, source_target_pairs={{0,2},{2,0},{4,6},{6,4},{8,10},{10,8},{12,14},{14,12},{16,18},{18,... | collective-permute-start | bytes 3538952 | tf_op jit(solution)/shard_map/ppermute | solution.py:827
  198.5 33.1 %collective-permute-start.19 = (bf16[2,1,384,768]{3,2,1,0:T(8,128)(2,1)}, bf16[2,1,384,768]{3,2,1,0:T(8,128)(2,1)}, u32[]{:S(2)}, u32[]{:S(2)}) collective-permute-start(bf16[2,1,384,768]{3,2,1,0:T(8,128)(2,1)} %maximum_add_fusion.7.rest_1_.out_near_ref), channel_id=1, source_target_pairs={{0,2},{2,0},{4,6},{6,4},{8,10},{10,8},{12,14},{14,12},{16,18},{18,... | collective-permute-start | bytes 3538952 | tf_op jit(solution)/shard_map/ppermute | solution.py:827
  199.9 25.3 %collective-permute-start.20 = (bf16[1408,384]{1,0:T(8,128)(2,1)}, bf16[1408,384]{1,0:T(8,128)(2,1)}, u32[]{:S(2)}, u32[]{:S(2)}) collective-permute-start(bf16[1408,384]{1,0:T(8,128)(2,1)} %maximum_add_fusion.9.rest_2_), channel_id=1, source_target_pairs={{0,1},{1,0},{2,3},{3,2},{4,5},{5,4},{6,7},{7,6},{8,9},{9,8},{10,11... | collective-permute-start | bytes 3244040 | tf_op jit(solution)/shard_map/ppermute | solution.py:825
  283.0 28.4 %collective-permute-start.21 = (bf16[2,2,8,96,768]{4,3,2,1,0:T(8,128)(2,1)}, bf16[2,2,8,96,768]{4,3,2,1,0:T(8,128)(2,1)}, u32[]{:S(2)}, u32[]{:S(2)}) collective-permute-start(bf16[2,2,8,96,768]{4,3,2,1,0:T(8,128)(2,1)} %get-tuple-element.161.rest_1_), channel_id=1, source_target_pairs={{0,2},{2,0},{4,6},{6,4},{8,10},{10,8},{12,14},{14,12},{16,18},{18,... | collective-permute-start | bytes 14155784 | tf_op jit(solution)/shard_map/ppermute | solution.py:827
  316.5 30.6 %collective-permute-start.22 = (bf16[2,4,96,768]{3,2,1,0:T(8,128)(2,1)}, bf16[2,4,96,768]{3,2,1,0:T(8,128)(2,1)}, u32[]{:S(2)}, u32[]{:S(2)}) collective-permute-start(bf16[2,4,96,768]{3,2,1,0:T(8,128)(2,1)} %get-tuple-element.297.rest_0_), channel_id=1, source_target_pairs={{0,1},{1,0},{2,3},{3,2},{4,5},{5,4},{6,7},{7,6},{8,9},{9,8},{10,11... | collective-permute-start | bytes 3538952 | tf_op jit(solution)/shard_map/ppermute | solution.py:825
  346.6 32.5 %collective-permute-start.23 = (bf16[4,2,56,768]{3,2,0,1:T(8,128)(2,1)}, bf16[4,2,56,768]{3,2,0,1:T(8,128)(2,1)}, u32[]{:S(2)}, u32[]{:S(2)}) collective-permute-start(bf16[4,2,56,768]{3,2,0,1:T(8,128)(2,1)} %fusion.37), channel_id=1, source_target_pairs={{0,2},{2,0},{4,6},{6,4},{8,10},{10,8},{12,14},{14,12},{16,18},{18,... | collective-permute-start | bytes 2064392 | tf_op jit(solution)/shard_map/ppermute | solution.py:827
  346.8 36.5 %collective-permute-start.24 = (bf16[2,4,96,768]{3,2,1,0:T(8,128)(2,1)}, bf16[2,4,96,768]{3,2,1,0:T(8,128)(2,1)}, u32[]{:S(2)}, u32[]{:S(2)}) collective-permute-start(bf16[2,4,96,768]{3,2,1,0:T(8,128)(2,1)} %get-tuple-element.296.rest_1_), channel_id=1, source_target_pairs={{0,1},{1,0},{2,3},{3,2},{4,5},{5,4},{6,7},{7,6},{8,9},{9,8},{10,11... | collective-permute-start | bytes 3538952 | tf_op jit(solution)/shard_map/ppermute | solution.py:825
  352.0 31.3 %collective-permute-start.25 = (bf16[2,4,96,768]{3,2,1,0:T(8,128)(2,1)}, bf16[2,4,96,768]{3,2,1,0:T(8,128)(2,1)}, u32[]{:S(2)}, u32[]{:S(2)}) collective-permute-start(bf16[2,4,96,768]{3,2,1,0:T(8,128)(2,1)} %fusion.9.rest_2_), channel_id=1, source_target_pairs={{0,4},{2,6},{4,0},{6,2},{8,12},{10,14},{12,8},{14,10},{16,20},{18,... | collective-permute-start | bytes 3538952 | tf_op jit(solution)/shard_map/ppermute | solution.py:827
  381.9 38.3 %collective-permute-start.26 = (bf16[4,56,768]{2,1,0:T(8,128)(2,1)}, bf16[4,56,768]{2,1,0:T(8,128)(2,1)}, u32[]{:S(2)}, u32[]{:S(2)}) collective-permute-start(bf16[4,56,768]{2,1,0:T(8,128)(2,1)} %dynamic-slice_bitcast_fusion.9.rest_1_), channel_id=1, source_target_pairs={{0,4},{2,6},{4,0},{6,2},{8,12},{10,14},{12,8},{14,10},{16,20},{18,... | collective-permute-start | bytes 1032200 | tf_op jit(solution)/shard_map/ppermute | solution.py:827
  382.1 43.8 %collective-permute-start.27 = (bf16[2,2,8,96,768]{4,3,2,1,0:T(8,128)(2,1)}, bf16[2,2,8,96,768]{4,3,2,1,0:T(8,128)(2,1)}, u32[]{:S(2)}, u32[]{:S(2)}) collective-permute-start(bf16[2,2,8,96,768]{4,3,2,1,0:T(8,128)(2,1)} %get-tuple-element.192.rest_5_), channel_id=1, source_target_pairs={{0,2},{2,0},{4,6},{6,4},{8,10},{10,8},{12,14},{14,12},{16,18},{18,... | collective-permute-start | bytes 14155784 | tf_op jit(solution)/shard_map/ppermute | solution.py:827
  389.5 34.3 %collective-permute-start.68 = (bf16[192,768]{1,0:T(8,128)(2,1)}, bf16[192,768]{1,0:T(8,128)(2,1)}, u32[]{:S(2)}, u32[]{:S(2)}) collective-permute-start(bf16[192,768]{1,0:T(8,128)(2,1)} %get-tuple-element.318.rest_4_), channel_id=1, source_target_pairs={{0,24},{2,26},{4,28},{6,30},{8,16},{10,18},{12,20},{14,22},{16,8},... | collective-permute-start | bytes 884744 | tf_op jit(solution)/shard_map/ppermute | solution.py:827
  392.8 31.1 %collective-permute-start.67 = (bf16[192,768]{1,0:T(8,128)(2,1)}, bf16[192,768]{1,0:T(8,128)(2,1)}, u32[]{:S(2)}, u32[]{:S(2)}) collective-permute-start(bf16[192,768]{1,0:T(8,128)(2,1)} %get-tuple-element.320.rest_3_), channel_id=1, source_target_pairs={{0,16},{2,18},{4,20},{6,22},{8,24},{10,26},{12,28},{14,30},{16,0},... | collective-permute-start | bytes 884744 | tf_op jit(solution)/shard_map/ppermute | solution.py:827
  392.8 31.1 %collective-permute-start.66 = (bf16[192,768]{1,0:T(8,128)(2,1)}, bf16[192,768]{1,0:T(8,128)(2,1)}, u32[]{:S(2)}, u32[]{:S(2)}) collective-permute-start(bf16[192,768]{1,0:T(8,128)(2,1)} %get-tuple-element.319.rest_2_), channel_id=1, source_target_pairs={{0,8},{2,10},{4,12},{6,14},{8,0},{10,2},{12,4},{14,6},{16,24},{18,... | collective-permute-start | bytes 884744 | tf_op jit(solution)/shard_map/ppermute | solution.py:827
  422.6 40.3 %collective-permute-start.28 = (bf16[4,56,768]{2,1,0:T(8,128)(2,1)}, bf16[4,56,768]{2,1,0:T(8,128)(2,1)}, u32[]{:S(2)}, u32[]{:S(2)}) collective-permute-start(bf16[4,56,768]{2,1,0:T(8,128)(2,1)} %fusion.41.rest_0_), channel_id=1, source_target_pairs={{0,1},{1,0},{2,3},{3,2},{4,5},{5,4},{6,7},{7,6},{8,9},{9,8},{10,11... | collective-permute-start | bytes 1032200 | tf_op jit(solution)/shard_map/ppermute | solution.py:825
  425.9 247.6 %all-gather.9.cloned.1.call-start = ((), (), s32[]{:S(2)}) async-start(), calls=%async_computation.1 | async-start | bytes 5013504 | tf_op jit(solution)/shard_map/all_gather | solution.py:1164
  431.1 35.1 %collective-permute-start.29 = (bf16[2,4,96,768]{3,2,1,0:T(8,128)(2,1)}, bf16[2,4,96,768]{3,2,1,0:T(8,128)(2,1)}, u32[]{:S(2)}, u32[]{:S(2)}) collective-permute-start(bf16[2,4,96,768]{3,2,1,0:T(8,128)(2,1)} %get-tuple-element.295.rest_1_), channel_id=1, source_target_pairs={{0,1},{1,0},{2,3},{3,2},{4,5},{5,4},{6,7},{7,6},{8,9},{9,8},{10,11... | collective-permute-start | bytes 3538952 | tf_op jit(solution)/shard_map/ppermute | solution.py:825
  460.7 38.1 %collective-permute-start.30 = (bf16[4,2,56,768]{3,2,0,1:T(8,128)(2,1)}, bf16[4,2,56,768]{3,2,0,1:T(8,128)(2,1)}, u32[]{:S(2)}, u32[]{:S(2)}) collective-permute-start(bf16[4,2,56,768]{3,2,0,1:T(8,128)(2,1)} %fusion.36), channel_id=1, source_target_pairs={{0,2},{2,0},{4,6},{6,4},{8,10},{10,8},{12,14},{14,12},{16,18},{18,... | collective-permute-start | bytes 2064392 | tf_op jit(solution)/shard_map/ppermute | solution.py:827
  461.9 40.7 %collective-permute-start.31 = (bf16[2,4,96,768]{3,2,1,0:T(8,128)(2,1)}, bf16[2,4,96,768]{3,2,1,0:T(8,128)(2,1)}, u32[]{:S(2)}, u32[]{:S(2)}) collective-permute-start(bf16[2,4,96,768]{3,2,1,0:T(8,128)(2,1)} %get-tuple-element.294.rest_4_), channel_id=1, source_target_pairs={{0,1},{1,0},{2,3},{3,2},{4,5},{5,4},{6,7},{7,6},{8,9},{9,8},{10,11... | collective-permute-start | bytes 3538952 | tf_op jit(solution)/shard_map/ppermute | solution.py:825
  471.1 31.5 %collective-permute-start.32 = (bf16[2,4,96,768]{3,2,1,0:T(8,128)(2,1)}, bf16[2,4,96,768]{3,2,1,0:T(8,128)(2,1)}, u32[]{:S(2)}, u32[]{:S(2)}) collective-permute-start(bf16[2,4,96,768]{3,2,1,0:T(8,128)(2,1)} %fusion.4.rest_5_), channel_id=1, source_target_pairs={{0,4},{2,6},{4,0},{6,2},{8,12},{10,14},{12,8},{14,10},{16,20},{18,... | collective-permute-start | bytes 3538952 | tf_op jit(solution)/shard_map/ppermute | solution.py:827
  501.6 37.8 %collective-permute-start.33 = (bf16[4,56,768]{2,1,0:T(8,128)(2,1)}, bf16[4,56,768]{2,1,0:T(8,128)(2,1)}, u32[]{:S(2)}, u32[]{:S(2)}) collective-permute-start(bf16[4,56,768]{2,1,0:T(8,128)(2,1)} %dynamic-slice_bitcast_fusion.8.rest_1_), channel_id=1, source_target_pairs={{0,4},{2,6},{4,0},{6,2},{8,12},{10,14},{12,8},{14,10},{16,20},{18,... | collective-permute-start | bytes 1032200 | tf_op jit(solution)/shard_map/ppermute | solution.py:827
  501.7 43.8 %collective-permute-start.34 = (bf16[2,2,8,96,768]{4,3,2,1,0:T(8,128)(2,1)}, bf16[2,2,8,96,768]{4,3,2,1,0:T(8,128)(2,1)}, u32[]{:S(2)}, u32[]{:S(2)}) collective-permute-start(bf16[2,2,8,96,768]{4,3,2,1,0:T(8,128)(2,1)} %get-tuple-element.223.rest_5_), channel_id=1, source_target_pairs={{0,2},{2,0},{4,6},{6,4},{8,10},{10,8},{12,14},{14,12},{16,18},{18,... | collective-permute-start | bytes 14155784 | tf_op jit(solution)/shard_map/ppermute | solution.py:827
  508.8 34.6 %collective-permute-start.65 = (bf16[192,768]{1,0:T(8,128)(2,1)}, bf16[192,768]{1,0:T(8,128)(2,1)}, u32[]{:S(2)}, u32[]{:S(2)}) collective-permute-start(bf16[192,768]{1,0:T(8,128)(2,1)} %get-tuple-element.313.rest_4_), channel_id=1, source_target_pairs={{0,24},{2,26},{4,28},{6,30},{8,16},{10,18},{12,20},{14,22},{16,8},... | collective-permute-start | bytes 884744 | tf_op jit(solution)/shard_map/ppermute | solution.py:827
  512.2 31.2 %collective-permute-start.64 = (bf16[192,768]{1,0:T(8,128)(2,1)}, bf16[192,768]{1,0:T(8,128)(2,1)}, u32[]{:S(2)}, u32[]{:S(2)}) collective-permute-start(bf16[192,768]{1,0:T(8,128)(2,1)} %get-tuple-element.315.rest_3_), channel_id=1, source_target_pairs={{0,16},{2,18},{4,20},{6,22},{8,24},{10,26},{12,28},{14,30},{16,0},... | collective-permute-start | bytes 884744 | tf_op jit(solution)/shard_map/ppermute | solution.py:827
  512.2 31.2 %collective-permute-start.63 = (bf16[192,768]{1,0:T(8,128)(2,1)}, bf16[192,768]{1,0:T(8,128)(2,1)}, u32[]{:S(2)}, u32[]{:S(2)}) collective-permute-start(bf16[192,768]{1,0:T(8,128)(2,1)} %get-tuple-element.314.rest_2_), channel_id=1, source_target_pairs={{0,8},{2,10},{4,12},{6,14},{8,0},{10,2},{12,4},{14,6},{16,24},{18,... | collective-permute-start | bytes 884744 | tf_op jit(solution)/shard_map/ppermute | solution.py:827
  541.9 43.8 %collective-permute-start.36 = (bf16[4,56,768]{2,1,0:T(8,128)(2,1)}, bf16[4,56,768]{2,1,0:T(8,128)(2,1)}, u32[]{:S(2)}, u32[]{:S(2)}) collective-permute-start(bf16[4,56,768]{2,1,0:T(8,128)(2,1)} %fusion.39.rest_0_), channel_id=1, source_target_pairs={{0,1},{1,0},{2,3},{3,2},{4,5},{5,4},{6,7},{7,6},{8,9},{9,8},{10,11... | collective-permute-start | bytes 1032200 | tf_op jit(solution)/shard_map/ppermute | solution.py:825
  545.5 253.7 %all-gather.11.cloned.1.call-start = ((), (), s32[]{:S(2)}) async-start(), calls=%async_computation.2 | async-start | bytes 5013504 | tf_op jit(solution)/shard_map/all_gather | solution.py:1164
  549.2 32.2 %collective-permute-start.42 = (bf16[2,4,96,768]{3,2,1,0:T(8,128)(2,1)}, bf16[2,4,96,768]{3,2,1,0:T(8,128)(2,1)}, u32[]{:S(2)}, u32[]{:S(2)}) collective-permute-start(bf16[2,4,96,768]{3,2,1,0:T(8,128)(2,1)} %fusion.25.rest_2_), channel_id=1, source_target_pairs={{0,4},{2,6},{4,0},{6,2},{8,12},{10,14},{12,8},{14,10},{16,20},{18,... | collective-permute-start | bytes 3538952 | tf_op jit(solution)/shard_map/ppermute | solution.py:827
  554.1 27.3 %collective-permute-start.40 = (bf16[8,96,768]{2,1,0:T(8,128)(2,1)}, bf16[8,96,768]{2,1,0:T(8,128)(2,1)}, u32[]{:S(2)}, u32[]{:S(2)}) collective-permute-start(bf16[8,96,768]{2,1,0:T(8,128)(2,1)} %fusion.24.rest_1_), channel_id=1, source_target_pairs={{0,1},{1,0},{2,3},{3,2},{4,5},{5,4},{6,7},{7,6},{8,9},{9,8},{10,11... | collective-permute-start | bytes 3538952 | tf_op jit(solution)/shard_map/ppermute | solution.py:825
  580.3 18.6 %collective-permute-start.35 = (bf16[4,2,56,768]{3,2,1,0:T(8,128)(2,1)S(1)}, bf16[4,2,56,768]{3,2,1,0:T(8,128)(2,1)S(1)}, u32[]{:S(2)}, u32[]{:S(2)}) collective-permute-start(bf16[4,2,56,768]{3,2,1,0:T(8,128)(2,1)S(1)} %fusion.35), channel_id=1, source_target_pairs={{0,2},{2,0},{4,6},{6,4},{8,10},{10,8},{12,14},{14,12},{16,18},{18,... | collective-permute-start | bytes 2064392 | tf_op jit(solution)/shard_map/ppermute | solution.py:827
  584.9 20.1 %collective-permute-start.41 = (bf16[4,96,768]{2,1,0:T(8,128)(2,1)S(1)}, bf16[4,96,768]{2,1,0:T(8,128)(2,1)S(1)}, u32[]{:S(2)}, u32[]{:S(2)}) collective-permute-start(bf16[4,96,768]{2,1,0:T(8,128)(2,1)S(1)} %get-tuple-element.293), channel_id=1, source_target_pairs={{0,4},{2,6},{4,0},{6,2},{8,12},{10,14},{12,8},{14,10},{16,20},{18,... | collective-permute-start | bytes 1769480 | tf_op jit(solution)/shard_map/ppermute | solution.py:827
  585.8 19.2 %collective-permute-start.43 = (bf16[4,96,768]{2,1,0:T(8,128)(2,1)S(1)}, bf16[4,96,768]{2,1,0:T(8,128)(2,1)S(1)}, u32[]{:S(2)}, u32[]{:S(2)}) collective-permute-start(bf16[4,96,768]{2,1,0:T(8,128)(2,1)S(1)} %get-tuple-element.292), channel_id=1, source_target_pairs={{0,1},{1,0},{2,3},{3,2},{4,5},{5,4},{6,7},{7,6},{8,9},{9,8},{10,11... | collective-permute-start | bytes 1769480 | tf_op jit(solution)/shard_map/ppermute | solution.py:825
  615.6 23.3 %collective-permute-start.46 = (bf16[4,56,768]{2,1,0:T(8,128)(2,1)}, bf16[4,56,768]{2,1,0:T(8,128)(2,1)S(1)}, u32[]{:S(2)}, u32[]{:S(2)}) collective-permute-start(bf16[4,56,768]{2,1,0:T(8,128)(2,1)} %get-tuple-element.328), channel_id=1, source_target_pairs={{0,5},{1,4},{2,7},{3,6},{4,1},{5,0},{6,3},{7,2},{8,13},{9,12},{10,... | collective-permute-start | bytes 1032200 | tf_op jit(solution)/shard_map/ppermute | solution.py:828
  617.1 21.9 %collective-permute-start.45 = (bf16[4,56,768]{2,1,0:T(8,128)(2,1)}, bf16[4,56,768]{2,1,0:T(8,128)(2,1)S(1)}, u32[]{:S(2)}, u32[]{:S(2)}) collective-permute-start(bf16[4,56,768]{2,1,0:T(8,128)(2,1)} %get-tuple-element.328), channel_id=1, source_target_pairs={{0,4},{2,6},{4,0},{6,2},{8,12},{10,14},{12,8},{14,10},{16,20},{18,... | collective-permute-start | bytes 1032200 | tf_op jit(solution)/shard_map/ppermute | solution.py:827
  617.8 21.2 %collective-permute-start.44 = (bf16[4,56,768]{2,1,0:T(8,128)(2,1)S(1)}, bf16[4,56,768]{2,1,0:T(8,128)(2,1)S(1)}, u32[]{:S(2)}, u32[]{:S(2)}) collective-permute-start(bf16[4,56,768]{2,1,0:T(8,128)(2,1)S(1)} %get-tuple-element.327), channel_id=1, source_target_pairs={{0,1},{1,0},{2,3},{3,2},{4,5},{5,4},{6,7},{7,6},{8,9},{9,8},{10,11... | collective-permute-start | bytes 1032200 | tf_op jit(solution)/shard_map/ppermute | solution.py:825
  618.3 20.6 %collective-permute-start.48 = (bf16[192,768]{1,0:T(8,128)(2,1)}, bf16[192,768]{1,0:T(8,128)(2,1)S(1)}, u32[]{:S(2)}, u32[]{:S(2)}) collective-permute-start(bf16[192,768]{1,0:T(8,128)(2,1)} %get-tuple-element.312), channel_id=1, source_target_pairs={{0,16},{2,18},{4,20},{6,22},{8,24},{10,26},{12,28},{14,30},{16,0},... | collective-permute-start | bytes 884744 | tf_op jit(solution)/shard_map/ppermute | solution.py:827
  620.6 18.4 %collective-permute-start.49 = (bf16[192,768]{1,0:T(8,128)(2,1)}, bf16[192,768]{1,0:T(8,128)(2,1)S(1)}, u32[]{:S(2)}, u32[]{:S(2)}) collective-permute-start(bf16[192,768]{1,0:T(8,128)(2,1)} %get-tuple-element.310), channel_id=1, source_target_pairs={{0,24},{2,26},{4,28},{6,30},{8,16},{10,18},{12,20},{14,22},{16,8},... | collective-permute-start | bytes 884744 | tf_op jit(solution)/shard_map/ppermute | solution.py:827
  643.7 25.3 %collective-permute-start.53 = (bf16[1408,384]{1,0:T(8,128)(2,1)S(1)}, bf16[1408,384]{1,0:T(8,128)(2,1)S(1)}, u32[]{:S(2)}, u32[]{:S(2)}) collective-permute-start(bf16[1408,384]{1,0:T(8,128)(2,1)S(1)} %fusion.34), channel_id=1, source_target_pairs={{0,1},{1,0},{2,3},{3,2},{4,5},{5,4},{6,7},{7,6},{8,9},{9,8},{10,11... | collective-permute-start | bytes 3244040 | tf_op jit(solution)/shard_map/ppermute | solution.py:825
  647.2 13.0 %collective-permute-start.57 = (bf16[56,768]{1,0:T(8,128)(2,1)S(1)}, bf16[56,768]{1,0:T(8,128)(2,1)S(1)}, u32[]{:S(2)}, u32[]{:S(2)}) collective-permute-start(bf16[56,768]{1,0:T(8,128)(2,1)S(1)} %copy-done.73), channel_id=1, source_target_pairs={{0,24},{2,26},{4,28},{6,30},{8,16},{10,18},{12,20},{14,22},{16,8},... | collective-permute-start | bytes 258056 | tf_op jit(solution)/shard_map/ppermute | solution.py:827
  652.4 9.8 %collective-permute-start.56 = (bf16[56,768]{1,0:T(8,128)(2,1)S(1)}, bf16[56,768]{1,0:T(8,128)(2,1)S(1)}, u32[]{:S(2)}, u32[]{:S(2)}) collective-permute-start(bf16[56,768]{1,0:T(8,128)(2,1)S(1)} %copy-done.72), channel_id=1, source_target_pairs={{0,16},{2,18},{4,20},{6,22},{8,24},{10,26},{12,28},{14,30},{16,0},... | collective-permute-start | bytes 258056 | tf_op jit(solution)/shard_map/ppermute | solution.py:827
  673.0 43.2 %collective-permute-start.54 = (bf16[1408,384]{1,0:T(8,128)(2,1)}, bf16[1408,384]{1,0:T(8,128)(2,1)}, u32[]{:S(2)}, u32[]{:S(2)}) collective-permute-start(bf16[1408,384]{1,0:T(8,128)(2,1)} %dynamic-slice_add_fusion), channel_id=1, source_target_pairs={{0,1},{1,0},{2,3},{3,2},{4,5},{5,4},{6,7},{7,6},{8,9},{9,8},{10,11... | collective-permute-start | bytes 3244040 | tf_op jit(solution)/shard_map/ppermute | solution.py:825
  681.0 10.1 %collective-permute-start.60 = (bf16[3,56,768]{2,1,0:T(8,128)(2,1)S(1)}, bf16[3,56,768]{2,1,0:T(8,128)(2,1)S(1)}, u32[]{:S(2)}, u32[]{:S(2)}) collective-permute-start(bf16[3,56,768]{2,1,0:T(8,128)(2,1)S(1)} %get-tuple-element.340), channel_id=1, source_target_pairs={{0,24},{2,26},{4,28},{6,30},{8,16},{10,18},{12,20},{14,22},{16,8},... | collective-permute-start | bytes 774152 | tf_op jit(solution)/shard_map/ppermute | solution.py:827
  685.3 31.0 %collective-permute-start.59 = (bf16[3,56,768]{2,1,0:T(8,128)(2,1)S(1)}, bf16[3,56,768]{2,1,0:T(8,128)(2,1)S(1)}, u32[]{:S(2)}, u32[]{:S(2)}) collective-permute-start(bf16[3,56,768]{2,1,0:T(8,128)(2,1)S(1)} %get-tuple-element.340), channel_id=1, source_target_pairs={{0,16},{2,18},{4,20},{6,22},{8,24},{10,26},{12,28},{14,30},{16,0},... | collective-permute-start | bytes 774152 | tf_op jit(solution)/shard_map/ppermute | solution.py:827
  690.9 25.4 %collective-permute-start.58 = (bf16[3,56,768]{2,1,0:T(8,128)(2,1)S(1)}, bf16[3,56,768]{2,1,0:T(8,128)(2,1)S(1)}, u32[]{:S(2)}, u32[]{:S(2)}) collective-permute-start(bf16[3,56,768]{2,1,0:T(8,128)(2,1)S(1)} %get-tuple-element.340), channel_id=1, source_target_pairs={{0,8},{2,10},{4,12},{6,14},{8,0},{10,2},{12,4},{14,6},{16,24},{18,... | collective-permute-start | bytes 774152 | tf_op jit(solution)/shard_map/ppermute | solution.py:827
  719.7 34.2 %collective-permute-start.61 = (bf16[4,3,56,768]{3,2,1,0:T(8,128)(2,1)S(1)}, bf16[4,3,56,768]{3,2,1,0:T(8,128)(2,1)S(1)}, u32[]{:S(2)}, u32[]{:S(2)}) collective-permute-start(bf16[4,3,56,768]{3,2,1,0:T(8,128)(2,1)S(1)} %maximum_add_fusion.11), channel_id=1, source_target_pairs={{0,4},{2,6},{4,0},{6,2},{8,12},{10,14},{12,8},{14,10},{16,20},{18,... | collective-permute-start | bytes 3096584 | tf_op jit(solution)/shard_map/ppermute | solution.py:827
  758.7 21.9 %collective-permute-start.62 = (bf16[4,2,3,56,768]{4,3,2,0,1:T(8,128)(2,1)}, bf16[4,2,3,56,768]{4,3,2,0,1:T(8,128)(2,1)}, u32[]{:S(2)}, u32[]{:S(2)}) collective-permute-start(bf16[4,2,3,56,768]{4,3,2,0,1:T(8,128)(2,1)} %maximum_add_fusion.1), channel_id=1, source_target_pairs={{0,2},{2,0},{4,6},{6,4},{8,10},{10,8},{12,14},{14,12},{16,18},{18,... | collective-permute-start | bytes 6193160 | tf_op jit(solution)/shard_map/ppermute | solution.py:827
  (106 other events, 656.0 us)
Sparse Core Ops, SparseCore 0:
  426.0 54.5 all-gather.6
  545.6 66.1 all-gather.8
  676.8 77.7 all-gather.10

commit v2 on v1

--- a/solution.py
+++ b/solution.py
@@ -591,7 +591,7 @@
 
 def chan_backward_kernel(
     blocks,
-    first,
+    halves,
     info_ref,
     grad_ref,
     rows_ref,
@@ -603,7 +603,7 @@
     out_other_ref,
     *rest,
 ):
-    sum_ref, small_ref, back_ref, mark_ref, low_ref = rest[-5:]
+    *sum_refs, small_ref, back_ref, mark_ref, low_ref = rest[-4 - len(halves) :]
     mark_ref[0, 0] = 0.0
     step = pl.program_id(0)
 
@@ -612,67 +612,82 @@
         low = grad_ref[...].astype(B16)
         low_ref[...] = low
         small_ref[...] = jnp.zeros_like(small_ref)
-        if first:
+        if halves[0] == 0:
             small_ref[0:1, :] = jnp.sum(low.astype(F32), 0, keepdims=True)
             back_ref[...] = jnp.zeros_like(back_ref)
         else:
             back_ref[...] = rest[0][...]
 
-    def body(other, in_ref, out_ref):
+    def body(other, keep, in_ref, out_ref, sum_ref):
         low = low_ref[...]
         hidden = (dims_nt(low, out_ref[...]) * slope_ref[...].astype(F32)).astype(B16)
-        core = 1 - info_ref[CORE] if first else info_ref[CORE]
+        core = info_ref[CORE] if keep else 1 - info_ref[CORE]
         row = 1 + 2 * (info_ref[SIDE] ^ other) + core
         small_ref[pl.ds(row, 1), :] = jnp.sum(hidden.astype(F32), 0, keepdims=True)
         for item, grads in enumerate(
             (dims_tn(hidden, rows_ref[...]), dims_tn(quant_ref[...], low))
         ):
-            place = info_ref[PLACE]
             size = grads.shape[0] // blocks
             for k in range(blocks):
                 part = grads[k * size : (k + 1) * size, :].astype(B16)
-                sum_ref[item, k ^ place] = part
+                sum_ref[item, k ^ info_ref[PLACE]] = part
         back_ref[...] += dims_nt(hidden, in_ref[...])
 
-    pl.when(step == 0)(lambda: body(1, in_other_ref, out_other_ref))
-    pl.when(step == 1)(lambda: body(0, in_own_ref, out_own_ref))
+    sides = ((in_own_ref, out_own_ref), (in_other_ref, out_other_ref))
+    for k in range(2 * len(halves)):
+        other, place = 1 - k % 2, k // 2
+
+        @pl.when(step == k)
+        def _(other=other, place=place):
+            body(other, halves[place], *sides[other], sum_refs[place])
 
 
 def chan_backward(
-    info, grad, rows, quant, slope, own, other, pos, back, blocks, after=()
+    info, grad, rows, quant, slope, own, other, pos, back, blocks, halves, after=()
 ):
     count, width = rows.shape
     chunk = own[0].shape[2] // 2
-    first = back is None
-    core = lambda info: 1 - info[CORE] if first else info[CORE]
-    lanes = pl.BlockSpec((count, chunk), lambda s, info: (0, 2 * (1 - s) + core(info)))
+    if len(halves) == 2:
+        core = lambda s, info: jnp.where(s < 2, 1 - info[CORE], info[CORE])
+        which = lambda s: (jnp.minimum(s, 1), jnp.maximum(s - 2, 0))
+    else:
+        core = lambda s, info: info[CORE] if halves[0] else 1 - info[CORE]
+        which = lambda s: (s,)
+    lanes = pl.BlockSpec(
+        (count, chunk), lambda s, info: (0, 2 * (1 - lax.rem(s, 2)) + core(s, info))
+    )
     once = lambda rows, cols: pl.BlockSpec((rows, cols), lambda s, _: (0, 0))
     part = (None, 2, blocks, chunk // blocks, width)
-    sums = pl.BlockSpec(part, lambda s, _: (s,) + (0,) * (len(part) - 1))
-    extra = () if first else (back,)
+    sums = [
+        pl.BlockSpec(part, lambda s, _, i=i: (which(s)[i], 0, 0, 0, 0))
+        for i in range(len(halves))
+    ]
+    extra = () if halves[0] == 0 else (back,)
     mark = mark_spec()
     return kernel_call(
-        functools.partial(chan_backward_kernel, blocks, first),
-        (2,),
+        functools.partial(chan_backward_kernel, blocks, halves),
+        (2 * len(halves),),
         [once(count, width), once(count, width), lanes, lanes]
         + [
-            pl.BlockSpec((None, width, chunk), lambda s, info: (pos, 0, core(info))),
-            pl.BlockSpec((None, chunk, width), lambda s, info: (pos, core(info), 0)),
-            pl.BlockSpec((width, chunk), lambda s, info: (0, core(info))),
-            pl.BlockSpec((chunk, width), lambda s, info: (core(info), 0)),
+            pl.BlockSpec((None, width, chunk), lambda s, info: (pos, 0, core(s, info))),
+            pl.BlockSpec((None, chunk, width), lambda s, info: (pos, core(s, info), 0)),
+            pl.BlockSpec((width, chunk), lambda s, info: (0, core(s, info))),
+            pl.BlockSpec((chunk, width), lambda s, info: (core(s, info), 0)),
         ]
         + [once(count, width)] * len(extra)
         + free_specs(after),
-        [sums, once(8, width), once(count, width), mark[0]],
-        [
-            jax.ShapeDtypeStruct((2,) + part[1:], B16),
+        sums + [once(8, width), once(count, width), mark[0]],
+        [jax.ShapeDtypeStruct((2,) + part[1:], B16)] * len(halves)
+        + [
             jax.ShapeDtypeStruct((8, width), F32),
             jax.ShapeDtypeStruct((count, width), F32),
             mark[1],
         ],
         scratch=[pltpu.VMEM((count, width), B16)],
         prefetch=1,
-        cost=cost_of(16 * count * chunk * width, 8 * count * chunk + 16 * count * width),
+        cost=cost_of(
+            16 * len(halves) * count * chunk * width, 8 * count * chunk + 16 * count * width
+        ),
     )(info, grad, rows, quant, slope, *own, *other, *extra, *after)
 
 
@@ -847,8 +862,8 @@
         self.flows = []
         self.mark = None
 
-    def start(self, steps, first=False):
-        flow = {"steps": steps, "got": None}
+    def start(self, steps, first=False, tied=False):
+        flow = {"steps": steps, "got": None, "tied": tied}
         self.flows.insert(0 if first else len(self.flows), flow)
         return flow
 
@@ -860,7 +875,7 @@
                 sends = flow["steps"].send(flow["got"])
         except StopIteration:
             self.flows.remove(flow)
-            return []
+            return list(flow["got"]) if flow["tied"] else []
         flow["got"] = [exchange(value, *masks) for value, *masks in sends]
         return [send[0] for send in sends]
 
@@ -873,8 +888,8 @@
     def finish(self, flow):
         self.step(flow)
 
-    def arrived(self):
-        self.mark = mark_after(*[got for flow in self.flows for got in flow["got"]])
+    def arrived(self, *also):
+        self.mark = mark_after(*[got for flow in self.flows for got in flow["got"]], *also)
 
     def zero(self):
         return self.mark[0, 0]
@@ -922,7 +937,7 @@
     return total.astype(B16)
 
 
-def upper_grad_steps(line, send, keep, found):
+def upper_grad_steps(line, send, keep, pack, found):
     (got,) = yield [(send, 1, 0)]
     keep = keep[0]
     half = keep.shape[2] // 2
@@ -934,13 +949,13 @@
     own[1] = line.add(own[1], got)
     got = yield [(other[0], 0, 1), (own[1], 2, 0)]
     own = line.add(own[0], *got)
-    own = jnp.concatenate([own[0], own[1]], 1)
+    own = jnp.concatenate([own[0], own[1], *pack], 1)
     mine, sends = far_blocks(line, own)
     got = yield sends
     found.append(plain_sum(mine, *got))
 
 
-def lowest_grad_steps(line, send, keep, found):
+def lowest_grad_steps(line, send, keep, pack, found):
     (got,) = yield [(send, 1, 0)]
     keep = keep[0]
     half = keep.shape[2] // 2
@@ -953,38 +968,33 @@
     in_low, in_high = line.add(in_low, got[0][:half]), line.add(in_high, got[0][half:])
     out_other, out_own = line.add(out_other, got[1][0]), line.add(out_own, got[1][1])
     got = yield [(in_high, 2, 0), (out_other, 0, 1)]
-    own = jnp.concatenate([line.add(in_low, got[0]), line.add(out_own, got[1])], 1)
+    own = jnp.concatenate([line.add(in_low, got[0]), line.add(out_own, got[1]), *pack], 1)
     mine, sends = far_blocks(line, own)
     got = yield sends
-    found.append(plain_sum(mine, *got))
-
-
-def pack_sum_steps(line, pack, at_once, found):
+    found.append(line.add(mine, *got))
+
+
+def pack_near_steps(line, pack, found):
     count = lax.axis_size("dp")
     here = lax.axis_index("dp")
     pack = pack.reshape(count // 4, 2, 2, -1, pack.shape[1])
     near = lambda value, bit, k, axis: lax.dynamic_index_in_dim(value, dp_bit(bit) ^ k, axis, False)
     (got,) = yield [(line.gate(near(pack, 0, 1, 2)), 1, 0)]
     pack = line.add(near(pack, 0, 0, 2), got)
-    mine, away = near(pack, 1, 0, 1), near(pack, 1, 1, 1)
-    if at_once:
-        got = yield [(mine, 0, 1), (away, 2, 0), (away, 2, 1)]
-        mine = line.add(mine, *got)
-    else:
-        (got,) = yield [(away, 2, 0)]
-        mine = line.add(mine, got)
-        (got,) = yield [(mine, 0, 1)]
-        mine = line.add(mine, got)
+    (got,) = yield [(near(pack, 1, 1, 1), 2, 0)]
+    mine = line.add(near(pack, 1, 0, 1), got)
+    (got,) = yield [(mine, 0, 1)]
+    mine = line.add(mine, got)
     far = lambda k: lax.dynamic_index_in_dim(mine, (here >> 2) ^ k, 0, False)
-    mine, sends = far_blocks(line, [far(k) for k in range(count // 4)])
+    found.append(jnp.stack([far(k) for k in range(count // 4)]))
+
+
+def pack_all_steps(line, pack, found):
+    near = []
+    yield from pack_near_steps(line, pack, near)
+    mine, sends = far_blocks(line, near[0])
     got = yield sends
-    found.append(line.add(mine, *got))
-
-
-def pack_all_steps(line, pack, sums, found):
-    mine = []
-    yield from pack_sum_steps(line, pack, True, mine)
-    mine = jnp.stack(mine + [s[0] for s in sums])
+    mine = line.add(mine, *got)
     got = yield [(mine, k << 2, 0) for k in range(1, lax.axis_size("dp") // 4)]
     parts = line.gate(jnp.stack([mine, *got]))
     (got,) = yield [(parts, 2, 0)]
@@ -1121,7 +1131,7 @@
     kept = []
     for pos in range(layers):
         if pos > 0:
-            if pos == layers - 1:
+            if pos == 1:
                 line.start(one_step(line, pick(cots, 1 - side), cot_found))
             ties = line.tick()
         parts, base = [], ()
@@ -1147,9 +1157,11 @@
             line.tick()
         line.tick()
     out = (stream * live[:, 0:1]).astype(B16)
-    grad, line.mark = join_features(info, pick(cots, side), cot_found[0], live)
+    grad, line.mark = join_features(info, line.gate(pick(cots, side)), cot_found[0], live)
 
     block = units // count
+    line.start(one_step(line, features(out, 1 - side), out_found), tied=True)
+
     grads_found = [[] for _ in range(layers)]
     pack_found = [[] for _ in range(layers)]
     gathered = [None] * layers
@@ -1158,26 +1170,24 @@
     def gather_ready():
         for pos in reversed(range(layers)):
             if gathered[pos] is None and grads_found[pos]:
-                payload = grads_found[pos][0]
-                if pos + 1 < layers:
-                    payload = payload + mark_after(gathered[pos + 1])[0, 0].astype(B16)
-                gathered[pos] = lax.all_gather(payload, "dp")
+                gathered[pos] = lax.all_gather(grads_found[pos][0], "dp")
 
     for pos in reversed(range(layers)):
         parts, rows, quant, slope, other = kept[pos]
         back, small, keep = None, 0.0, []
-        for half in range(2):
+        for halves in ((0,), (1,)):
             ties = line.tick()
             gather_ready()
-            value, part_small, back, line.mark = chan_backward(
-                info, grad, rows, quant, slope, own, other, pos, back, count // 2, ties
+            *sums, part_small, back, line.mark = chan_backward(
+                info, grad, rows, quant, slope, own, other, pos, back, count // 2, halves, ties
             )
             small = small + part_small
-            if half == 0:
+            if 0 in halves:
                 steps = upper_grad_steps if pos > 0 else lowest_grad_steps
-                line.start(steps(line, value, keep, grads_found[pos]))
-            else:
-                keep.append(value)
+                above = pack_found[pos + 1] if pos + 1 < layers else []
+                line.start(steps(line, sums[0], keep, above, grads_found[pos]))
+            if 1 in halves:
+                keep.append(sums[-1])
         ties = line.tick()
         gather_ready()
         base, token_grads, smalls = (), [], []
@@ -1204,31 +1214,34 @@
         fill = jnp.zeros((-size % (8 * count), width), F32)
         pack = jnp.concatenate(pieces + [fill], 0).astype(B16)
         if pos > 0:
-            line.start(pack_sum_steps(line, pack, False, pack_found[pos]), first=True)
+            line.start(pack_near_steps(line, pack, pack_found[pos]), first=True)
         else:
-            line.start(pack_all_steps(line, pack, pack_found[1:], pack_found[0]))
+            line.start(pack_all_steps(line, pack, pack_found[0]))
 
     grad_found = []
-    line.start(one_step(line, features(grad, 1 - side).astype(B16), grad_found, 2))
-    line.start(one_step(line, features(out, 1 - side), out_found, 3))
-    done = layers
+    line.start(one_step(line, features(grad, 1 - side).astype(B16), grad_found, 3))
+    done, ticks = layers, 0
     while line.flows:
         line.tick()
+        ticks += 1
         gather_ready()
-        if done > 1 and (done == layers or gathered[done - 2] is not None):
+        also = []
+        if done > 1 and ticks > 1:
             done -= 1
-            *chan_grads, line.mark = assemble(
+            *chan_grads, mark = assemble(
                 gathered[done], places, done, layers, block, tuple(chan_grads)
             )
+            also = [mark]
         if any(flow["got"] for flow in line.flows):
-            line.arrived()
-    outs = to_features(features(out, side), out_found[0])
-    grads = to_features(features(grad, side), grad_found[0].astype(F32))
+            line.arrived(*also)
+    outs = to_features(features(out, side), line.gate(out_found[0]))
+    grads = to_features(features(grad, side), line.gate(grad_found[0].astype(F32)))
     while done:
         done -= 1
         *chan_grads, _ = assemble(gathered[done], places, done, layers, block, tuple(chan_grads))
     pack_rows = pack.shape[0]
-    pack = jnp.swapaxes(pack_found[0][0], 0, 1).reshape(layers, pack_rows, width)
+    pack = pack_found[0] + [g[:, 2 * block :] for g in gathered[: layers - 1]]
+    pack = jnp.stack([p.reshape(pack_rows, width) for p in pack])
     hidden_tok = mix_bias_small.shape[1]
     token_parts = []
     at = 0

time: 820 us -> 782 us (0.954)
  starting transfers between devices: 85.1 us -> 59.2 us
  waiting for transfers between devices: 123 us -> 109 us
  local copies, waits for them, and re-layouts: 60.1 us -> 68.5 us
    ppermute x48 -> x42, starting transfers between devices: 68.5 us -> 43 us  [exchange(): return lax.ppermute(value, 'dp', [(i, i ^ mask) for i in range(count)])]
    ppermute x48 -> x42, waiting for transfers between devices: 88.6 us -> 72.6 us  [exchange(): return lax.ppermute(value, 'dp', [(i, i ^ mask) for i in range(count)])]
    convert_element_type x18 -> x21, other arithmetic: 58.4 us -> 63.8 us  [add(): return (total + self.zero()).astype(B16)]
    unnamed x228 -> x194, local copies, waits for them, and re-layouts: 18 us -> 21.4 us
    add x28 -> x31, other arithmetic: 41.4 us -> 44.3 us  [gate(): value + self.zero().astype(value.dtype)]
  transfers between devices with their start and end apart: 72 -> 65, of which waited for: 11 -> 15; matrix products, arithmetic and copies ran while one was open for 22% -> 22% of each run, Pallas kernels for 39% -> 47%
where the time goes in v2:
time: 782 us; the launch traced here: 775 us
  Pallas kernels  378 us (48%)
  other arithmetic  134 us (17%)
  waiting for transfers between devices  109 us (14%)
  local copies, waits for them, and re-layouts  68.5 us (9%)
  starting transfers between devices  59.2 us (8%)
  between operations  26 us (3%)
    pallas_call x6, Pallas kernels, chan_backward(): kernel_call(functools.partial(chan_backward_kernel, blocks, halves), (2 *...  159 us
    pallas_call x3, Pallas kernels, chan_forward(): kernel_call(functools.partial(chan_forward_kernel, part), (count // tile,...  74.7 us
    ppermute x42, waiting for transfers between devices, exchange(): return lax.ppermute(value, 'dp', [(i, i ^ mask) for i in range(count)])  72.6 us
    convert_element_type x21, other arithmetic, add(): return (total + self.zero()).astype(B16)  63.8 us
    pallas_call x6, Pallas kernels, token_backward(): kernel_call(token_backward_kernel, (images,), [placed, placed, block(patc...  62.1 us
    pallas_call x6, Pallas kernels, token_forward(): kernel_call(token_forward_kernel, (images,), [placed] + [layer_spec(a, po...  44.7 us
    add x31, other arithmetic, gate(): value + self.zero().astype(value.dtype)  44.3 us
    ppermute x42, starting transfers between devices, exchange(): return lax.ppermute(value, 'dp', [(i, i ^ mask) for i in range(count)])  43 us
  transfers between devices with their start and end apart: 65, of which 15 were waited for; matrix products, arithmetic and copies ran while one was open for 22% of the time, Pallas kernels for 47%

profile of v2, /device:TPU:1, one launch (start us, length us, event | category | flops | bytes accessed | tf_op | source)
XLA Modules:
  0.0 774.7 jit_solution(14295206518510667363)
XLA Ops:
  17.1 2.9 constant_dynamic-slice_fusion.18
  28.1 8.2 %collective-permute-done.refs_0_ = bf16[1,192,1536]{2,1,0:T(8,128)(2,1)S(1)} collective-permute-done((bf16[1,192,1536]{2,1,0:T(8,128)(2,1)}, bf16[1,192,1536]{2,1,0:T(8,128)(2,1)S(1)}, u32[]{:S(2)}, u32[]{:S(2)}) %collective-permute-start) | collective-permute-done | bytes 589856 | tf_op jit(solution)/shard_map/ppermute | solution.py:840
  50.4 15.6 %collective-permute-done.2.got_ref.refs_0_ = bf16[1408,384]{1,0:T(8,128)(2,1)S(1)} collective-permute-done((bf16[1408,384]{1,0:T(8,128)(2,1)}, bf16[1408,384]{1,0:T(8,128)(2,1)S(1)}, u32[]{:S(2)}, u32[]{:S(2)}) %collective-permute-start.2) | collective-permute-done | bytes 1081376 | tf_op jit(solution)/shard_map/ppermute | solution.py:840
  75.0 2.9 collective-permute-start.6
  80.0 5.3 shard_map.323
  85.3 8.7 %shard_map.325 = (f32[1408,768]{1,0:T(8,128)}, bf16[1408,768]{1,0:T(8,128)(2,1)}, bf16[832,768]{1,0:T(8,128)(2,1)}, bf16[1536,768]{1,0:T(8,128)(2,1)}, bf16[1536...) custom-call(f32[1408,768]{1,0:T(8,128)} %get-tuple-element.140.x_ref, ...), custom_call_target="tpu_custom_call" | custom-call | flops 196293427200 | bytes 3833856000 | tf_op jit(solution)/shard_map/pallas_call | solution.py:459
  94.0 6.0 shard_map.326
  111.4 24.5 %shard_map.327 = (bf16[1408,3072]{1,0:T(8,128)(2,1)}, bf16[1408,3072]{1,0:T(8,128)(2,1)}, f32[1408,768]{1,0:T(8,128)}, bf16[768,1536]{1,0:T(8,128)(2,1)}, bf16[1536,768]{1,0:T(8,128)(2,1)}, /*index=5*/f32[1,1]{1,0:T(1,128)}) custom-call(s32[4]{0:T(128)} %pad_add_fusion.info_ref, bf16[1408,768]{1,0:T(8,128)(2,1)} %get-tuple-element.143.rows_ref, ...), custom_call_target="tpu_custom_call" | custom-call | flops 2657511014400 | bytes 5622988800 | tf_op jit(solution)/shard_map/pallas_call | solution.py:570
  144.2 2.4 maximum_add_fusion.2.rest_0_.in_near_ref
  146.6 2.5 collective-permute-start.14
  149.1 2.4 maximum_add_fusion.3.rest_1_.out_near_ref
  151.4 9.2 %shard_map.328 = (f32[1408,768]{1,0:T(8,128)}, bf16[1408,768]{1,0:T(8,128)(2,1)}, bf16[832,768]{1,0:T(8,128)(2,1)}, bf16[1536,768]{1,0:T(8,128)(2,1)}, bf16[1536...) custom-call(f32[1408,768]{1,0:T(8,128)} %get-tuple-element.146.x_ref, ...), custom_call_target="tpu_custom_call" | custom-call | flops 196293427200 | bytes 3833856000 | tf_op jit(solution)/shard_map/pallas_call | solution.py:459
  160.6 6.1 shard_map.329
  166.7 25.1 %shard_map.330 = (bf16[1408,3072]{1,0:T(8,128)(2,1)}, bf16[1408,3072]{1,0:T(8,128)(2,1)}, f32[1408,768]{1,0:T(8,128)}, bf16[768,1536]{1,0:T(8,128)(2,1)}, bf16[1536,768]{1,0:T(8,128)(2,1)}, /*index=5*/f32[1,1]{1,0:T(1,128)}) custom-call(s32[4]{0:T(128)} %pad_add_fusion.info_ref, bf16[1408,768]{1,0:T(8,128)(2,1)} %get-tuple-element.150.rows_ref, ...), custom_call_target="tpu_custom_call" | custom-call | flops 2657511014400 | bytes 5622988800 | tf_op jit(solution)/shard_map/pallas_call | solution.py:570
  192.5 2.4 maximum_add_fusion.4.rest_0_.in_near_ref
  195.3 2.4 maximum_add_fusion.5.rest_1_.out_near_ref
  197.7 8.7 %shard_map.331 = (f32[1408,768]{1,0:T(8,128)}, bf16[1408,768]{1,0:T(8,128)(2,1)}, bf16[832,768]{1,0:T(8,128)(2,1)}, bf16[1536,768]{1,0:T(8,128)(2,1)}, bf16[1536...) custom-call(f32[1408,768]{1,0:T(8,128)} %get-tuple-element.152.x_ref, ...), custom_call_target="tpu_custom_call" | custom-call | flops 196293427200 | bytes 3833856000 | tf_op jit(solution)/shard_map/pallas_call | solution.py:459
  206.4 6.1 shard_map.332
  212.5 25.2 %shard_map.333 = (bf16[1408,3072]{1,0:T(8,128)(2,1)}, bf16[1408,3072]{1,0:T(8,128)(2,1)}, f32[1408,768]{1,0:T(8,128)}, bf16[768,1536]{1,0:T(8,128)(2,1)}, bf16[1536,768]{1,0:T(8,128)(2,1)}, /*index=5*/f32[1,1]{1,0:T(1,128)}) custom-call(s32[4]{0:T(128)} %pad_add_fusion.info_ref, bf16[1408,768]{1,0:T(8,128)(2,1)} %get-tuple-element.156.rows_ref, ...), custom_call_target="tpu_custom_call" | custom-call | flops 2657511014400 | bytes 5622988800 | tf_op jit(solution)/shard_map/pallas_call | solution.py:570
  239.6 2.5 multiply_convert_fusion
  243.5 5.2 shard_map.334
  251.0 26.1 %shard_map.335 = (bf16[2,2,8,96,768]{4,3,2,1,0:T(8,128)(2,1)}, f32[8,768]{1,0:T(8,128)}, f32[1408,768]{1,0:T(8,128)}, f32[1,1]{1,0:T(1,128)}) custom-call(s32[4]{0:T(128)} %pad_add_fusion.info_ref, f32[1408,768]{1,0:T(8,128)} %get-tuple-element.161.grad_ref, bf16[1408,768]{1,0:T(8,128)(2,1)} %get-tuple-element.156.rows_ref, ...), custom_call_target="tpu_custom_call" | custom-call | flops 2657511014400 | bytes 5190451200 | tf_op jit(solution)/shard_map/pallas_call | solution.py:667
  278.0 26.6 %shard_map.336 = (bf16[2,2,8,96,768]{4,3,2,1,0:T(8,128)(2,1)}, f32[8,768]{1,0:T(8,128)}, f32[1408,768]{1,0:T(8,128)}, f32[1,1]{1,0:T(1,128)}) custom-call(s32[4]{0:T(128)} %pad_add_fusion.info_ref, f32[1408,768]{1,0:T(8,128)} %get-tuple-element.161.grad_ref, bf16[1408,768]{1,0:T(8,128)(2,1)} %get-tuple-element.156.rows_ref, ...), custom_call_target="tpu_custom_call" | custom-call | flops 2657511014400 | bytes 5190451200 | tf_op jit(solution)/shard_map/pallas_call | solution.py:667
  304.7 5.2 fusion.18
  310.8 12.4 %shard_map.337 = (f32[1408,768]{1,0:T(8,128)}, f32[208,768]{1,0:T(8,128)}, f32[8,768]{1,0:T(8,128)}, f32[1,1]{1,0:T(1,128)}) custom-call(f32[1408,768]{1,0:T(8,128)} %get-tuple-element.161.grad_ref, f32[1408,768]{1,0:T(8,128)} %get-tuple-element.168.back_ref, bf16[832,768]{1,0:T(8,128)(2,1)} %get-tuple-element.175.vhat_two_ref, ...), custom_call_target="tpu_custom_call" | custom-call | flops 392586854400 | bytes 3833856000 | tf_op jit(solution)/shard_map/pallas_call | solution.py:817
  323.2 8.4 %shard_map.338 = (f32[1408,768]{1,0:T(8,128)}, f32[576,768]{1,0:T(8,128)}, f32[8,768]{1,0:T(8,128)}, f32[1,1]{1,0:T(1,128)}) custom-call(f32[1408,768]{1,0:T(8,128)} %get-tuple-element.161.grad_ref, f32[1408,768]{1,0:T(8,128)} %get-tuple-element.168.back_ref, bf16[576,768]{1,0:T(8,128)(2,1)} %get-tuple-element.169.vhat_two_ref, ...), custom_call_target="tpu_custom_call", output_to_operand_aliasing={{0}: (11, {})} | custom-call | flops 271790899200 | bytes 2654208000 | tf_op jit(solution)/shard_map/pallas_call | solution.py:817
  338.8 4.9 fusion.10.rest_2_
  344.9 25.9 %shard_map.339 = (bf16[2,2,8,96,768]{4,3,2,1,0:T(8,128)(2,1)}, f32[8,768]{1,0:T(8,128)}, f32[1408,768]{1,0:T(8,128)}, f32[1,1]{1,0:T(1,128)}) custom-call(s32[4]{0:T(128)} %pad_add_fusion.info_ref, f32[1408,768]{1,0:T(8,128)} %get-tuple-element.184.grad_ref, bf16[1408,768]{1,0:T(8,128)(2,1)} %get-tuple-element.150.rows_ref, ...), custom_call_target="tpu_custom_call" | custom-call | flops 2657511014400 | bytes 5190451200 | tf_op jit(solution)/shard_map/pallas_call | solution.py:667
  374.9 4.4 fusion.8
  381.2 3.3 collective-permute-start.48
  384.8 27.2 %shard_map.340 = (bf16[2,2,8,96,768]{4,3,2,1,0:T(8,128)(2,1)}, f32[8,768]{1,0:T(8,128)}, f32[1408,768]{1,0:T(8,128)}, f32[1,1]{1,0:T(1,128)}) custom-call(s32[4]{0:T(128)} %pad_add_fusion.info_ref, f32[1408,768]{1,0:T(8,128)} %get-tuple-element.184.grad_ref, bf16[1408,768]{1,0:T(8,128)(2,1)} %get-tuple-element.150.rows_ref, ...), custom_call_target="tpu_custom_call" | custom-call | flops 2657511014400 | bytes 5190451200 | tf_op jit(solution)/shard_map/pallas_call | solution.py:667
  412.1 2.5 fusion.51.rest_0_
  417.7 5.2 fusion.22
  423.5 12.3 %shard_map.341 = (f32[1408,768]{1,0:T(8,128)}, f32[208,768]{1,0:T(8,128)}, f32[8,768]{1,0:T(8,128)}, f32[1,1]{1,0:T(1,128)}) custom-call(f32[1408,768]{1,0:T(8,128)} %get-tuple-element.184.grad_ref, f32[1408,768]{1,0:T(8,128)} %get-tuple-element.199.back_ref, bf16[832,768]{1,0:T(8,128)(2,1)} %get-tuple-element.206.vhat_two_ref, ...), custom_call_target="tpu_custom_call" | custom-call | flops 392586854400 | bytes 3833856000 | tf_op jit(solution)/shard_map/pallas_call | solution.py:817
  437.6 8.4 %shard_map.342 = (f32[1408,768]{1,0:T(8,128)}, f32[576,768]{1,0:T(8,128)}, f32[8,768]{1,0:T(8,128)}, f32[1,1]{1,0:T(1,128)}) custom-call(f32[1408,768]{1,0:T(8,128)} %get-tuple-element.184.grad_ref, f32[1408,768]{1,0:T(8,128)} %get-tuple-element.199.back_ref, bf16[576,768]{1,0:T(8,128)(2,1)} %get-tuple-element.200.vhat_two_ref, ...), custom_call_target="tpu_custom_call", output_to_operand_aliasing={{0}: (11, {})} | custom-call | flops 271790899200 | bytes 2654208000 | tf_op jit(solution)/shard_map/pallas_call | solution.py:817
  457.3 4.9 fusion.5.rest_2_
  463.4 26.4 %shard_map.343 = (bf16[2,2,8,96,768]{4,3,2,1,0:T(8,128)(2,1)}, f32[8,768]{1,0:T(8,128)}, f32[1408,768]{1,0:T(8,128)}, f32[1,1]{1,0:T(1,128)}) custom-call(s32[4]{0:T(128)} %pad_add_fusion.info_ref, f32[1408,768]{1,0:T(8,128)} %get-tuple-element.215.grad_ref, bf16[1408,768]{1,0:T(8,128)(2,1)} %get-tuple-element.143.rows_ref, ...), custom_call_target="tpu_custom_call" | custom-call | flops 2657511014400 | bytes 5190451200 | tf_op jit(solution)/shard_map/pallas_call | solution.py:667
  493.7 4.4 fusion.3
  501.3 3.5 collective-permute-start.52
  505.1 27.0 %shard_map.344 = (bf16[2,2,8,96,768]{4,3,2,1,0:T(8,128)(2,1)}, f32[8,768]{1,0:T(8,128)}, f32[1408,768]{1,0:T(8,128)}, f32[1,1]{1,0:T(1,128)}) custom-call(s32[4]{0:T(128)} %pad_add_fusion.info_ref, f32[1408,768]{1,0:T(8,128)} %get-tuple-element.215.grad_ref, bf16[1408,768]{1,0:T(8,128)(2,1)} %get-tuple-element.143.rows_ref, ...), custom_call_target="tpu_custom_call" | custom-call | flops 2657511014400 | bytes 5190451200 | tf_op jit(solution)/shard_map/pallas_call | solution.py:667
  532.2 2.5 fusion.49.rest_0_
  539.8 3.6 fusion.25.rest_1_
  543.9 3.6 fusion.26.rest_2_
  548.8 12.2 %shard_map.345 = (f32[1408,768]{1,0:T(8,128)}, f32[208,768]{1,0:T(8,128)}, f32[8,768]{1,0:T(8,128)}, f32[1,1]{1,0:T(1,128)}) custom-call(f32[1408,768]{1,0:T(8,128)} %get-tuple-element.215.grad_ref, f32[1408,768]{1,0:T(8,128)} %get-tuple-element.230.back_ref, bf16[832,768]{1,0:T(8,128)(2,1)} %get-tuple-element.231.vhat_two_ref, ...), custom_call_target="tpu_custom_call" | custom-call | flops 392586854400 | bytes 3833856000 | tf_op jit(solution)/shard_map/pallas_call | solution.py:817
  561.1 8.4 %shard_map.346 = (f32[1408,768]{1,0:T(8,128)}, f32[576,768]{1,0:T(8,128)}, f32[8,768]{1,0:T(8,128)}, f32[1,1]{1,0:T(1,128)}) custom-call(f32[1408,768]{1,0:T(8,128)} %get-tuple-element.215.grad_ref, f32[1408,768]{1,0:T(8,128)} %get-tuple-element.230.back_ref, bf16[576,768]{1,0:T(8,128)(2,1)} %get-tuple-element.240.vhat_two_ref, ...), custom_call_target="tpu_custom_call", output_to_operand_aliasing={{0}: (11, {})} | custom-call | flops 271790899200 | bytes 2654208000 | tf_op jit(solution)/shard_map/pallas_call | solution.py:817
  573.9 10.7 %collective-permute-done.39 = bf16[2,4,96,768]{3,2,1,0:T(8,128)(2,1)} collective-permute-done((bf16[2,4,96,768]{3,2,1,0:T(8,128)(2,1)}, bf16[2,4,96,768]{3,2,1,0:T(8,128)(2,1)}, u32[]{:S(2)}, u32[]{:S(2)}) %collective-permute-start.39) | collective-permute-done | bytes 1179680 | tf_op jit(solution)/shard_map/ppermute | solution.py:842
  584.7 3.5 fusion.32
  592.2 8.8 %collective-permute-done.40.refs_1_ = bf16[4,96,768]{2,1,0:T(8,128)(2,1)S(1)} collective-permute-done((bf16[4,96,768]{2,1,0:T(8,128)(2,1)S(1)}, bf16[4,96,768]{2,1,0:T(8,128)(2,1)S(1)}, u32[]{:S(2)}, u32[]{:S(2)}) %collective-permute-start.40) | collective-permute-done | bytes 589856 | tf_op jit(solution)/shard_map/ppermute | solution.py:840
  601.0 6.9 collective-permute-done.38.refs_0_
  609.2 4.8 add_convert_fusion.12
  621.1 6.5 shard_map.348
  628.9 18.4 %collective-permute-done.44.refs_1_ = bf16[248,768]{1,0:T(8,128)(2,1)S(1)} collective-permute-done((bf16[248,768]{1,0:T(8,128)(2,1)}, bf16[248,768]{1,0:T(8,128)(2,1)S(1)}, u32[]{:S(2)}, u32[]{:S(2)}) %collective-permute-start.44) | collective-permute-done | bytes 380960 | tf_op jit(solution)/shard_map/ppermute | solution.py:842
  649.4 2.9 fusion.39
  654.0 7.1 shard_map.350
  667.0 2.4 collective-permute-start.55
  669.7 5.2 collective-permute-done.53.refs_0_
  676.7 8.1 %collective-permute-done.54.refs_1_ = bf16[56,768]{1,0:T(8,128)(2,1)S(1)} collective-permute-done((bf16[56,768]{1,0:T(8,128)(2,1)S(1)}, bf16[56,768]{1,0:T(8,128)(2,1)S(1)}, u32[]{:S(2)}, u32[]{:S(2)}) %collective-permute-start.54) | collective-permute-done | bytes 86048 | tf_op jit(solution)/shard_map/ppermute | solution.py:842
  684.8 3.4 collective-permute-done.56.refs_3_
  694.9 3.5 collective-permute-done.59.refs_2_
  698.4 10.1 %collective-permute-done.58.refs_1_ = bf16[56,768]{1,0:T(8,128)(2,1)S(1)} collective-permute-done((bf16[56,768]{1,0:T(8,128)(2,1)S(1)}, bf16[56,768]{1,0:T(8,128)(2,1)S(1)}, u32[]{:S(2)}, u32[]{:S(2)}) %collective-permute-start.58) | collective-permute-done | bytes 86048 | tf_op jit(solution)/shard_map/ppermute | solution.py:842
  714.0 4.5 collective-permute-done.60.refs_0_
  721.7 4.2 collective-permute-start.61
  757.7 2.7 slice_bitcast_fusion
  760.4 6.9 shard_map.356
  (456 shorter events, 184.9 us)
Async XLA Ops:
  7.3 613.8 %all-gather.7.cloned.1.call-start = ((), (), s32[]{:S(2)}) async-start(), calls=%async_computation | async-start | bytes 5013504 | tf_op jit(solution)/shard_map/all_gather | solution.py:1173
  8.5 19.6 %collective-permute-start.1 = (bf16[1,384,768]{2,1,0:T(8,128)(2,1)S(1)}, bf16[1,384,768]{2,1,0:T(8,128)(2,1)S(1)}, u32[]{:S(2)}, u32[]{:S(2)}) collective-permute-start(bf16[1,384,768]{2,1,0:T(8,128)(2,1)S(1)} %constant_dynamic-slice_fusion.20), channel_id=1, source_target_pairs={{0,1},{1,0},{2,3},{3,2},{4,5},{5,4},{6,7},{7,6},{8,9},{9,8},{10,11... | collective-permute-start | bytes 1769480 | tf_op jit(solution)/shard_map/ppermute | solution.py:840
  12.6 23.8 %collective-permute-start = (bf16[1,192,1536]{2,1,0:T(8,128)(2,1)}, bf16[1,192,1536]{2,1,0:T(8,128)(2,1)S(1)}, u32[]{:S(2)}, u32[]{:S(2)}) collective-permute-start(bf16[1,192,1536]{2,1,0:T(8,128)(2,1)} %constant_dynamic-slice_fusion.21), channel_id=1, source_target_pairs={{0,1},{1,0},{2,3},{3,2},{4,5},{5,4},{6,7},{7,6},{8,9},{9,8},{10,11... | collective-permute-start | bytes 1769480 | tf_op jit(solution)/shard_map/ppermute | solution.py:840
  42.2 23.7 %collective-permute-start.2 = (bf16[1408,384]{1,0:T(8,128)(2,1)}, bf16[1408,384]{1,0:T(8,128)(2,1)S(1)}, u32[]{:S(2)}, u32[]{:S(2)}) collective-permute-start(bf16[1408,384]{1,0:T(8,128)(2,1)} %maximum_add_fusion.6), channel_id=1, source_target_pairs={{0,1},{1,0},{2,3},{3,2},{4,5},{5,4},{6,7},{7,6},{8,9},{9,8},{10,11... | collective-permute-start | bytes 3244040 | tf_op jit(solution)/shard_map/ppermute | solution.py:840
  43.4 30.5 %collective-permute-start.4 = (bf16[1,192,1536]{2,1,0:T(8,128)(2,1)}, bf16[1,192,1536]{2,1,0:T(8,128)(2,1)S(1)}, u32[]{:S(2)}, u32[]{:S(2)}) collective-permute-start(bf16[1,192,1536]{2,1,0:T(8,128)(2,1)} %broadcast_add_fusion.6), channel_id=1, source_target_pairs={{0,4},{2,6},{4,0},{6,2},{8,12},{10,14},{12,8},{14,10},{16,20},{18,... | collective-permute-start | bytes 1769480 | tf_op jit(solution)/shard_map/ppermute | solution.py:842
  45.5 32.5 %collective-permute-start.5 = (bf16[1,384,768]{2,1,0:T(8,128)(2,1)}, bf16[1,384,768]{2,1,0:T(8,128)(2,1)S(1)}, u32[]{:S(2)}, u32[]{:S(2)}) collective-permute-start(bf16[1,384,768]{2,1,0:T(8,128)(2,1)} %broadcast_add_fusion.5), channel_id=1, source_target_pairs={{0,4},{2,6},{4,0},{6,2},{8,12},{10,14},{12,8},{14,10},{16,20},{18,... | collective-permute-start | bytes 1769480 | tf_op jit(solution)/shard_map/ppermute | solution.py:842
  70.1 35.5 %collective-permute-start.8 = (bf16[1,192,1536]{2,1,0:T(8,128)(2,1)}, bf16[1,192,1536]{2,1,0:T(8,128)(2,1)}, u32[]{:S(2)}, u32[]{:S(2)}) collective-permute-start(bf16[1,192,1536]{2,1,0:T(8,128)(2,1)} %dynamic-slice_add_fusion.4.rest_2_), channel_id=1, source_target_pairs={{0,1},{1,0},{2,3},{3,2},{4,5},{5,4},{6,7},{7,6},{8,9},{9,8},{10,11... | collective-permute-start | bytes 1769480 | tf_op jit(solution)/shard_map/ppermute | solution.py:840
  73.9 34.1 %collective-permute-start.9 = (bf16[1,384,768]{2,1,0:T(8,128)(2,1)}, bf16[1,384,768]{2,1,0:T(8,128)(2,1)}, u32[]{:S(2)}, u32[]{:S(2)}) collective-permute-start(bf16[1,384,768]{2,1,0:T(8,128)(2,1)} %dynamic-slice_add_fusion.3.rest_3_), channel_id=1, source_target_pairs={{0,1},{1,0},{2,3},{3,2},{4,5},{5,4},{6,7},{7,6},{8,9},{9,8},{10,11... | collective-permute-start | bytes 1769480 | tf_op jit(solution)/shard_map/ppermute | solution.py:840
  75.0 36.2 %collective-permute-start.6 = (bf16[2,1,192,1536]{3,2,1,0:T(8,128)(2,1)}, bf16[2,1,192,1536]{3,2,1,0:T(8,128)(2,1)}, u32[]{:S(2)}, u32[]{:S(2)}) collective-permute-start(bf16[2,1,192,1536]{3,2,1,0:T(8,128)(2,1)} %maximum_add_fusion.rest_0_.in_near_ref), channel_id=1, source_target_pairs={{0,2},{2,0},{4,6},{6,4},{8,10},{10,8},{12,14},{14,12},{16,18},{18,... | collective-permute-start | bytes 3538952 | tf_op jit(solution)/shard_map/ppermute | solution.py:842
  79.1 32.4 %collective-permute-start.7 = (bf16[2,1,384,768]{3,2,1,0:T(8,128)(2,1)}, bf16[2,1,384,768]{3,2,1,0:T(8,128)(2,1)}, u32[]{:S(2)}, u32[]{:S(2)}) collective-permute-start(bf16[2,1,384,768]{3,2,1,0:T(8,128)(2,1)} %maximum_add_fusion.1.rest_1_.out_near_ref), channel_id=1, source_target_pairs={{0,2},{2,0},{4,6},{6,4},{8,10},{10,8},{12,14},{14,12},{16,18},{18,... | collective-permute-start | bytes 3538952 | tf_op jit(solution)/shard_map/ppermute | solution.py:842
  104.7 35.3 %collective-permute-start.13 = (bf16[1,384,768]{2,1,0:T(8,128)(2,1)}, bf16[1,384,768]{2,1,0:T(8,128)(2,1)}, u32[]{:S(2)}, u32[]{:S(2)}) collective-permute-start(bf16[1,384,768]{2,1,0:T(8,128)(2,1)} %dynamic-slice_add_fusion.1.rest_3_), channel_id=1, source_target_pairs={{0,1},{1,0},{2,3},{3,2},{4,5},{5,4},{6,7},{7,6},{8,9},{9,8},{10,11... | collective-permute-start | bytes 1769480 | tf_op jit(solution)/shard_map/ppermute | solution.py:840
  105.6 31.2 %collective-permute-start.12 = (bf16[1,192,1536]{2,1,0:T(8,128)(2,1)}, bf16[1,192,1536]{2,1,0:T(8,128)(2,1)}, u32[]{:S(2)}, u32[]{:S(2)}) collective-permute-start(bf16[1,192,1536]{2,1,0:T(8,128)(2,1)} %dynamic-slice_add_fusion.2.rest_2_), channel_id=1, source_target_pairs={{0,1},{1,0},{2,3},{3,2},{4,5},{5,4},{6,7},{7,6},{8,9},{9,8},{10,11... | collective-permute-start | bytes 1769480 | tf_op jit(solution)/shard_map/ppermute | solution.py:840
  108.0 36.2 %collective-permute-start.10 = (bf16[1,192,1536]{2,1,0:T(8,128)(2,1)}, bf16[1,192,1536]{2,1,0:T(8,128)(2,1)}, u32[]{:S(2)}, u32[]{:S(2)}) collective-permute-start(bf16[1,192,1536]{2,1,0:T(8,128)(2,1)} %broadcast_add_fusion.4.rest_0_), channel_id=1, source_target_pairs={{0,4},{2,6},{4,0},{6,2},{8,12},{10,14},{12,8},{14,10},{16,20},{18,... | collective-permute-start | bytes 1769480 | tf_op jit(solution)/shard_map/ppermute | solution.py:842
  111.2 37.8 %collective-permute-start.11 = (bf16[1,384,768]{2,1,0:T(8,128)(2,1)}, bf16[1,384,768]{2,1,0:T(8,128)(2,1)}, u32[]{:S(2)}, u32[]{:S(2)}) collective-permute-start(bf16[1,384,768]{2,1,0:T(8,128)(2,1)} %broadcast_add_fusion.3.rest_1_), channel_id=1, source_target_pairs={{0,4},{2,6},{4,0},{6,2},{8,12},{10,14},{12,8},{14,10},{16,20},{18,... | collective-permute-start | bytes 1769480 | tf_op jit(solution)/shard_map/ppermute | solution.py:842
  138.7 53.8 %collective-permute-start.16 = (bf16[1,192,1536]{2,1,0:T(8,128)(2,1)}, bf16[1,192,1536]{2,1,0:T(8,128)(2,1)}, u32[]{:S(2)}, u32[]{:S(2)}) collective-permute-start(bf16[1,192,1536]{2,1,0:T(8,128)(2,1)} %broadcast_add_fusion.2.rest_2_), channel_id=1, source_target_pairs={{0,4},{2,6},{4,0},{6,2},{8,12},{10,14},{12,8},{14,10},{16,20},{18,... | collective-permute-start | bytes 1769480 | tf_op jit(solution)/shard_map/ppermute | solution.py:842
  141.8 53.5 %collective-permute-start.17 = (bf16[1,384,768]{2,1,0:T(8,128)(2,1)}, bf16[1,384,768]{2,1,0:T(8,128)(2,1)}, u32[]{:S(2)}, u32[]{:S(2)}) collective-permute-start(bf16[1,384,768]{2,1,0:T(8,128)(2,1)} %broadcast_add_fusion.1.rest_3_), channel_id=1, source_target_pairs={{0,4},{2,6},{4,0},{6,2},{8,12},{10,14},{12,8},{14,10},{16,20},{18,... | collective-permute-start | bytes 1769480 | tf_op jit(solution)/shard_map/ppermute | solution.py:842
  143.3 98.8 %collective-permute-start.20 = (bf16[1408,384]{1,0:T(8,128)(2,1)}, bf16[1408,384]{1,0:T(8,128)(2,1)}, u32[]{:S(2)}, u32[]{:S(2)}) collective-permute-start(bf16[1408,384]{1,0:T(8,128)(2,1)} %maximum_add_fusion.7.rest_4_), channel_id=1, source_target_pairs={{0,1},{1,0},{2,3},{3,2},{4,5},{5,4},{6,7},{7,6},{8,9},{9,8},{10,11... | collective-permute-start | bytes 3244040 | tf_op jit(solution)/shard_map/ppermute | solution.py:840
  146.6 20.1 %collective-permute-start.14 = (bf16[2,1,192,1536]{3,2,1,0:T(8,128)(2,1)}, bf16[2,1,192,1536]{3,2,1,0:T(8,128)(2,1)}, u32[]{:S(2)}, u32[]{:S(2)}) collective-permute-start(bf16[2,1,192,1536]{3,2,1,0:T(8,128)(2,1)} %maximum_add_fusion.2.rest_0_.in_near_ref), channel_id=1, source_target_pairs={{0,2},{2,0},{4,6},{6,4},{8,10},{10,8},{12,14},{14,12},{16,18},{18,... | collective-permute-start | bytes 3538952 | tf_op jit(solution)/shard_map/ppermute | solution.py:842
  151.4 15.3 %collective-permute-start.15 = (bf16[2,1,384,768]{3,2,1,0:T(8,128)(2,1)}, bf16[2,1,384,768]{3,2,1,0:T(8,128)(2,1)}, u32[]{:S(2)}, u32[]{:S(2)}) collective-permute-start(bf16[2,1,384,768]{3,2,1,0:T(8,128)(2,1)} %maximum_add_fusion.3.rest_1_.out_near_ref), channel_id=1, source_target_pairs={{0,2},{2,0},{4,6},{6,4},{8,10},{10,8},{12,14},{14,12},{16,18},{18,... | collective-permute-start | bytes 3538952 | tf_op jit(solution)/shard_map/ppermute | solution.py:842
  194.8 17.7 %collective-permute-start.18 = (bf16[2,1,192,1536]{3,2,1,0:T(8,128)(2,1)}, bf16[2,1,192,1536]{3,2,1,0:T(8,128)(2,1)}, u32[]{:S(2)}, u32[]{:S(2)}) collective-permute-start(bf16[2,1,192,1536]{3,2,1,0:T(8,128)(2,1)} %maximum_add_fusion.4.rest_0_.in_near_ref), channel_id=1, source_target_pairs={{0,2},{2,0},{4,6},{6,4},{8,10},{10,8},{12,14},{14,12},{16,18},{18,... | collective-permute-start | bytes 3538952 | tf_op jit(solution)/shard_map/ppermute | solution.py:842
  197.7 14.8 %collective-permute-start.19 = (bf16[2,1,384,768]{3,2,1,0:T(8,128)(2,1)}, bf16[2,1,384,768]{3,2,1,0:T(8,128)(2,1)}, u32[]{:S(2)}, u32[]{:S(2)}) collective-permute-start(bf16[2,1,384,768]{3,2,1,0:T(8,128)(2,1)} %maximum_add_fusion.5.rest_1_.out_near_ref), channel_id=1, source_target_pairs={{0,2},{2,0},{4,6},{6,4},{8,10},{10,8},{12,14},{14,12},{16,18},{18,... | collective-permute-start | bytes 3538952 | tf_op jit(solution)/shard_map/ppermute | solution.py:842
  250.5 27.5 %collective-permute-start.21 = (bf16[1408,384]{1,0:T(8,128)(2,1)}, bf16[1408,384]{1,0:T(8,128)(2,1)}, u32[]{:S(2)}, u32[]{:S(2)}) collective-permute-start(bf16[1408,384]{1,0:T(8,128)(2,1)} %dynamic-slice_add_fusion.rest_0_), channel_id=1, source_target_pairs={{0,1},{1,0},{2,3},{3,2},{4,5},{5,4},{6,7},{7,6},{8,9},{9,8},{10,11... | collective-permute-start | bytes 3244040 | tf_op jit(solution)/shard_map/ppermute | solution.py:840
  277.2 27.5 %collective-permute-start.22 = (bf16[2,2,8,96,768]{4,3,2,1,0:T(8,128)(2,1)}, bf16[2,2,8,96,768]{4,3,2,1,0:T(8,128)(2,1)}, u32[]{:S(2)}, u32[]{:S(2)}) collective-permute-start(bf16[2,2,8,96,768]{4,3,2,1,0:T(8,128)(2,1)} %get-tuple-element.167.rest_2_), channel_id=1, source_target_pairs={{0,2},{2,0},{4,6},{6,4},{8,10},{10,8},{12,14},{14,12},{16,18},{18,... | collective-permute-start | bytes 14155784 | tf_op jit(solution)/shard_map/ppermute | solution.py:842
  309.9 29.0 %collective-permute-start.23 = (bf16[2,4,96,768]{3,2,1,0:T(8,128)(2,1)}, bf16[2,4,96,768]{3,2,1,0:T(8,128)(2,1)}, u32[]{:S(2)}, u32[]{:S(2)}) collective-permute-start(bf16[2,4,96,768]{3,2,1,0:T(8,128)(2,1)} %get-tuple-element.287.rest_0_), channel_id=1, source_target_pairs={{0,1},{1,0},{2,3},{3,2},{4,5},{5,4},{6,7},{7,6},{8,9},{9,8},{10,11... | collective-permute-start | bytes 3538952 | tf_op jit(solution)/shard_map/ppermute | solution.py:840
  337.9 32.9 %collective-permute-start.24 = (bf16[4,2,56,768]{3,2,0,1:T(8,128)(2,1)}, bf16[4,2,56,768]{3,2,0,1:T(8,128)(2,1)}, u32[]{:S(2)}, u32[]{:S(2)}) collective-permute-start(bf16[4,2,56,768]{3,2,0,1:T(8,128)(2,1)} %fusion.45), channel_id=1, source_target_pairs={{0,2},{2,0},{4,6},{6,4},{8,10},{10,8},{12,14},{14,12},{16,18},{18,... | collective-permute-start | bytes 2064392 | tf_op jit(solution)/shard_map/ppermute | solution.py:842
  338.3 36.7 %collective-permute-start.25 = (bf16[2,4,96,768]{3,2,1,0:T(8,128)(2,1)}, bf16[2,4,96,768]{3,2,1,0:T(8,128)(2,1)}, u32[]{:S(2)}, u32[]{:S(2)}) collective-permute-start(bf16[2,4,96,768]{3,2,1,0:T(8,128)(2,1)} %get-tuple-element.286.rest_1_), channel_id=1, source_target_pairs={{0,1},{1,0},{2,3},{3,2},{4,5},{5,4},{6,7},{7,6},{8,9},{9,8},{10,11... | collective-permute-start | bytes 3538952 | tf_op jit(solution)/shard_map/ppermute | solution.py:840
  343.7 31.2 %collective-permute-start.26 = (bf16[2,4,96,768]{3,2,1,0:T(8,128)(2,1)}, bf16[2,4,96,768]{3,2,1,0:T(8,128)(2,1)}, u32[]{:S(2)}, u32[]{:S(2)}) collective-permute-start(bf16[2,4,96,768]{3,2,1,0:T(8,128)(2,1)} %fusion.10.rest_2_), channel_id=1, source_target_pairs={{0,4},{2,6},{4,0},{6,2},{8,12},{10,14},{12,8},{14,10},{16,20},{18,... | collective-permute-start | bytes 3538952 | tf_op jit(solution)/shard_map/ppermute | solution.py:842
  373.7 38.4 %collective-permute-start.27 = (bf16[4,56,768]{2,1,0:T(8,128)(2,1)}, bf16[4,56,768]{2,1,0:T(8,128)(2,1)}, u32[]{:S(2)}, u32[]{:S(2)}) collective-permute-start(bf16[4,56,768]{2,1,0:T(8,128)(2,1)} %dynamic-slice_bitcast_fusion.8.rest_1_), channel_id=1, source_target_pairs={{0,4},{2,6},{4,0},{6,2},{8,12},{10,14},{12,8},{14,10},{16,20},{18,... | collective-permute-start | bytes 1032200 | tf_op jit(solution)/shard_map/ppermute | solution.py:842
  373.9 43.8 %collective-permute-start.28 = (bf16[2,2,8,96,768]{4,3,2,1,0:T(8,128)(2,1)}, bf16[2,2,8,96,768]{4,3,2,1,0:T(8,128)(2,1)}, u32[]{:S(2)}, u32[]{:S(2)}) collective-permute-start(bf16[2,2,8,96,768]{4,3,2,1,0:T(8,128)(2,1)} %get-tuple-element.198.rest_5_), channel_id=1, source_target_pairs={{0,2},{2,0},{4,6},{6,4},{8,10},{10,8},{12,14},{14,12},{16,18},{18,... | collective-permute-start | bytes 14155784 | tf_op jit(solution)/shard_map/ppermute | solution.py:842
  381.2 34.3 %collective-permute-start.48 = (bf16[192,768]{1,0:T(8,128)(2,1)}, bf16[192,768]{1,0:T(8,128)(2,1)}, u32[]{:S(2)}, u32[]{:S(2)}) collective-permute-start(bf16[192,768]{1,0:T(8,128)(2,1)} %get-tuple-element.310.rest_4_), channel_id=1, source_target_pairs={{0,24},{2,26},{4,28},{6,30},{8,16},{10,18},{12,20},{14,22},{16,8},... | collective-permute-start | bytes 884744 | tf_op jit(solution)/shard_map/ppermute | solution.py:842
  384.5 31.0 %collective-permute-start.46 = (bf16[192,768]{1,0:T(8,128)(2,1)}, bf16[192,768]{1,0:T(8,128)(2,1)}, u32[]{:S(2)}, u32[]{:S(2)}) collective-permute-start(bf16[192,768]{1,0:T(8,128)(2,1)} %get-tuple-element.311.rest_2_), channel_id=1, source_target_pairs={{0,8},{2,10},{4,12},{6,14},{8,0},{10,2},{12,4},{14,6},{16,24},{18,... | collective-permute-start | bytes 884744 | tf_op jit(solution)/shard_map/ppermute | solution.py:842
  384.5 31.0 %collective-permute-start.47 = (bf16[192,768]{1,0:T(8,128)(2,1)}, bf16[192,768]{1,0:T(8,128)(2,1)}, u32[]{:S(2)}, u32[]{:S(2)}) collective-permute-start(bf16[192,768]{1,0:T(8,128)(2,1)} %get-tuple-element.312.rest_3_), channel_id=1, source_target_pairs={{0,16},{2,18},{4,20},{6,22},{8,24},{10,26},{12,28},{14,30},{16,0},... | collective-permute-start | bytes 884744 | tf_op jit(solution)/shard_map/ppermute | solution.py:842
  414.7 40.0 %collective-permute-start.33 = (bf16[4,56,768]{2,1,0:T(8,128)(2,1)}, bf16[4,56,768]{2,1,0:T(8,128)(2,1)}, u32[]{:S(2)}, u32[]{:S(2)}) collective-permute-start(bf16[4,56,768]{2,1,0:T(8,128)(2,1)} %fusion.51.rest_0_), channel_id=1, source_target_pairs={{0,1},{1,0},{2,3},{3,2},{4,5},{5,4},{6,7},{7,6},{8,9},{9,8},{10,11... | collective-permute-start | bytes 1032200 | tf_op jit(solution)/shard_map/ppermute | solution.py:840
  417.6 236.4 %all-gather.9.cloned.1.call-start = ((), (), s32[]{:S(2)}) async-start(), calls=%async_computation.1 | async-start | bytes 6475776 | tf_op jit(solution)/shard_map/all_gather | solution.py:1173
  422.9 34.5 %collective-permute-start.29 = (bf16[2,4,96,768]{3,2,1,0:T(8,128)(2,1)}, bf16[2,4,96,768]{3,2,1,0:T(8,128)(2,1)}, u32[]{:S(2)}, u32[]{:S(2)}) collective-permute-start(bf16[2,4,96,768]{3,2,1,0:T(8,128)(2,1)} %get-tuple-element.285.rest_1_), channel_id=1, source_target_pairs={{0,1},{1,0},{2,3},{3,2},{4,5},{5,4},{6,7},{7,6},{8,9},{9,8},{10,11... | collective-permute-start | bytes 3538952 | tf_op jit(solution)/shard_map/ppermute | solution.py:840
  452.7 37.2 %collective-permute-start.30 = (bf16[4,2,56,768]{3,2,0,1:T(8,128)(2,1)}, bf16[4,2,56,768]{3,2,0,1:T(8,128)(2,1)}, u32[]{:S(2)}, u32[]{:S(2)}) collective-permute-start(bf16[4,2,56,768]{3,2,0,1:T(8,128)(2,1)} %fusion.44), channel_id=1, source_target_pairs={{0,2},{2,0},{4,6},{6,4},{8,10},{10,8},{12,14},{14,12},{16,18},{18,... | collective-permute-start | bytes 2064392 | tf_op jit(solution)/shard_map/ppermute | solution.py:842
  453.9 39.8 %collective-permute-start.31 = (bf16[2,4,96,768]{3,2,1,0:T(8,128)(2,1)}, bf16[2,4,96,768]{3,2,1,0:T(8,128)(2,1)}, u32[]{:S(2)}, u32[]{:S(2)}) collective-permute-start(bf16[2,4,96,768]{3,2,1,0:T(8,128)(2,1)} %get-tuple-element.284.rest_1_), channel_id=1, source_target_pairs={{0,1},{1,0},{2,3},{3,2},{4,5},{5,4},{6,7},{7,6},{8,9},{9,8},{10,11... | collective-permute-start | bytes 3538952 | tf_op jit(solution)/shard_map/ppermute | solution.py:840
  462.2 31.5 %collective-permute-start.32 = (bf16[2,4,96,768]{3,2,1,0:T(8,128)(2,1)}, bf16[2,4,96,768]{3,2,1,0:T(8,128)(2,1)}, u32[]{:S(2)}, u32[]{:S(2)}) collective-permute-start(bf16[2,4,96,768]{3,2,1,0:T(8,128)(2,1)} %fusion.5.rest_2_), channel_id=1, source_target_pairs={{0,4},{2,6},{4,0},{6,2},{8,12},{10,14},{12,8},{14,10},{16,20},{18,... | collective-permute-start | bytes 3538952 | tf_op jit(solution)/shard_map/ppermute | solution.py:842
  492.7 39.5 %collective-permute-start.34 = (bf16[4,56,768]{2,1,0:T(8,128)(2,1)}, bf16[4,56,768]{2,1,0:T(8,128)(2,1)}, u32[]{:S(2)}, u32[]{:S(2)}) collective-permute-start(bf16[4,56,768]{2,1,0:T(8,128)(2,1)} %dynamic-slice_bitcast_fusion.7.rest_1_), channel_id=1, source_target_pairs={{0,4},{2,6},{4,0},{6,2},{8,12},{10,14},{12,8},{14,10},{16,20},{18,... | collective-permute-start | bytes 1032200 | tf_op jit(solution)/shard_map/ppermute | solution.py:842
  492.9 46.8 %collective-permute-start.35 = (bf16[2,2,8,96,768]{4,3,2,1,0:T(8,128)(2,1)}, bf16[2,2,8,96,768]{4,3,2,1,0:T(8,128)(2,1)}, u32[]{:S(2)}, u32[]{:S(2)}) collective-permute-start(bf16[2,2,8,96,768]{4,3,2,1,0:T(8,128)(2,1)} %get-tuple-element.229.rest_5_), channel_id=1, source_target_pairs={{0,2},{2,0},{4,6},{6,4},{8,10},{10,8},{12,14},{14,12},{16,18},{18,... | collective-permute-start | bytes 14155784 | tf_op jit(solution)/shard_map/ppermute | solution.py:842
  501.3 33.9 %collective-permute-start.52 = (bf16[248,768]{1,0:T(8,128)(2,1)}, bf16[248,768]{1,0:T(8,128)(2,1)}, u32[]{:S(2)}, u32[]{:S(2)}) collective-permute-start(bf16[248,768]{1,0:T(8,128)(2,1)} %get-tuple-element.295.rest_4_), channel_id=1, source_target_pairs={{0,24},{2,26},{4,28},{6,30},{8,16},{10,18},{12,20},{14,22},{16,8},... | collective-permute-start | bytes 1142792 | tf_op jit(solution)/shard_map/ppermute | solution.py:842
  504.8 32.6 %collective-permute-start.51 = (bf16[248,768]{1,0:T(8,128)(2,1)}, bf16[248,768]{1,0:T(8,128)(2,1)}, u32[]{:S(2)}, u32[]{:S(2)}) collective-permute-start(bf16[248,768]{1,0:T(8,128)(2,1)} %get-tuple-element.296.rest_3_), channel_id=1, source_target_pairs={{0,16},{2,18},{4,20},{6,22},{8,24},{10,26},{12,28},{14,30},{16,0},... | collective-permute-start | bytes 1142792 | tf_op jit(solution)/shard_map/ppermute | solution.py:842
  504.8 32.6 %collective-permute-start.50 = (bf16[248,768]{1,0:T(8,128)(2,1)}, bf16[248,768]{1,0:T(8,128)(2,1)}, u32[]{:S(2)}, u32[]{:S(2)}) collective-permute-start(bf16[248,768]{1,0:T(8,128)(2,1)} %get-tuple-element.297.rest_2_), channel_id=1, source_target_pairs={{0,8},{2,10},{4,12},{6,14},{8,0},{10,2},{12,4},{14,6},{16,24},{18,... | collective-permute-start | bytes 1142792 | tf_op jit(solution)/shard_map/ppermute | solution.py:842
  534.6 54.8 %collective-permute-start.42 = (bf16[4,56,768]{2,1,0:T(8,128)(2,1)}, bf16[4,56,768]{2,1,0:T(8,128)(2,1)}, u32[]{:S(2)}, u32[]{:S(2)}) collective-permute-start(bf16[4,56,768]{2,1,0:T(8,128)(2,1)} %fusion.49.rest_0_), channel_id=1, source_target_pairs={{0,1},{1,0},{2,3},{3,2},{4,5},{5,4},{6,7},{7,6},{8,9},{9,8},{10,11... | collective-permute-start | bytes 1032200 | tf_op jit(solution)/shard_map/ppermute | solution.py:840
  539.7 210.9 %all-gather.11.cloned.1.call-start = ((), (), s32[]{:S(2)}) async-start(), calls=%async_computation.2 | async-start | bytes 6475776 | tf_op jit(solution)/shard_map/all_gather | solution.py:1173
  543.4 30.5 %collective-permute-start.37 = (bf16[8,96,768]{2,1,0:T(8,128)(2,1)}, bf16[8,96,768]{2,1,0:T(8,128)(2,1)}, u32[]{:S(2)}, u32[]{:S(2)}) collective-permute-start(bf16[8,96,768]{2,1,0:T(8,128)(2,1)} %fusion.25.rest_1_), channel_id=1, source_target_pairs={{0,1},{1,0},{2,3},{3,2},{4,5},{5,4},{6,7},{7,6},{8,9},{9,8},{10,11... | collective-permute-start | bytes 3538952 | tf_op jit(solution)/shard_map/ppermute | solution.py:840
  547.6 37.1 %collective-permute-start.39 = (bf16[2,4,96,768]{3,2,1,0:T(8,128)(2,1)}, bf16[2,4,96,768]{3,2,1,0:T(8,128)(2,1)}, u32[]{:S(2)}, u32[]{:S(2)}) collective-permute-start(bf16[2,4,96,768]{3,2,1,0:T(8,128)(2,1)} %fusion.26.rest_2_), channel_id=1, source_target_pairs={{0,4},{2,6},{4,0},{6,2},{8,12},{10,14},{12,8},{14,10},{16,20},{18,... | collective-permute-start | bytes 3538952 | tf_op jit(solution)/shard_map/ppermute | solution.py:842
  572.2 19.2 %collective-permute-start.36 = (bf16[4,2,56,768]{3,2,0,1:T(8,128)(2,1)S(1)}, bf16[4,2,56,768]{3,2,0,1:T(8,128)(2,1)S(1)}, u32[]{:S(2)}, u32[]{:S(2)}) collective-permute-start(bf16[4,2,56,768]{3,2,0,1:T(8,128)(2,1)S(1)} %fusion.43), channel_id=1, source_target_pairs={{0,2},{2,0},{4,6},{6,4},{8,10},{10,8},{12,14},{14,12},{16,18},{18,... | collective-permute-start | bytes 2064392 | tf_op jit(solution)/shard_map/ppermute | solution.py:842
  588.1 12.9 %collective-permute-start.40 = (bf16[4,96,768]{2,1,0:T(8,128)(2,1)S(1)}, bf16[4,96,768]{2,1,0:T(8,128)(2,1)S(1)}, u32[]{:S(2)}, u32[]{:S(2)}) collective-permute-start(bf16[4,96,768]{2,1,0:T(8,128)(2,1)S(1)} %get-tuple-element.282), channel_id=1, source_target_pairs={{0,1},{1,0},{2,3},{3,2},{4,5},{5,4},{6,7},{7,6},{8,9},{9,8},{10,11... | collective-permute-start | bytes 1769480 | tf_op jit(solution)/shard_map/ppermute | solution.py:840
  589.3 18.6 %collective-permute-start.38 = (bf16[4,96,768]{2,1,0:T(8,128)(2,1)S(1)}, bf16[4,96,768]{2,1,0:T(8,128)(2,1)S(1)}, u32[]{:S(2)}, u32[]{:S(2)}) collective-permute-start(bf16[4,96,768]{2,1,0:T(8,128)(2,1)S(1)} %get-tuple-element.283), channel_id=1, source_target_pairs={{0,4},{2,6},{4,0},{6,2},{8,12},{10,14},{12,8},{14,10},{16,20},{18,... | collective-permute-start | bytes 1769480 | tf_op jit(solution)/shard_map/ppermute | solution.py:842
  615.1 13.8 %collective-permute-start.45 = (bf16[248,768]{1,0:T(8,128)(2,1)}, bf16[248,768]{1,0:T(8,128)(2,1)S(1)}, u32[]{:S(2)}, u32[]{:S(2)}) collective-permute-start(bf16[248,768]{1,0:T(8,128)(2,1)} %get-tuple-element.292), channel_id=1, source_target_pairs={{0,24},{2,26},{4,28},{6,30},{8,16},{10,18},{12,20},{14,22},{16,8},... | collective-permute-start | bytes 1142792 | tf_op jit(solution)/shard_map/ppermute | solution.py:842
  617.2 30.1 %collective-permute-start.44 = (bf16[248,768]{1,0:T(8,128)(2,1)}, bf16[248,768]{1,0:T(8,128)(2,1)S(1)}, u32[]{:S(2)}, u32[]{:S(2)}) collective-permute-start(bf16[248,768]{1,0:T(8,128)(2,1)} %get-tuple-element.293), channel_id=1, source_target_pairs={{0,16},{2,18},{4,20},{6,22},{8,24},{10,26},{12,28},{14,30},{16,0},... | collective-permute-start | bytes 1142792 | tf_op jit(solution)/shard_map/ppermute | solution.py:842
  617.2 30.1 %collective-permute-start.43 = (bf16[248,768]{1,0:T(8,128)(2,1)S(1)}, bf16[248,768]{1,0:T(8,128)(2,1)S(1)}, u32[]{:S(2)}, u32[]{:S(2)}) collective-permute-start(bf16[248,768]{1,0:T(8,128)(2,1)S(1)} %get-tuple-element.294), channel_id=1, source_target_pairs={{0,8},{2,10},{4,12},{6,14},{8,0},{10,2},{12,4},{14,6},{16,24},{18,... | collective-permute-start | bytes 1142792 | tf_op jit(solution)/shard_map/ppermute | solution.py:842
  621.1 7.8 %collective-permute-start.41 = (bf16[4,56,768]{2,1,0:T(8,128)(2,1)}, bf16[4,56,768]{2,1,0:T(8,128)(2,1)S(1)}, u32[]{:S(2)}, u32[]{:S(2)}) collective-permute-start(bf16[4,56,768]{2,1,0:T(8,128)(2,1)} %dynamic-slice_bitcast_fusion.6), channel_id=1, source_target_pairs={{0,4},{2,6},{4,0},{6,2},{8,12},{10,14},{12,8},{14,10},{16,20},{18,... | collective-permute-start | bytes 1032200 | tf_op jit(solution)/shard_map/ppermute | solution.py:842
  653.1 8.0 %collective-permute-start.49 = (bf16[4,56,768]{2,1,0:T(8,128)(2,1)S(1)}, bf16[4,56,768]{2,1,0:T(8,128)(2,1)S(1)}, u32[]{:S(2)}, u32[]{:S(2)}) collective-permute-start(bf16[4,56,768]{2,1,0:T(8,128)(2,1)S(1)} %fusion.47), channel_id=1, source_target_pairs={{0,1},{1,0},{2,3},{3,2},{4,5},{5,4},{6,7},{7,6},{8,9},{9,8},{10,11... | collective-permute-start | bytes 1032200 | tf_op jit(solution)/shard_map/ppermute | solution.py:840
  665.5 22.6 %collective-permute-start.56 = (bf16[1408,384]{1,0:T(8,128)(2,1)S(1)}, bf16[1408,384]{1,0:T(8,128)(2,1)S(1)}, u32[]{:S(2)}, u32[]{:S(2)}) collective-permute-start(bf16[1408,384]{1,0:T(8,128)(2,1)S(1)} %fusion.35), channel_id=1, source_target_pairs={{0,1},{1,0},{2,3},{3,2},{4,5},{5,4},{6,7},{7,6},{8,9},{9,8},{10,11... | collective-permute-start | bytes 3244040 | tf_op jit(solution)/shard_map/ppermute | solution.py:840
  667.0 7.9 %collective-permute-start.53 = (bf16[56,768]{1,0:T(8,128)(2,1)S(1)}, bf16[56,768]{1,0:T(8,128)(2,1)S(1)}, u32[]{:S(2)}, u32[]{:S(2)}) collective-permute-start(bf16[56,768]{1,0:T(8,128)(2,1)S(1)} %get-tuple-element.319), channel_id=1, source_target_pairs={{0,8},{2,10},{4,12},{6,14},{8,0},{10,2},{12,4},{14,6},{16,24},{18,... | collective-permute-start | bytes 258056 | tf_op jit(solution)/shard_map/ppermute | solution.py:842
  667.0 9.7 %collective-permute-start.55 = (bf16[56,768]{1,0:T(8,128)(2,1)S(1)}, bf16[56,768]{1,0:T(8,128)(2,1)S(1)}, u32[]{:S(2)}, u32[]{:S(2)}) collective-permute-start(bf16[56,768]{1,0:T(8,128)(2,1)S(1)} %get-tuple-element.320), channel_id=1, source_target_pairs={{0,24},{2,26},{4,28},{6,30},{8,16},{10,18},{12,20},{14,22},{16,8},... | collective-permute-start | bytes 258056 | tf_op jit(solution)/shard_map/ppermute | solution.py:842
  669.5 15.3 %collective-permute-start.54 = (bf16[56,768]{1,0:T(8,128)(2,1)S(1)}, bf16[56,768]{1,0:T(8,128)(2,1)S(1)}, u32[]{:S(2)}, u32[]{:S(2)}) collective-permute-start(bf16[56,768]{1,0:T(8,128)(2,1)S(1)} %get-tuple-element.321), channel_id=1, source_target_pairs={{0,16},{2,18},{4,20},{6,22},{8,24},{10,26},{12,28},{14,30},{16,0},... | collective-permute-start | bytes 258056 | tf_op jit(solution)/shard_map/ppermute | solution.py:842
  691.3 7.1 collective-permute-start.59
  693.4 15.1 %collective-permute-start.58 = (bf16[56,768]{1,0:T(8,128)(2,1)S(1)}, bf16[56,768]{1,0:T(8,128)(2,1)S(1)}, u32[]{:S(2)}, u32[]{:S(2)}) collective-permute-start(bf16[56,768]{1,0:T(8,128)(2,1)S(1)} %fusion.69), channel_id=1, source_target_pairs={{0,16},{2,18},{4,20},{6,22},{8,24},{10,26},{12,28},{14,30},{16,0},... | collective-permute-start | bytes 258056 | tf_op jit(solution)/shard_map/ppermute | solution.py:842
  693.4 15.1 %collective-permute-start.57 = (bf16[56,768]{1,0:T(8,128)(2,1)S(1)}, bf16[56,768]{1,0:T(8,128)(2,1)S(1)}, u32[]{:S(2)}, u32[]{:S(2)}) collective-permute-start(bf16[56,768]{1,0:T(8,128)(2,1)S(1)} %fusion.69), channel_id=1, source_target_pairs={{0,8},{2,10},{4,12},{6,14},{8,0},{10,2},{12,4},{14,6},{16,24},{18,... | collective-permute-start | bytes 258056 | tf_op jit(solution)/shard_map/ppermute | solution.py:842
  712.0 6.6 collective-permute-start.60
  721.7 12.0 %collective-permute-start.61 = (bf16[4,2,56,768]{3,2,1,0:T(8,128)(2,1)S(1)}, bf16[4,2,56,768]{3,2,1,0:T(8,128)(2,1)S(1)}, u32[]{:S(2)}, u32[]{:S(2)}) collective-permute-start(bf16[4,2,56,768]{3,2,1,0:T(8,128)(2,1)S(1)} %copy.91), channel_id=1, source_target_pairs={{0,2},{2,0},{4,6},{6,4},{8,10},{10,8},{12,14},{14,12},{16,18},{18,... | collective-permute-start | bytes 2064392 | tf_op jit(solution)/shard_map/ppermute | solution.py:842
  (82 other events, 485.3 us)
Sparse Core Ops, SparseCore 0:
  417.8 54.7 all-gather.6
  539.8 73.7 all-gather.8
  652.4 74.0 all-gather.10

commit v3 on v2

--- a/solution.py
+++ b/solution.py
@@ -1234,8 +1234,8 @@
             also = [mark]
         if any(flow["got"] for flow in line.flows):
             line.arrived(*also)
-    outs = to_features(features(out, side), line.gate(out_found[0]))
-    grads = to_features(features(grad, side), line.gate(grad_found[0].astype(F32)))
+    outs = to_features(features(out, side), out_found[0])
+    grads = to_features(features(grad, side), grad_found[0].astype(F32))
     while done:
         done -= 1
         *chan_grads, _ = assemble(gathered[done], places, done, layers, block, tuple(chan_grads))

time: 782 us -> 767 us (0.981)
  waiting for transfers between devices: 109 us -> 85.5 us
  starting transfers between devices: 59.2 us -> 70.1 us
    ppermute x42, starting transfers between devices: 43 us -> 56.1 us  [exchange(): return lax.ppermute(value, 'dp', [(i, i ^ mask) for i in range(count)])]
    ppermute x42, waiting for transfers between devices: 72.6 us -> 59.8 us  [exchange(): return lax.ppermute(value, 'dp', [(i, i ^ mask) for i in range(count)])]
    ppermute x20, waiting for transfers between devices: 36 us -> 25.6 us  [exchange(): return lax.ppermute(value, 'mp', [(0, 1), (1, 0)])]
    add x31 -> x29, other arithmetic: 44.3 us -> 41.4 us  [gate(): value + self.zero().astype(value.dtype)]
    unnamed x194 -> x188, local copies, waits for them, and re-layouts: 21.4 us -> 20.2 us
  transfers between devices with their start and end apart: 65 -> 65, of which waited for: 15 -> 9; matrix products, arithmetic and copies ran while one was open for 22% -> 22% of each run, Pallas kernels for 47% -> 48%
where the time goes in v3:
time: 767 us; the launch traced here: 759 us
  Pallas kernels  377 us (49%)
  other arithmetic  133 us (17%)
  waiting for transfers between devices  85.5 us (11%)
  starting transfers between devices  70.1 us (9%)
  local copies, waits for them, and re-layouts  68.1 us (9%)
  between operations  25 us (3%)
    pallas_call x6, Pallas kernels, chan_backward(): kernel_call(functools.partial(chan_backward_kernel, blocks, halves), (2 *...  159 us
    pallas_call x3, Pallas kernels, chan_forward(): kernel_call(functools.partial(chan_forward_kernel, part), (count // tile,...  74.7 us
    convert_element_type x21, other arithmetic, add(): return (total + self.zero()).astype(B16)  64 us
    pallas_call x6, Pallas kernels, token_backward(): kernel_call(token_backward_kernel, (images,), [placed, placed, block(patc...  62.1 us
    ppermute x42, waiting for transfers between devices, exchange(): return lax.ppermute(value, 'dp', [(i, i ^ mask) for i in range(count)])  59.8 us
    ppermute x42, starting transfers between devices, exchange(): return lax.ppermute(value, 'dp', [(i, i ^ mask) for i in range(count)])  56.1 us
    pallas_call x6, Pallas kernels, token_forward(): kernel_call(token_forward_kernel, (images,), [placed] + [layer_spec(a, po...  44.6 us
    add x29, other arithmetic, gate(): value + self.zero().astype(value.dtype)  41.4 us
  transfers between devices with their start and end apart: 65, of which 9 were waited for; matrix products, arithmetic and copies ran while one was open for 22% of the time, Pallas kernels for 48%

profile of v3, /device:TPU:1, one launch (start us, length us, event | category | flops | bytes accessed | tf_op | source)
XLA Modules:
  0.0 759.4 jit_solution(12844555402247958599)
XLA Ops:
  13.1 4.5 constant_dynamic-slice_fusion.18
  31.7 5.4 collective-permute-done.1.refs_1_
  45.8 20.1 %collective-permute-done.3 = f32[3,3456]{1,0:T(4,128)S(1)} collective-permute-done((f32[3,3456]{1,0:T(4,128)S(1)}, f32[3,3456]{1,0:T(4,128)S(1)}, u32[]{:S(2)}, u32[]{:S(2)}) %collective-permute-start.3) | collective-permute-done | bytes 41504 | tf_op jit(solution)/shard_map/ppermute | solution.py:840
  82.8 5.3 shard_map.323
  88.2 8.7 %shard_map.325 = (f32[1408,768]{1,0:T(8,128)}, bf16[1408,768]{1,0:T(8,128)(2,1)}, bf16[832,768]{1,0:T(8,128)(2,1)}, bf16[1536,768]{1,0:T(8,128)(2,1)}, bf16[1536...) custom-call(f32[1408,768]{1,0:T(8,128)} %get-tuple-element.140.x_ref, ...), custom_call_target="tpu_custom_call" | custom-call | flops 196293427200 | bytes 3833856000 | tf_op jit(solution)/shard_map/pallas_call | solution.py:459
  96.8 6.0 shard_map.326
  114.3 24.5 %shard_map.327 = (bf16[1408,3072]{1,0:T(8,128)(2,1)}, bf16[1408,3072]{1,0:T(8,128)(2,1)}, f32[1408,768]{1,0:T(8,128)}, bf16[768,1536]{1,0:T(8,128)(2,1)}, bf16[1536,768]{1,0:T(8,128)(2,1)}, /*index=5*/f32[1,1]{1,0:T(1,128)}) custom-call(s32[4]{0:T(128)} %pad_add_fusion.info_ref, bf16[1408,768]{1,0:T(8,128)(2,1)} %get-tuple-element.143.rows_ref, ...), custom_call_target="tpu_custom_call" | custom-call | flops 2657511014400 | bytes 5622988800 | tf_op jit(solution)/shard_map/pallas_call | solution.py:570
  139.5 2.4 maximum_add_fusion.2.rest_0_.in_near_ref
  144.0 2.4 maximum_add_fusion.3.rest_1_.out_near_ref
  154.2 9.1 %shard_map.328 = (f32[1408,768]{1,0:T(8,128)}, bf16[1408,768]{1,0:T(8,128)(2,1)}, bf16[832,768]{1,0:T(8,128)(2,1)}, bf16[1536,768]{1,0:T(8,128)(2,1)}, bf16[1536...) custom-call(f32[1408,768]{1,0:T(8,128)} %get-tuple-element.146.x_ref, ...), custom_call_target="tpu_custom_call" | custom-call | flops 196293427200 | bytes 3833856000 | tf_op jit(solution)/shard_map/pallas_call | solution.py:459
  163.4 6.0 shard_map.329
  169.4 25.1 %shard_map.330 = (bf16[1408,3072]{1,0:T(8,128)(2,1)}, bf16[1408,3072]{1,0:T(8,128)(2,1)}, f32[1408,768]{1,0:T(8,128)}, bf16[768,1536]{1,0:T(8,128)(2,1)}, bf16[1536,768]{1,0:T(8,128)(2,1)}, /*index=5*/f32[1,1]{1,0:T(1,128)}) custom-call(s32[4]{0:T(128)} %pad_add_fusion.info_ref, bf16[1408,768]{1,0:T(8,128)(2,1)} %get-tuple-element.150.rows_ref, ...), custom_call_target="tpu_custom_call" | custom-call | flops 2657511014400 | bytes 5622988800 | tf_op jit(solution)/shard_map/pallas_call | solution.py:570
  195.1 2.4 maximum_add_fusion.4.rest_0_.in_near_ref
  198.8 2.4 maximum_add_fusion.5.rest_1_.out_near_ref
  201.2 8.7 %shard_map.331 = (f32[1408,768]{1,0:T(8,128)}, bf16[1408,768]{1,0:T(8,128)(2,1)}, bf16[832,768]{1,0:T(8,128)(2,1)}, bf16[1536,768]{1,0:T(8,128)(2,1)}, bf16[1536...) custom-call(f32[1408,768]{1,0:T(8,128)} %get-tuple-element.152.x_ref, ...), custom_call_target="tpu_custom_call" | custom-call | flops 196293427200 | bytes 3833856000 | tf_op jit(solution)/shard_map/pallas_call | solution.py:459
  209.8 6.1 shard_map.332
  215.9 25.1 %shard_map.333 = (bf16[1408,3072]{1,0:T(8,128)(2,1)}, bf16[1408,3072]{1,0:T(8,128)(2,1)}, f32[1408,768]{1,0:T(8,128)}, bf16[768,1536]{1,0:T(8,128)(2,1)}, bf16[1536,768]{1,0:T(8,128)(2,1)}, /*index=5*/f32[1,1]{1,0:T(1,128)}) custom-call(s32[4]{0:T(128)} %pad_add_fusion.info_ref, bf16[1408,768]{1,0:T(8,128)(2,1)} %get-tuple-element.156.rows_ref, ...), custom_call_target="tpu_custom_call" | custom-call | flops 2657511014400 | bytes 5622988800 | tf_op jit(solution)/shard_map/pallas_call | solution.py:570
  243.0 2.5 multiply_convert_fusion
  246.9 5.2 shard_map.334
  254.2 26.1 %shard_map.335 = (bf16[2,2,8,96,768]{4,3,2,1,0:T(8,128)(2,1)}, f32[8,768]{1,0:T(8,128)}, f32[1408,768]{1,0:T(8,128)}, f32[1,1]{1,0:T(1,128)}) custom-call(s32[4]{0:T(128)} %pad_add_fusion.info_ref, f32[1408,768]{1,0:T(8,128)} %get-tuple-element.161.grad_ref, bf16[1408,768]{1,0:T(8,128)(2,1)} %get-tuple-element.156.rows_ref, ...), custom_call_target="tpu_custom_call" | custom-call | flops 2657511014400 | bytes 5190451200 | tf_op jit(solution)/shard_map/pallas_call | solution.py:667
  281.2 26.6 %shard_map.336 = (bf16[2,2,8,96,768]{4,3,2,1,0:T(8,128)(2,1)}, f32[8,768]{1,0:T(8,128)}, f32[1408,768]{1,0:T(8,128)}, f32[1,1]{1,0:T(1,128)}) custom-call(s32[4]{0:T(128)} %pad_add_fusion.info_ref, f32[1408,768]{1,0:T(8,128)} %get-tuple-element.161.grad_ref, bf16[1408,768]{1,0:T(8,128)(2,1)} %get-tuple-element.156.rows_ref, ...), custom_call_target="tpu_custom_call" | custom-call | flops 2657511014400 | bytes 5190451200 | tf_op jit(solution)/shard_map/pallas_call | solution.py:667
  307.9 5.2 fusion.18
  314.2 12.4 %shard_map.337 = (f32[1408,768]{1,0:T(8,128)}, f32[208,768]{1,0:T(8,128)}, f32[8,768]{1,0:T(8,128)}, f32[1,1]{1,0:T(1,128)}) custom-call(f32[1408,768]{1,0:T(8,128)} %get-tuple-element.161.grad_ref, f32[1408,768]{1,0:T(8,128)} %get-tuple-element.168.back_ref, bf16[832,768]{1,0:T(8,128)(2,1)} %get-tuple-element.175.vhat_two_ref, ...), custom_call_target="tpu_custom_call" | custom-call | flops 392586854400 | bytes 3833856000 | tf_op jit(solution)/shard_map/pallas_call | solution.py:817
  328.4 8.5 %shard_map.338 = (f32[1408,768]{1,0:T(8,128)}, f32[576,768]{1,0:T(8,128)}, f32[8,768]{1,0:T(8,128)}, f32[1,1]{1,0:T(1,128)}) custom-call(f32[1408,768]{1,0:T(8,128)} %get-tuple-element.161.grad_ref, f32[1408,768]{1,0:T(8,128)} %get-tuple-element.168.back_ref, bf16[576,768]{1,0:T(8,128)(2,1)} %get-tuple-element.169.vhat_two_ref, ...), custom_call_target="tpu_custom_call", output_to_operand_aliasing={{0}: (11, {})} | custom-call | flops 271790899200 | bytes 2654208000 | tf_op jit(solution)/shard_map/pallas_call | solution.py:817
  343.8 4.9 fusion.10.rest_2_
  349.8 25.9 %shard_map.339 = (bf16[2,2,8,96,768]{4,3,2,1,0:T(8,128)(2,1)}, f32[8,768]{1,0:T(8,128)}, f32[1408,768]{1,0:T(8,128)}, f32[1,1]{1,0:T(1,128)}) custom-call(s32[4]{0:T(128)} %pad_add_fusion.info_ref, f32[1408,768]{1,0:T(8,128)} %get-tuple-element.184.grad_ref, bf16[1408,768]{1,0:T(8,128)(2,1)} %get-tuple-element.150.rows_ref, ...), custom_call_target="tpu_custom_call" | custom-call | flops 2657511014400 | bytes 5190451200 | tf_op jit(solution)/shard_map/pallas_call | solution.py:667
  379.9 4.4 fusion.8
  386.1 3.3 collective-permute-start.48
  389.7 27.3 %shard_map.340 = (bf16[2,2,8,96,768]{4,3,2,1,0:T(8,128)(2,1)}, f32[8,768]{1,0:T(8,128)}, f32[1408,768]{1,0:T(8,128)}, f32[1,1]{1,0:T(1,128)}) custom-call(s32[4]{0:T(128)} %pad_add_fusion.info_ref, f32[1408,768]{1,0:T(8,128)} %get-tuple-element.184.grad_ref, bf16[1408,768]{1,0:T(8,128)(2,1)} %get-tuple-element.150.rows_ref, ...), custom_call_target="tpu_custom_call" | custom-call | flops 2657511014400 | bytes 5190451200 | tf_op jit(solution)/shard_map/pallas_call | solution.py:667
  417.0 2.5 fusion.51.rest_0_
  422.9 5.2 fusion.22
  428.3 12.3 %shard_map.341 = (f32[1408,768]{1,0:T(8,128)}, f32[208,768]{1,0:T(8,128)}, f32[8,768]{1,0:T(8,128)}, f32[1,1]{1,0:T(1,128)}) custom-call(f32[1408,768]{1,0:T(8,128)} %get-tuple-element.184.grad_ref, f32[1408,768]{1,0:T(8,128)} %get-tuple-element.199.back_ref, bf16[832,768]{1,0:T(8,128)(2,1)} %get-tuple-element.206.vhat_two_ref, ...), custom_call_target="tpu_custom_call" | custom-call | flops 392586854400 | bytes 3833856000 | tf_op jit(solution)/shard_map/pallas_call | solution.py:817
  442.4 8.4 %shard_map.342 = (f32[1408,768]{1,0:T(8,128)}, f32[576,768]{1,0:T(8,128)}, f32[8,768]{1,0:T(8,128)}, f32[1,1]{1,0:T(1,128)}) custom-call(f32[1408,768]{1,0:T(8,128)} %get-tuple-element.184.grad_ref, f32[1408,768]{1,0:T(8,128)} %get-tuple-element.199.back_ref, bf16[576,768]{1,0:T(8,128)(2,1)} %get-tuple-element.200.vhat_two_ref, ...), custom_call_target="tpu_custom_call", output_to_operand_aliasing={{0}: (11, {})} | custom-call | flops 271790899200 | bytes 2654208000 | tf_op jit(solution)/shard_map/pallas_call | solution.py:817
  462.4 4.9 fusion.5.rest_2_
  468.6 26.4 %shard_map.343 = (bf16[2,2,8,96,768]{4,3,2,1,0:T(8,128)(2,1)}, f32[8,768]{1,0:T(8,128)}, f32[1408,768]{1,0:T(8,128)}, f32[1,1]{1,0:T(1,128)}) custom-call(s32[4]{0:T(128)} %pad_add_fusion.info_ref, f32[1408,768]{1,0:T(8,128)} %get-tuple-element.215.grad_ref, bf16[1408,768]{1,0:T(8,128)(2,1)} %get-tuple-element.143.rows_ref, ...), custom_call_target="tpu_custom_call" | custom-call | flops 2657511014400 | bytes 5190451200 | tf_op jit(solution)/shard_map/pallas_call | solution.py:667
  498.9 4.4 fusion.3
  506.5 3.5 collective-permute-start.52
  510.3 27.0 %shard_map.344 = (bf16[2,2,8,96,768]{4,3,2,1,0:T(8,128)(2,1)}, f32[8,768]{1,0:T(8,128)}, f32[1408,768]{1,0:T(8,128)}, f32[1,1]{1,0:T(1,128)}) custom-call(s32[4]{0:T(128)} %pad_add_fusion.info_ref, f32[1408,768]{1,0:T(8,128)} %get-tuple-element.215.grad_ref, bf16[1408,768]{1,0:T(8,128)(2,1)} %get-tuple-element.143.rows_ref, ...), custom_call_target="tpu_custom_call" | custom-call | flops 2657511014400 | bytes 5190451200 | tf_op jit(solution)/shard_map/pallas_call | solution.py:667
  537.3 2.5 fusion.49.rest_0_
  540.0 2.5 collective-permute-done.51
  542.5 2.3 fusion.42
  545.0 3.6 fusion.26.rest_2_
  549.8 3.7 fusion.25.rest_1_
  553.6 12.2 %shard_map.345 = (f32[1408,768]{1,0:T(8,128)}, f32[208,768]{1,0:T(8,128)}, f32[8,768]{1,0:T(8,128)}, f32[1,1]{1,0:T(1,128)}) custom-call(f32[1408,768]{1,0:T(8,128)} %get-tuple-element.215.grad_ref, f32[1408,768]{1,0:T(8,128)} %get-tuple-element.230.back_ref, bf16[832,768]{1,0:T(8,128)(2,1)} %get-tuple-element.237.vhat_two_ref, ...), custom_call_target="tpu_custom_call" | custom-call | flops 392586854400 | bytes 3833856000 | tf_op jit(solution)/shard_map/pallas_call | solution.py:817
  565.9 8.4 %shard_map.346 = (f32[1408,768]{1,0:T(8,128)}, f32[576,768]{1,0:T(8,128)}, f32[8,768]{1,0:T(8,128)}, f32[1,1]{1,0:T(1,128)}) custom-call(f32[1408,768]{1,0:T(8,128)} %get-tuple-element.215.grad_ref, f32[1408,768]{1,0:T(8,128)} %get-tuple-element.230.back_ref, bf16[576,768]{1,0:T(8,128)(2,1)} %get-tuple-element.231.vhat_two_ref, ...), custom_call_target="tpu_custom_call", output_to_operand_aliasing={{0}: (11, {})} | custom-call | flops 271790899200 | bytes 2654208000 | tf_op jit(solution)/shard_map/pallas_call | solution.py:817
  580.6 3.5 fusion.32
  584.1 2.3 collective-permute-start.38
  589.2 19.2 %collective-permute-done.38.refs_0_ = bf16[4,96,768]{2,1,0:T(8,128)(2,1)S(1)} collective-permute-done((bf16[4,96,768]{2,1,0:T(8,128)(2,1)S(1)}, bf16[4,96,768]{2,1,0:T(8,128)(2,1)S(1)}, u32[]{:S(2)}, u32[]{:S(2)}) %collective-permute-start.38) | collective-permute-done | bytes 589856 | tf_op jit(solution)/shard_map/ppermute | solution.py:842
  610.5 4.8 add_convert_fusion.12
  616.5 2.2 collective-permute-start.44
  622.8 6.5 shard_map.348
  629.3 4.0 collective-permute-done.43.refs_0_
  633.3 9.0 %collective-permute-done.45.refs_2_ = bf16[248,768]{1,0:T(8,128)(2,1)S(1)} collective-permute-done((bf16[248,768]{1,0:T(8,128)(2,1)}, bf16[248,768]{1,0:T(8,128)(2,1)S(1)}, u32[]{:S(2)}, u32[]{:S(2)}) %collective-permute-start.45) | collective-permute-done | bytes 380960 | tf_op jit(solution)/shard_map/ppermute | solution.py:842
  644.2 2.9 fusion.39
  649.3 7.1 shard_map.350
  659.0 2.8 fusion.35
  667.1 8.6 %collective-permute-start.55 = (bf16[56,768]{1,0:T(8,128)(2,1)S(1)}, bf16[56,768]{1,0:T(8,128)(2,1)S(1)}, u32[]{:S(2)}, u32[]{:S(2)}) collective-permute-start(bf16[56,768]{1,0:T(8,128)(2,1)S(1)} %get-tuple-element.321), channel_id=1, source_target_pairs={{0,16},{2,18},{4,20},{6,22},{8,24},{10,26},{12,28},{14,30},{16,0},... | collective-permute-start | bytes 258056 | tf_op jit(solution)/shard_map/ppermute | solution.py:842
  677.9 9.6 %collective-permute-done.55.refs_1_ = bf16[56,768]{1,0:T(8,128)(2,1)S(1)} collective-permute-done((bf16[56,768]{1,0:T(8,128)(2,1)S(1)}, bf16[56,768]{1,0:T(8,128)(2,1)S(1)}, u32[]{:S(2)}, u32[]{:S(2)}) %collective-permute-start.55) | collective-permute-done | bytes 86048 | tf_op jit(solution)/shard_map/ppermute | solution.py:842
  692.1 5.6 collective-permute-start.58
  698.9 13.7 %collective-permute-done.58.refs_1_ = bf16[56,768]{1,0:T(8,128)(2,1)S(1)} collective-permute-done((bf16[56,768]{1,0:T(8,128)(2,1)S(1)}, bf16[56,768]{1,0:T(8,128)(2,1)S(1)}, u32[]{:S(2)}, u32[]{:S(2)}) %collective-permute-start.58) | collective-permute-done | bytes 86048 | tf_op jit(solution)/shard_map/ppermute | solution.py:842
  726.5 3.9 collective-permute-start.61
  732.3 2.3 maximum_select_fusion
  740.6 2.7 slice_bitcast_fusion
  745.2 6.9 shard_map.355
  (447 shorter events, 170.9 us)
Async XLA Ops:
  7.2 615.6 %all-gather.7.cloned.1.call-start = ((), (), s32[]{:S(2)}) async-start(), calls=%async_computation | async-start | bytes 5013504 | tf_op jit(solution)/shard_map/all_gather | solution.py:1173
  9.2 22.6 %collective-permute-start = (bf16[1,192,1536]{2,1,0:T(8,128)(2,1)}, bf16[1,192,1536]{2,1,0:T(8,128)(2,1)S(1)}, u32[]{:S(2)}, u32[]{:S(2)}) collective-permute-start(bf16[1,192,1536]{2,1,0:T(8,128)(2,1)} %constant_dynamic-slice_fusion.21), channel_id=1, source_target_pairs={{0,1},{1,0},{2,3},{3,2},{4,5},{5,4},{6,7},{7,6},{8,9},{9,8},{10,11... | collective-permute-start | bytes 1769480 | tf_op jit(solution)/shard_map/ppermute | solution.py:840
  13.1 24.0 %collective-permute-start.1 = (bf16[1,384,768]{2,1,0:T(8,128)(2,1)}, bf16[1,384,768]{2,1,0:T(8,128)(2,1)S(1)}, u32[]{:S(2)}, u32[]{:S(2)}) collective-permute-start(bf16[1,384,768]{2,1,0:T(8,128)(2,1)} %constant_dynamic-slice_fusion.20), channel_id=1, source_target_pairs={{0,1},{1,0},{2,3},{3,2},{4,5},{5,4},{6,7},{7,6},{8,9},{9,8},{10,11... | collective-permute-start | bytes 1769480 | tf_op jit(solution)/shard_map/ppermute | solution.py:840
  40.4 29.6 %collective-permute-start.2 = (bf16[1408,384]{1,0:T(8,128)(2,1)}, bf16[1408,384]{1,0:T(8,128)(2,1)S(1)}, u32[]{:S(2)}, u32[]{:S(2)}) collective-permute-start(bf16[1408,384]{1,0:T(8,128)(2,1)} %maximum_add_fusion.6), channel_id=1, source_target_pairs={{0,1},{1,0},{2,3},{3,2},{4,5},{5,4},{6,7},{7,6},{8,9},{9,8},{10,11... | collective-permute-start | bytes 3244040 | tf_op jit(solution)/shard_map/ppermute | solution.py:840
  42.2 23.7 %collective-permute-start.3 = (f32[3,3456]{1,0:T(4,128)S(1)}, f32[3,3456]{1,0:T(4,128)S(1)}, u32[]{:S(2)}, u32[]{:S(2)}) collective-permute-start(f32[3,3456]{1,0:T(4,128)S(1)} %maximum_add_fusion.13), channel_id=1, source_target_pairs={{0,1},{1,0},{2,3},{3,2},{4,5},{5,4},{6,7},{7,6},{8,9},{9,8},{10,11... | collective-permute-start | bytes 124424 | tf_op jit(solution)/shard_map/ppermute | solution.py:840
  43.5 28.7 %collective-permute-start.4 = (bf16[1,192,1536]{2,1,0:T(8,128)(2,1)}, bf16[1,192,1536]{2,1,0:T(8,128)(2,1)S(1)}, u32[]{:S(2)}, u32[]{:S(2)}) collective-permute-start(bf16[1,192,1536]{2,1,0:T(8,128)(2,1)} %broadcast_add_fusion.5), channel_id=1, source_target_pairs={{0,4},{2,6},{4,0},{6,2},{8,12},{10,14},{12,8},{14,10},{16,20},{18,... | collective-permute-start | bytes 1769480 | tf_op jit(solution)/shard_map/ppermute | solution.py:842
  45.5 33.9 %collective-permute-start.5 = (bf16[1,384,768]{2,1,0:T(8,128)(2,1)}, bf16[1,384,768]{2,1,0:T(8,128)(2,1)S(1)}, u32[]{:S(2)}, u32[]{:S(2)}) collective-permute-start(bf16[1,384,768]{2,1,0:T(8,128)(2,1)} %broadcast_add_fusion.4), channel_id=1, source_target_pairs={{0,4},{2,6},{4,0},{6,2},{8,12},{10,14},{12,8},{14,10},{16,20},{18,... | collective-permute-start | bytes 1769480 | tf_op jit(solution)/shard_map/ppermute | solution.py:842
  73.2 40.8 %collective-permute-start.6 = (bf16[2,1,192,1536]{3,2,1,0:T(8,128)(2,1)}, bf16[2,1,192,1536]{3,2,1,0:T(8,128)(2,1)}, u32[]{:S(2)}, u32[]{:S(2)}) collective-permute-start(bf16[2,1,192,1536]{3,2,1,0:T(8,128)(2,1)} %maximum_add_fusion.rest_0_.in_near_ref), channel_id=1, source_target_pairs={{0,2},{2,0},{4,6},{6,4},{8,10},{10,8},{12,14},{14,12},{16,18},{18,... | collective-permute-start | bytes 3538952 | tf_op jit(solution)/shard_map/ppermute | solution.py:842
  80.5 33.8 %collective-permute-start.7 = (bf16[2,1,384,768]{3,2,1,0:T(8,128)(2,1)}, bf16[2,1,384,768]{3,2,1,0:T(8,128)(2,1)}, u32[]{:S(2)}, u32[]{:S(2)}) collective-permute-start(bf16[2,1,384,768]{3,2,1,0:T(8,128)(2,1)} %maximum_add_fusion.1.rest_1_.out_near_ref), channel_id=1, source_target_pairs={{0,2},{2,0},{4,6},{6,4},{8,10},{10,8},{12,14},{14,12},{16,18},{18,... | collective-permute-start | bytes 3538952 | tf_op jit(solution)/shard_map/ppermute | solution.py:842
  80.5 28.2 %collective-permute-start.8 = (bf16[1,192,1536]{2,1,0:T(8,128)(2,1)}, bf16[1,192,1536]{2,1,0:T(8,128)(2,1)}, u32[]{:S(2)}, u32[]{:S(2)}) collective-permute-start(bf16[1,192,1536]{2,1,0:T(8,128)(2,1)} %dynamic-slice_add_fusion.4.rest_2_), channel_id=1, source_target_pairs={{0,1},{1,0},{2,3},{3,2},{4,5},{5,4},{6,7},{7,6},{8,9},{9,8},{10,11... | collective-permute-start | bytes 1769480 | tf_op jit(solution)/shard_map/ppermute | solution.py:840
  81.6 29.3 %collective-permute-start.9 = (bf16[1,384,768]{2,1,0:T(8,128)(2,1)}, bf16[1,384,768]{2,1,0:T(8,128)(2,1)}, u32[]{:S(2)}, u32[]{:S(2)}) collective-permute-start(bf16[1,384,768]{2,1,0:T(8,128)(2,1)} %dynamic-slice_add_fusion.3.rest_3_), channel_id=1, source_target_pairs={{0,1},{1,0},{2,3},{3,2},{4,5},{5,4},{6,7},{7,6},{8,9},{9,8},{10,11... | collective-permute-start | bytes 1769480 | tf_op jit(solution)/shard_map/ppermute | solution.py:840
  105.5 40.9 %collective-permute-start.12 = (bf16[1,192,1536]{2,1,0:T(8,128)(2,1)}, bf16[1,192,1536]{2,1,0:T(8,128)(2,1)}, u32[]{:S(2)}, u32[]{:S(2)}) collective-permute-start(bf16[1,192,1536]{2,1,0:T(8,128)(2,1)} %dynamic-slice_add_fusion.2.rest_2_), channel_id=1, source_target_pairs={{0,1},{1,0},{2,3},{3,2},{4,5},{5,4},{6,7},{7,6},{8,9},{9,8},{10,11... | collective-permute-start | bytes 1769480 | tf_op jit(solution)/shard_map/ppermute | solution.py:840
  108.7 41.0 %collective-permute-start.13 = (bf16[1,384,768]{2,1,0:T(8,128)(2,1)}, bf16[1,384,768]{2,1,0:T(8,128)(2,1)}, u32[]{:S(2)}, u32[]{:S(2)}) collective-permute-start(bf16[1,384,768]{2,1,0:T(8,128)(2,1)} %dynamic-slice_add_fusion.1.rest_3_), channel_id=1, source_target_pairs={{0,1},{1,0},{2,3},{3,2},{4,5},{5,4},{6,7},{7,6},{8,9},{9,8},{10,11... | collective-permute-start | bytes 1769480 | tf_op jit(solution)/shard_map/ppermute | solution.py:840
  110.9 28.6 %collective-permute-start.10 = (bf16[1,192,1536]{2,1,0:T(8,128)(2,1)}, bf16[1,192,1536]{2,1,0:T(8,128)(2,1)}, u32[]{:S(2)}, u32[]{:S(2)}) collective-permute-start(bf16[1,192,1536]{2,1,0:T(8,128)(2,1)} %broadcast_add_fusion.3.rest_0_), channel_id=1, source_target_pairs={{0,4},{2,6},{4,0},{6,2},{8,12},{10,14},{12,8},{14,10},{16,20},{18,... | collective-permute-start | bytes 1769480 | tf_op jit(solution)/shard_map/ppermute | solution.py:842
  114.0 30.0 %collective-permute-start.11 = (bf16[1,384,768]{2,1,0:T(8,128)(2,1)}, bf16[1,384,768]{2,1,0:T(8,128)(2,1)}, u32[]{:S(2)}, u32[]{:S(2)}) collective-permute-start(bf16[1,384,768]{2,1,0:T(8,128)(2,1)} %broadcast_add_fusion.2.rest_1_), channel_id=1, source_target_pairs={{0,4},{2,6},{4,0},{6,2},{8,12},{10,14},{12,8},{14,10},{16,20},{18,... | collective-permute-start | bytes 1769480 | tf_op jit(solution)/shard_map/ppermute | solution.py:842
  141.8 27.6 %collective-permute-start.14 = (bf16[2,1,192,1536]{3,2,1,0:T(8,128)(2,1)}, bf16[2,1,192,1536]{3,2,1,0:T(8,128)(2,1)}, u32[]{:S(2)}, u32[]{:S(2)}) collective-permute-start(bf16[2,1,192,1536]{3,2,1,0:T(8,128)(2,1)} %maximum_add_fusion.2.rest_0_.in_near_ref), channel_id=1, source_target_pairs={{0,2},{2,0},{4,6},{6,4},{8,10},{10,8},{12,14},{14,12},{16,18},{18,... | collective-permute-start | bytes 3538952 | tf_op jit(solution)/shard_map/ppermute | solution.py:842
  146.4 23.0 %collective-permute-start.15 = (bf16[2,1,384,768]{3,2,1,0:T(8,128)(2,1)}, bf16[2,1,384,768]{3,2,1,0:T(8,128)(2,1)}, u32[]{:S(2)}, u32[]{:S(2)}) collective-permute-start(bf16[2,1,384,768]{3,2,1,0:T(8,128)(2,1)} %maximum_add_fusion.3.rest_1_.out_near_ref), channel_id=1, source_target_pairs={{0,2},{2,0},{4,6},{6,4},{8,10},{10,8},{12,14},{14,12},{16,18},{18,... | collective-permute-start | bytes 3538952 | tf_op jit(solution)/shard_map/ppermute | solution.py:842
  148.4 46.7 %collective-permute-start.16 = (bf16[1,192,1536]{2,1,0:T(8,128)(2,1)}, bf16[1,192,1536]{2,1,0:T(8,128)(2,1)}, u32[]{:S(2)}, u32[]{:S(2)}) collective-permute-start(bf16[1,192,1536]{2,1,0:T(8,128)(2,1)} %broadcast_add_fusion.1.rest_2_), channel_id=1, source_target_pairs={{0,4},{2,6},{4,0},{6,2},{8,12},{10,14},{12,8},{14,10},{16,20},{18,... | collective-permute-start | bytes 1769480 | tf_op jit(solution)/shard_map/ppermute | solution.py:842
  151.5 47.2 %collective-permute-start.17 = (bf16[1,384,768]{2,1,0:T(8,128)(2,1)}, bf16[1,384,768]{2,1,0:T(8,128)(2,1)}, u32[]{:S(2)}, u32[]{:S(2)}) collective-permute-start(bf16[1,384,768]{2,1,0:T(8,128)(2,1)} %broadcast_add_fusion.rest_3_), channel_id=1, source_target_pairs={{0,4},{2,6},{4,0},{6,2},{8,12},{10,14},{12,8},{14,10},{16,20},{18,... | collective-permute-start | bytes 1769480 | tf_op jit(solution)/shard_map/ppermute | solution.py:842
  153.1 92.5 %collective-permute-start.20 = (bf16[1408,384]{1,0:T(8,128)(2,1)}, bf16[1408,384]{1,0:T(8,128)(2,1)}, u32[]{:S(2)}, u32[]{:S(2)}) collective-permute-start(bf16[1408,384]{1,0:T(8,128)(2,1)} %maximum_add_fusion.7.rest_4_), channel_id=1, source_target_pairs={{0,1},{1,0},{2,3},{3,2},{4,5},{5,4},{6,7},{7,6},{8,9},{9,8},{10,11... | collective-permute-start | bytes 3244040 | tf_op jit(solution)/shard_map/ppermute | solution.py:840
  197.5 18.4 %collective-permute-start.18 = (bf16[2,1,192,1536]{3,2,1,0:T(8,128)(2,1)}, bf16[2,1,192,1536]{3,2,1,0:T(8,128)(2,1)}, u32[]{:S(2)}, u32[]{:S(2)}) collective-permute-start(bf16[2,1,192,1536]{3,2,1,0:T(8,128)(2,1)} %maximum_add_fusion.4.rest_0_.in_near_ref), channel_id=1, source_target_pairs={{0,2},{2,0},{4,6},{6,4},{8,10},{10,8},{12,14},{14,12},{16,18},{18,... | collective-permute-start | bytes 3538952 | tf_op jit(solution)/shard_map/ppermute | solution.py:842
  201.1 14.8 %collective-permute-start.19 = (bf16[2,1,384,768]{3,2,1,0:T(8,128)(2,1)}, bf16[2,1,384,768]{3,2,1,0:T(8,128)(2,1)}, u32[]{:S(2)}, u32[]{:S(2)}) collective-permute-start(bf16[2,1,384,768]{3,2,1,0:T(8,128)(2,1)} %maximum_add_fusion.5.rest_1_.out_near_ref), channel_id=1, source_target_pairs={{0,2},{2,0},{4,6},{6,4},{8,10},{10,8},{12,14},{14,12},{16,18},{18,... | collective-permute-start | bytes 3538952 | tf_op jit(solution)/shard_map/ppermute | solution.py:842
  253.9 27.3 %collective-permute-start.21 = (bf16[1408,384]{1,0:T(8,128)(2,1)}, bf16[1408,384]{1,0:T(8,128)(2,1)}, u32[]{:S(2)}, u32[]{:S(2)}) collective-permute-start(bf16[1408,384]{1,0:T(8,128)(2,1)} %dynamic-slice_add_fusion.rest_0_), channel_id=1, source_target_pairs={{0,1},{1,0},{2,3},{3,2},{4,5},{5,4},{6,7},{7,6},{8,9},{9,8},{10,11... | collective-permute-start | bytes 3244040 | tf_op jit(solution)/shard_map/ppermute | solution.py:840
  280.4 27.5 %collective-permute-start.22 = (bf16[2,2,8,96,768]{4,3,2,1,0:T(8,128)(2,1)}, bf16[2,2,8,96,768]{4,3,2,1,0:T(8,128)(2,1)}, u32[]{:S(2)}, u32[]{:S(2)}) collective-permute-start(bf16[2,2,8,96,768]{4,3,2,1,0:T(8,128)(2,1)} %get-tuple-element.167.rest_2_), channel_id=1, source_target_pairs={{0,2},{2,0},{4,6},{6,4},{8,10},{10,8},{12,14},{14,12},{16,18},{18,... | collective-permute-start | bytes 14155784 | tf_op jit(solution)/shard_map/ppermute | solution.py:842
  313.0 30.7 %collective-permute-start.23 = (bf16[2,4,96,768]{3,2,1,0:T(8,128)(2,1)}, bf16[2,4,96,768]{3,2,1,0:T(8,128)(2,1)}, u32[]{:S(2)}, u32[]{:S(2)}) collective-permute-start(bf16[2,4,96,768]{3,2,1,0:T(8,128)(2,1)} %get-tuple-element.287.rest_0_), channel_id=1, source_target_pairs={{0,1},{1,0},{2,3},{3,2},{4,5},{5,4},{6,7},{7,6},{8,9},{9,8},{10,11... | collective-permute-start | bytes 3538952 | tf_op jit(solution)/shard_map/ppermute | solution.py:840
  343.1 32.6 %collective-permute-start.24 = (bf16[4,2,56,768]{3,2,0,1:T(8,128)(2,1)}, bf16[4,2,56,768]{3,2,0,1:T(8,128)(2,1)}, u32[]{:S(2)}, u32[]{:S(2)}) collective-permute-start(bf16[4,2,56,768]{3,2,0,1:T(8,128)(2,1)} %fusion.45), channel_id=1, source_target_pairs={{0,2},{2,0},{4,6},{6,4},{8,10},{10,8},{12,14},{14,12},{16,18},{18,... | collective-permute-start | bytes 2064392 | tf_op jit(solution)/shard_map/ppermute | solution.py:842
  343.5 36.4 %collective-permute-start.25 = (bf16[2,4,96,768]{3,2,1,0:T(8,128)(2,1)}, bf16[2,4,96,768]{3,2,1,0:T(8,128)(2,1)}, u32[]{:S(2)}, u32[]{:S(2)}) collective-permute-start(bf16[2,4,96,768]{3,2,1,0:T(8,128)(2,1)} %get-tuple-element.286.rest_1_), channel_id=1, source_target_pairs={{0,1},{1,0},{2,3},{3,2},{4,5},{5,4},{6,7},{7,6},{8,9},{9,8},{10,11... | collective-permute-start | bytes 3538952 | tf_op jit(solution)/shard_map/ppermute | solution.py:840
  348.6 31.2 %collective-permute-start.26 = (bf16[2,4,96,768]{3,2,1,0:T(8,128)(2,1)}, bf16[2,4,96,768]{3,2,1,0:T(8,128)(2,1)}, u32[]{:S(2)}, u32[]{:S(2)}) collective-permute-start(bf16[2,4,96,768]{3,2,1,0:T(8,128)(2,1)} %fusion.10.rest_2_), channel_id=1, source_target_pairs={{0,4},{2,6},{4,0},{6,2},{8,12},{10,14},{12,8},{14,10},{16,20},{18,... | collective-permute-start | bytes 3538952 | tf_op jit(solution)/shard_map/ppermute | solution.py:842
  378.6 38.4 %collective-permute-start.27 = (bf16[4,56,768]{2,1,0:T(8,128)(2,1)}, bf16[4,56,768]{2,1,0:T(8,128)(2,1)}, u32[]{:S(2)}, u32[]{:S(2)}) collective-permute-start(bf16[4,56,768]{2,1,0:T(8,128)(2,1)} %dynamic-slice_bitcast_fusion.8.rest_1_), channel_id=1, source_target_pairs={{0,4},{2,6},{4,0},{6,2},{8,12},{10,14},{12,8},{14,10},{16,20},{18,... | collective-permute-start | bytes 1032200 | tf_op jit(solution)/shard_map/ppermute | solution.py:842
  378.9 44.0 %collective-permute-start.28 = (bf16[2,2,8,96,768]{4,3,2,1,0:T(8,128)(2,1)}, bf16[2,2,8,96,768]{4,3,2,1,0:T(8,128)(2,1)}, u32[]{:S(2)}, u32[]{:S(2)}) collective-permute-start(bf16[2,2,8,96,768]{4,3,2,1,0:T(8,128)(2,1)} %get-tuple-element.198.rest_5_), channel_id=1, source_target_pairs={{0,2},{2,0},{4,6},{6,4},{8,10},{10,8},{12,14},{14,12},{16,18},{18,... | collective-permute-start | bytes 14155784 | tf_op jit(solution)/shard_map/ppermute | solution.py:842
  386.1 34.6 %collective-permute-start.48 = (bf16[192,768]{1,0:T(8,128)(2,1)}, bf16[192,768]{1,0:T(8,128)(2,1)}, u32[]{:S(2)}, u32[]{:S(2)}) collective-permute-start(bf16[192,768]{1,0:T(8,128)(2,1)} %get-tuple-element.310.rest_4_), channel_id=1, source_target_pairs={{0,24},{2,26},{4,28},{6,30},{8,16},{10,18},{12,20},{14,22},{16,8},... | collective-permute-start | bytes 884744 | tf_op jit(solution)/shard_map/ppermute | solution.py:842
  389.4 31.4 %collective-permute-start.47 = (bf16[192,768]{1,0:T(8,128)(2,1)}, bf16[192,768]{1,0:T(8,128)(2,1)}, u32[]{:S(2)}, u32[]{:S(2)}) collective-permute-start(bf16[192,768]{1,0:T(8,128)(2,1)} %get-tuple-element.312.rest_3_), channel_id=1, source_target_pairs={{0,16},{2,18},{4,20},{6,22},{8,24},{10,26},{12,28},{14,30},{16,0},... | collective-permute-start | bytes 884744 | tf_op jit(solution)/shard_map/ppermute | solution.py:842
  389.4 31.4 %collective-permute-start.46 = (bf16[192,768]{1,0:T(8,128)(2,1)}, bf16[192,768]{1,0:T(8,128)(2,1)}, u32[]{:S(2)}, u32[]{:S(2)}) collective-permute-start(bf16[192,768]{1,0:T(8,128)(2,1)} %get-tuple-element.311.rest_2_), channel_id=1, source_target_pairs={{0,8},{2,10},{4,12},{6,14},{8,0},{10,2},{12,4},{14,6},{16,24},{18,... | collective-permute-start | bytes 884744 | tf_op jit(solution)/shard_map/ppermute | solution.py:842
  419.5 40.3 %collective-permute-start.33 = (bf16[4,56,768]{2,1,0:T(8,128)(2,1)}, bf16[4,56,768]{2,1,0:T(8,128)(2,1)}, u32[]{:S(2)}, u32[]{:S(2)}) collective-permute-start(bf16[4,56,768]{2,1,0:T(8,128)(2,1)} %fusion.51.rest_0_), channel_id=1, source_target_pairs={{0,1},{1,0},{2,3},{3,2},{4,5},{5,4},{6,7},{7,6},{8,9},{9,8},{10,11... | collective-permute-start | bytes 1032200 | tf_op jit(solution)/shard_map/ppermute | solution.py:840
  422.8 226.5 %all-gather.9.cloned.1.call-start = ((), (), s32[]{:S(2)}) async-start(), calls=%async_computation.1 | async-start | bytes 6475776 | tf_op jit(solution)/shard_map/all_gather | solution.py:1173
  428.0 34.4 %collective-permute-start.29 = (bf16[2,4,96,768]{3,2,1,0:T(8,128)(2,1)}, bf16[2,4,96,768]{3,2,1,0:T(8,128)(2,1)}, u32[]{:S(2)}, u32[]{:S(2)}) collective-permute-start(bf16[2,4,96,768]{3,2,1,0:T(8,128)(2,1)} %get-tuple-element.285.rest_1_), channel_id=1, source_target_pairs={{0,1},{1,0},{2,3},{3,2},{4,5},{5,4},{6,7},{7,6},{8,9},{9,8},{10,11... | collective-permute-start | bytes 3538952 | tf_op jit(solution)/shard_map/ppermute | solution.py:840
  457.7 37.3 %collective-permute-start.30 = (bf16[4,2,56,768]{3,2,0,1:T(8,128)(2,1)}, bf16[4,2,56,768]{3,2,0,1:T(8,128)(2,1)}, u32[]{:S(2)}, u32[]{:S(2)}) collective-permute-start(bf16[4,2,56,768]{3,2,0,1:T(8,128)(2,1)} %fusion.44), channel_id=1, source_target_pairs={{0,2},{2,0},{4,6},{6,4},{8,10},{10,8},{12,14},{14,12},{16,18},{18,... | collective-permute-start | bytes 2064392 | tf_op jit(solution)/shard_map/ppermute | solution.py:842
  458.7 40.1 %collective-permute-start.31 = (bf16[2,4,96,768]{3,2,1,0:T(8,128)(2,1)}, bf16[2,4,96,768]{3,2,1,0:T(8,128)(2,1)}, u32[]{:S(2)}, u32[]{:S(2)}) collective-permute-start(bf16[2,4,96,768]{3,2,1,0:T(8,128)(2,1)} %get-tuple-element.284.rest_1_), channel_id=1, source_target_pairs={{0,1},{1,0},{2,3},{3,2},{4,5},{5,4},{6,7},{7,6},{8,9},{9,8},{10,11... | collective-permute-start | bytes 3538952 | tf_op jit(solution)/shard_map/ppermute | solution.py:840
  467.3 31.6 %collective-permute-start.32 = (bf16[2,4,96,768]{3,2,1,0:T(8,128)(2,1)}, bf16[2,4,96,768]{3,2,1,0:T(8,128)(2,1)}, u32[]{:S(2)}, u32[]{:S(2)}) collective-permute-start(bf16[2,4,96,768]{3,2,1,0:T(8,128)(2,1)} %fusion.5.rest_2_), channel_id=1, source_target_pairs={{0,4},{2,6},{4,0},{6,2},{8,12},{10,14},{12,8},{14,10},{16,20},{18,... | collective-permute-start | bytes 3538952 | tf_op jit(solution)/shard_map/ppermute | solution.py:842
  497.8 39.5 %collective-permute-start.34 = (bf16[4,56,768]{2,1,0:T(8,128)(2,1)}, bf16[4,56,768]{2,1,0:T(8,128)(2,1)}, u32[]{:S(2)}, u32[]{:S(2)}) collective-permute-start(bf16[4,56,768]{2,1,0:T(8,128)(2,1)} %dynamic-slice_bitcast_fusion.7.rest_1_), channel_id=1, source_target_pairs={{0,4},{2,6},{4,0},{6,2},{8,12},{10,14},{12,8},{14,10},{16,20},{18,... | collective-permute-start | bytes 1032200 | tf_op jit(solution)/shard_map/ppermute | solution.py:842
  498.1 46.9 %collective-permute-start.35 = (bf16[2,2,8,96,768]{4,3,2,1,0:T(8,128)(2,1)}, bf16[2,2,8,96,768]{4,3,2,1,0:T(8,128)(2,1)}, u32[]{:S(2)}, u32[]{:S(2)}) collective-permute-start(bf16[2,2,8,96,768]{4,3,2,1,0:T(8,128)(2,1)} %get-tuple-element.229.rest_5_), channel_id=1, source_target_pairs={{0,2},{2,0},{4,6},{6,4},{8,10},{10,8},{12,14},{14,12},{16,18},{18,... | collective-permute-start | bytes 14155784 | tf_op jit(solution)/shard_map/ppermute | solution.py:842
  506.5 33.4 %collective-permute-start.52 = (bf16[248,768]{1,0:T(8,128)(2,1)}, bf16[248,768]{1,0:T(8,128)(2,1)}, u32[]{:S(2)}, u32[]{:S(2)}) collective-permute-start(bf16[248,768]{1,0:T(8,128)(2,1)} %get-tuple-element.295.rest_4_), channel_id=1, source_target_pairs={{0,24},{2,26},{4,28},{6,30},{8,16},{10,18},{12,20},{14,22},{16,8},... | collective-permute-start | bytes 1142792 | tf_op jit(solution)/shard_map/ppermute | solution.py:842
  510.0 32.5 %collective-permute-start.51 = (bf16[248,768]{1,0:T(8,128)(2,1)}, bf16[248,768]{1,0:T(8,128)(2,1)}, u32[]{:S(2)}, u32[]{:S(2)}) collective-permute-start(bf16[248,768]{1,0:T(8,128)(2,1)} %get-tuple-element.296.rest_3_), channel_id=1, source_target_pairs={{0,16},{2,18},{4,20},{6,22},{8,24},{10,26},{12,28},{14,30},{16,0},... | collective-permute-start | bytes 1142792 | tf_op jit(solution)/shard_map/ppermute | solution.py:842
  510.0 32.5 %collective-permute-start.50 = (bf16[248,768]{1,0:T(8,128)(2,1)}, bf16[248,768]{1,0:T(8,128)(2,1)}, u32[]{:S(2)}, u32[]{:S(2)}) collective-permute-start(bf16[248,768]{1,0:T(8,128)(2,1)} %get-tuple-element.297.rest_2_), channel_id=1, source_target_pairs={{0,8},{2,10},{4,12},{6,14},{8,0},{10,2},{12,4},{14,6},{16,24},{18,... | collective-permute-start | bytes 1142792 | tf_op jit(solution)/shard_map/ppermute | solution.py:842
  539.8 46.6 %collective-permute-start.42 = (bf16[4,56,768]{2,1,0:T(8,128)(2,1)}, bf16[4,56,768]{2,1,0:T(8,128)(2,1)}, u32[]{:S(2)}, u32[]{:S(2)}) collective-permute-start(bf16[4,56,768]{2,1,0:T(8,128)(2,1)} %fusion.49.rest_0_), channel_id=1, source_target_pairs={{0,1},{1,0},{2,3},{3,2},{4,5},{5,4},{6,7},{7,6},{8,9},{9,8},{10,11... | collective-permute-start | bytes 1032200 | tf_op jit(solution)/shard_map/ppermute | solution.py:840
  544.9 190.4 %all-gather.11.cloned.1.call-start = ((), (), s32[]{:S(2)}) async-start(), calls=%async_computation.2 | async-start | bytes 6475776 | tf_op jit(solution)/shard_map/all_gather | solution.py:1173
  548.6 32.0 %collective-permute-start.39 = (bf16[2,4,96,768]{3,2,1,0:T(8,128)(2,1)}, bf16[2,4,96,768]{3,2,1,0:T(8,128)(2,1)}, u32[]{:S(2)}, u32[]{:S(2)}) collective-permute-start(bf16[2,4,96,768]{3,2,1,0:T(8,128)(2,1)} %fusion.26.rest_2_), channel_id=1, source_target_pairs={{0,4},{2,6},{4,0},{6,2},{8,12},{10,14},{12,8},{14,10},{16,20},{18,... | collective-permute-start | bytes 3538952 | tf_op jit(solution)/shard_map/ppermute | solution.py:842
  553.5 27.1 %collective-permute-start.37 = (bf16[8,96,768]{2,1,0:T(8,128)(2,1)}, bf16[8,96,768]{2,1,0:T(8,128)(2,1)}, u32[]{:S(2)}, u32[]{:S(2)}) collective-permute-start(bf16[8,96,768]{2,1,0:T(8,128)(2,1)} %fusion.25.rest_1_), channel_id=1, source_target_pairs={{0,1},{1,0},{2,3},{3,2},{4,5},{5,4},{6,7},{7,6},{8,9},{9,8},{10,11... | collective-permute-start | bytes 3538952 | tf_op jit(solution)/shard_map/ppermute | solution.py:840
  577.0 11.3 %collective-permute-start.36 = (bf16[4,2,56,768]{3,2,0,1:T(8,128)(2,1)S(1)}, bf16[4,2,56,768]{3,2,0,1:T(8,128)(2,1)S(1)}, u32[]{:S(2)}, u32[]{:S(2)}) collective-permute-start(bf16[4,2,56,768]{3,2,0,1:T(8,128)(2,1)S(1)} %fusion.43), channel_id=1, source_target_pairs={{0,2},{2,0},{4,6},{6,4},{8,10},{10,8},{12,14},{14,12},{16,18},{18,... | collective-permute-start | bytes 2064392 | tf_op jit(solution)/shard_map/ppermute | solution.py:842
  584.1 24.3 %collective-permute-start.38 = (bf16[4,96,768]{2,1,0:T(8,128)(2,1)S(1)}, bf16[4,96,768]{2,1,0:T(8,128)(2,1)S(1)}, u32[]{:S(2)}, u32[]{:S(2)}) collective-permute-start(bf16[4,96,768]{2,1,0:T(8,128)(2,1)S(1)} %get-tuple-element.283), channel_id=1, source_target_pairs={{0,4},{2,6},{4,0},{6,2},{8,12},{10,14},{12,8},{14,10},{16,20},{18,... | collective-permute-start | bytes 1769480 | tf_op jit(solution)/shard_map/ppermute | solution.py:842
  586.4 22.0 %collective-permute-start.40 = (bf16[4,96,768]{2,1,0:T(8,128)(2,1)S(1)}, bf16[4,96,768]{2,1,0:T(8,128)(2,1)S(1)}, u32[]{:S(2)}, u32[]{:S(2)}) collective-permute-start(bf16[4,96,768]{2,1,0:T(8,128)(2,1)S(1)} %get-tuple-element.282), channel_id=1, source_target_pairs={{0,1},{1,0},{2,3},{3,2},{4,5},{5,4},{6,7},{7,6},{8,9},{9,8},{10,11... | collective-permute-start | bytes 1769480 | tf_op jit(solution)/shard_map/ppermute | solution.py:840
  616.5 16.8 %collective-permute-start.43 = (bf16[248,768]{1,0:T(8,128)(2,1)}, bf16[248,768]{1,0:T(8,128)(2,1)S(1)}, u32[]{:S(2)}, u32[]{:S(2)}) collective-permute-start(bf16[248,768]{1,0:T(8,128)(2,1)} %get-tuple-element.294), channel_id=1, source_target_pairs={{0,8},{2,10},{4,12},{6,14},{8,0},{10,2},{12,4},{14,6},{16,24},{18,... | collective-permute-start | bytes 1142792 | tf_op jit(solution)/shard_map/ppermute | solution.py:842
  616.5 16.8 %collective-permute-start.44 = (bf16[248,768]{1,0:T(8,128)(2,1)}, bf16[248,768]{1,0:T(8,128)(2,1)S(1)}, u32[]{:S(2)}, u32[]{:S(2)}) collective-permute-start(bf16[248,768]{1,0:T(8,128)(2,1)} %get-tuple-element.293), channel_id=1, source_target_pairs={{0,16},{2,18},{4,20},{6,22},{8,24},{10,26},{12,28},{14,30},{16,0},... | collective-permute-start | bytes 1142792 | tf_op jit(solution)/shard_map/ppermute | solution.py:842
  618.7 23.6 %collective-permute-start.45 = (bf16[248,768]{1,0:T(8,128)(2,1)}, bf16[248,768]{1,0:T(8,128)(2,1)S(1)}, u32[]{:S(2)}, u32[]{:S(2)}) collective-permute-start(bf16[248,768]{1,0:T(8,128)(2,1)} %get-tuple-element.292), channel_id=1, source_target_pairs={{0,24},{2,26},{4,28},{6,30},{8,16},{10,18},{12,20},{14,22},{16,8},... | collective-permute-start | bytes 1142792 | tf_op jit(solution)/shard_map/ppermute | solution.py:842
  621.7 7.6 collective-permute-start.41
  648.0 8.5 %collective-permute-start.49 = (bf16[4,56,768]{2,1,0:T(8,128)(2,1)S(1)}, bf16[4,56,768]{2,1,0:T(8,128)(2,1)S(1)}, u32[]{:S(2)}, u32[]{:S(2)}) collective-permute-start(bf16[4,56,768]{2,1,0:T(8,128)(2,1)S(1)} %fusion.47), channel_id=1, source_target_pairs={{0,1},{1,0},{2,3},{3,2},{4,5},{5,4},{6,7},{7,6},{8,9},{9,8},{10,11... | collective-permute-start | bytes 1032200 | tf_op jit(solution)/shard_map/ppermute | solution.py:840
  661.8 25.7 %collective-permute-start.53 = (bf16[1408,384]{1,0:T(8,128)(2,1)}, bf16[1408,384]{1,0:T(8,128)(2,1)S(1)}, u32[]{:S(2)}, u32[]{:S(2)}) collective-permute-start(bf16[1408,384]{1,0:T(8,128)(2,1)} %fusion.35), channel_id=1, source_target_pairs={{0,1},{1,0},{2,3},{3,2},{4,5},{5,4},{6,7},{7,6},{8,9},{9,8},{10,11... | collective-permute-start | bytes 3244040 | tf_op jit(solution)/shard_map/ppermute | solution.py:840
  665.8 12.0 %collective-permute-start.56 = (bf16[56,768]{1,0:T(8,128)(2,1)S(1)}, bf16[56,768]{1,0:T(8,128)(2,1)S(1)}, u32[]{:S(2)}, u32[]{:S(2)}) collective-permute-start(bf16[56,768]{1,0:T(8,128)(2,1)S(1)} %get-tuple-element.320), channel_id=1, source_target_pairs={{0,24},{2,26},{4,28},{6,30},{8,16},{10,18},{12,20},{14,22},{16,8},... | collective-permute-start | bytes 258056 | tf_op jit(solution)/shard_map/ppermute | solution.py:842
  667.1 20.3 %collective-permute-start.55 = (bf16[56,768]{1,0:T(8,128)(2,1)S(1)}, bf16[56,768]{1,0:T(8,128)(2,1)S(1)}, u32[]{:S(2)}, u32[]{:S(2)}) collective-permute-start(bf16[56,768]{1,0:T(8,128)(2,1)S(1)} %get-tuple-element.321), channel_id=1, source_target_pairs={{0,16},{2,18},{4,20},{6,22},{8,24},{10,26},{12,28},{14,30},{16,0},... | collective-permute-start | bytes 258056 | tf_op jit(solution)/shard_map/ppermute | solution.py:842
  675.7 11.7 %collective-permute-start.54 = (bf16[56,768]{1,0:T(8,128)(2,1)S(1)}, bf16[56,768]{1,0:T(8,128)(2,1)S(1)}, u32[]{:S(2)}, u32[]{:S(2)}) collective-permute-start(bf16[56,768]{1,0:T(8,128)(2,1)S(1)} %get-tuple-element.319), channel_id=1, source_target_pairs={{0,8},{2,10},{4,12},{6,14},{8,0},{10,2},{12,4},{14,6},{16,24},{18,... | collective-permute-start | bytes 258056 | tf_op jit(solution)/shard_map/ppermute | solution.py:842
  691.4 7.5 collective-permute-start.59
  692.1 20.5 %collective-permute-start.58 = (bf16[56,768]{1,0:T(8,128)(2,1)S(1)}, bf16[56,768]{1,0:T(8,128)(2,1)S(1)}, u32[]{:S(2)}, u32[]{:S(2)}) collective-permute-start(bf16[56,768]{1,0:T(8,128)(2,1)S(1)} %fusion.69), channel_id=1, source_target_pairs={{0,16},{2,18},{4,20},{6,22},{8,24},{10,26},{12,28},{14,30},{16,0},... | collective-permute-start | bytes 258056 | tf_op jit(solution)/shard_map/ppermute | solution.py:842
  697.7 14.9 %collective-permute-start.57 = (bf16[56,768]{1,0:T(8,128)(2,1)S(1)}, bf16[56,768]{1,0:T(8,128)(2,1)S(1)}, u32[]{:S(2)}, u32[]{:S(2)}) collective-permute-start(bf16[56,768]{1,0:T(8,128)(2,1)S(1)} %fusion.69), channel_id=1, source_target_pairs={{0,8},{2,10},{4,12},{6,14},{8,0},{10,2},{12,4},{14,6},{16,24},{18,... | collective-permute-start | bytes 258056 | tf_op jit(solution)/shard_map/ppermute | solution.py:842
  726.5 8.2 %collective-permute-start.61 = (bf16[4,2,56,768]{3,2,0,1:T(8,128)(2,1)S(1)}, bf16[4,2,56,768]{3,2,0,1:T(8,128)(2,1)S(1)}, u32[]{:S(2)}, u32[]{:S(2)}) collective-permute-start(bf16[4,2,56,768]{3,2,0,1:T(8,128)(2,1)S(1)} %maximum_add_fusion.10), channel_id=1, source_target_pairs={{0,2},{2,0},{4,6},{6,4},{8,10},{10,8},{12,14},{14,12},{16,18},{18,... | collective-permute-start | bytes 2064392 | tf_op jit(solution)/shard_map/ppermute | solution.py:842
  (79 other events, 386.2 us)
Sparse Core Ops, SparseCore 0:
  423.0 54.5 all-gather.6
  545.0 72.8 all-gather.8
  647.3 80.4 all-gather.10
